TPU v7x, 32 devices: a whole 2x2x4 slice. The times are simulated.
32 devices in a mesh: gx: 2 (over core), gy: 4 (over y, x), gz: 4 (over z).
Axes of the slice: x: 2, y: 2, z: 4, core: 2. Of those that a mesh axis runs over, the one named last changes fastest.
Arguments:
- right_side: float32 [32, 256, 512], P('gx', 'gy', 'gz'), may hold values from -18 to 18
- inv_density: float32 [32, 256, 512], P('gx', 'gy', 'gz'), may hold values from 0.5 to 2
- active: int32 [32, 256, 512], P('gx', 'gy', 'gz'), may hold values 0 or 1
Outputs:
- solution_field: float32 [32, 256, 512], P('gx', 'gy', 'gz')
- residual: float32 [32, 256, 512], P('gx', 'gy', 'gz')
All inputs are finite; a program needn't handle non-finite values. No bound on the sum of `active` on one device may be relied on, other than what follows from the above.
Results may differ from a plain program's by a relative error of at most 0.0003.
Values sent between devices are 32-bit elements; how exact they have to be, the bound alone decides.
No kernel may reach another device: no remote copies, remote signals or barrier semaphores. Data moves between devices by JAX's collectives and lax.ppermute only.
A program may use at most 64 MiB of HBM per device.

v0:
```python
import jax
import jax.numpy as jnp
from jax import lax
from jax.sharding import PartitionSpec as P

STEPS = 6


basis_shift = 7.0
basis_scale = 7.0
NEIGHBOURS = ((2, 1, 1), (0, 1, 1), (1, 2, 1), (1, 0, 1), (1, 1, 2), (1, 1, 0))


def extended(cells, sides, width):
    for axis, dim in sides:
        count = lax.axis_size(axis)
        ends = count - 1
        head = lax.slice_in_dim(cells, 0, width, axis=dim)
        tail = lax.slice_in_dim(cells, cells.shape[dim] - width, cells.shape[dim], axis=dim)
        cells = jnp.concatenate(
            [
                lax.ppermute(tail, axis, [(i, (i + 1) % count) for i in range(ends)]),
                cells,
                lax.ppermute(head, axis, [((i + 1) % count, i) for i in range(ends)]),
            ],
            axis=dim,
        )
    return cells


def shifted(field, offset):
    extent = field.shape
    return field[
        offset[0] : extent[0] - 2 + offset[0],
        offset[1] : extent[1] - 2 + offset[1],
        offset[2] : extent[2] - 2 + offset[2],
    ]


def trimmed(field, margin):
    extent = field.shape
    return field[
        margin : extent[0] - margin, margin : extent[1] - margin, margin : extent[2] - margin
    ]


def face_table(weight_pad):
    center_weight = shifted(weight_pad, (1, 1, 1))
    diagonal = jnp.zeros_like(center_weight)
    faces = []
    for offset in NEIGHBOURS:
        other_weight = shifted(weight_pad, offset)
        liquid_side = other_weight > 0.0
        denominator = jnp.where(liquid_side, center_weight + other_weight, 1.0)
        face_value = jnp.where(
            liquid_side, 2.0 * center_weight * other_weight / denominator, center_weight
        )
        diagonal = diagonal + face_value
        faces.append(face_value)
    return (faces, diagonal)


def apply_faces(vector_pad, faces, diagonal):
    center_value = shifted(vector_pad, (1, 1, 1))
    beside = jnp.zeros_like(center_value)
    for offset, face_value in zip(NEIGHBOURS, faces):
        beside = beside + face_value * shifted(vector_pad, offset)
    return diagonal * center_value - beside


def next_basis(image_field, previous):
    return (image_field - basis_shift * previous) / basis_scale


def least_squares(triangle):
    column_count = triangle.shape[1] - 1
    row_ids = lax.broadcasted_iota(jnp.int32, (column_count + 1, column_count), 0)
    col_ids = lax.broadcasted_iota(jnp.int32, (column_count + 1, column_count), 1)
    change = jnp.where(row_ids == col_ids, basis_shift, 0.0) + jnp.where(
        row_ids == col_ids + 1, basis_scale, 0.0
    )
    change = change.astype(triangle.dtype)
    hess = jnp.dot(triangle, change, precision=lax.Precision.HIGHEST)
    target = triangle[:, 0]
    for pivot_index in range(column_count):
        first_value = hess[pivot_index, pivot_index]
        second_value = hess[pivot_index + 1, pivot_index]
        radius = jnp.sqrt(first_value * first_value + second_value * second_value)
        cosine = first_value / radius
        sine_value = second_value / radius
        upper_row = cosine * hess[pivot_index] + sine_value * hess[pivot_index + 1]
        lower_row = cosine * hess[pivot_index + 1] - sine_value * hess[pivot_index]
        hess = hess.at[pivot_index].set(upper_row).at[pivot_index + 1].set(lower_row)
        upper_target = cosine * target[pivot_index] + sine_value * target[pivot_index + 1]
        lower_target = cosine * target[pivot_index + 1] - sine_value * target[pivot_index]
        target = target.at[pivot_index].set(upper_target).at[pivot_index + 1].set(lower_target)
    solved = [None] * column_count
    for row_index in reversed(range(column_count)):
        running = target[row_index]
        for column_index in range(row_index + 1, column_count):
            running = running - hess[row_index, column_index] * solved[column_index]
        solved[row_index] = running / hess[row_index, row_index]
    coefficients = jnp.stack(solved)
    first_unit = jnp.where(
        lax.broadcasted_iota(jnp.int32, (column_count + 1,), 0) == 0, 1.0, 0.0
    ).astype(triangle.dtype)
    leftover = first_unit - jnp.dot(change, coefficients, precision=lax.Precision.HIGHEST)
    return (coefficients, leftover)


def on_device(right_side, inv_density, active):
    liquid = active.astype(jnp.float32)
    weight = inv_density * liquid
    vector = right_side * liquid
    basis_list = [vector]
    vector_pad, weight_pad = (
        extended(vector, (("gx", 0), ("gy", 1), ("gz", 2)), STEPS),
        extended(weight, (("gx", 0), ("gy", 1), ("gz", 2)), STEPS),
    )
    full_faces, full_diagonal = face_table(weight_pad)
    current = vector_pad
    for power_index in range(STEPS):
        depth = STEPS - power_index
        margin = STEPS - depth
        faces = [trimmed(face_value, margin) for face_value in full_faces]
        image_field = apply_faces(current, faces, trimmed(full_diagonal, margin))
        current = next_basis(image_field, trimmed(current, 1))
        basis_list.append(trimmed(current, depth - 1))
    stacked = jnp.stack(basis_list).reshape(STEPS + 1, -1)
    local_gram = jnp.dot(stacked, stacked.T, precision=lax.Precision.HIGHEST)
    gram_matrix = lax.psum(local_gram, ("gx", "gy", "gz"))
    triangle = jnp.linalg.cholesky(gram_matrix).T
    coefficients, leftover = least_squares(triangle)
    solution_field = jnp.zeros_like(right_side)
    for power_index in range(STEPS):
        solution_field = solution_field + coefficients[power_index] * basis_list[power_index]
    residual = jnp.zeros_like(right_side)
    for power_index in range(STEPS + 1):
        residual = residual + leftover[power_index] * basis_list[power_index]
    return (solution_field, residual)


def solution(mesh):
    placed = (P("gx", "gy", "gz"), P("gx", "gy", "gz"), P("gx", "gy", "gz"))
    return jax.shard_map(
        on_device,
        mesh=mesh,
        in_specs=placed,
        out_specs=(P("gx", "gy", "gz"), P("gx", "gy", "gz")),
        check_vma=False,
    )
```

profile of v0, /device:TPU:0, one launch (start us, length us, event | category | flops | bytes accessed | tf_op | source)
XLA Modules:
  0.0 246.6 jit_solution(1126371502032609983)
XLA Ops:
  0.6 1.5 convert_multiply_fusion
  2.1 2.4 collective-permute-start
  4.5 1.3 collective-permute-start.1
  5.9 3.0 %collective-permute-start.6 = (f32[6,64,128]{2,1,0:T(8,128)S(1)}, f32[6,64,128]{2,1,0:T(8,128)S(1)}, u32[]{:S(2)}, u32[]{:S(2)}) collective-permute-start(f32[6,64,128]{2,1,0:T(8,128)S(1)} %get-tuple-element.308), channel_id=1, source_target_pairs={{0,16},{1,17},{2,18},{3,19},{4,20},{5,21},{6,22},{7,23},{8,24},{9,... | collective-permute-start | bytes 589832 | tf_op jit(solution)/shard_map/ppermute | solution.py:22
  8.9 1.3 collective-permute-start.7
  10.3 4.2 %collective-permute-start.2 = (f32[28,6,128]{2,1,0:T(8,128)S(1)}, f32[28,6,128]{2,1,0:T(8,128)S(1)}, u32[]{:S(2)}, u32[]{:S(2)}) collective-permute-start(f32[28,6,128]{2,1,0:T(8,128)S(1)} %get-tuple-element.306), channel_id=1, source_target_pairs={{0,4},{4,8},{8,12},{1,5},{5,9},{9,13},{2,6},{6,10},{10,14},{3,7},{... | collective-permute-start | bytes 258056 | tf_op jit(solution)/shard_map/ppermute | solution.py:22
  14.5 1.3 collective-permute-start.3
  15.9 0.8 pad_maximum_fusion.6
  16.7 4.5 %collective-permute-start.8 = (f32[28,6,128]{2,1,0:T(8,128)}, f32[28,6,128]{2,1,0:T(8,128)S(1)}, u32[]{:S(2)}, u32[]{:S(2)}) collective-permute-start(f32[28,6,128]{2,1,0:T(8,128)} %get-tuple-element.304), channel_id=1, source_target_pairs={{0,4},{4,8},{8,12},{1,5},{5,9},{9,13},{2,6},{6,10},{10,14},{3,7},{... | collective-permute-start | bytes 258056 | tf_op jit(solution)/shard_map/ppermute | solution.py:22
  21.2 1.3 collective-permute-start.9
  24.0 1.4 fusion.68
  25.3 2.4 copy.13
  27.7 4.1 %collective-permute-start.4 = (f32[28,76,6]{1,0,2:T(8,128)}, f32[28,76,6]{1,0,2:T(8,128)}, u32[]{:S(2)}, u32[]{:S(2)}) collective-permute-start(f32[28,76,6]{1,0,2:T(8,128)} %copy.13), channel_id=1, source_target_pairs={{0,1},{1,2},{2,3},{4,5},{5,6},{6,7},{8,9},{9,10},{10,11},{12,13},{... | collective-permute-start | bytes 153224 | tf_op jit(solution)/shard_map/ppermute | solution.py:22
  31.8 1.1 copy.14
  32.9 1.3 collective-permute-start.5
  34.3 1.2 pad_maximum_fusion.3
  35.4 1.4 fusion.67
  36.8 2.4 copy.17
  39.2 5.2 %collective-permute-start.10 = (f32[28,76,6]{1,0,2:T(8,128)}, f32[28,76,6]{1,0,2:T(8,128)}, u32[]{:S(2)}, u32[]{:S(2)}) collective-permute-start(f32[28,76,6]{1,0,2:T(8,128)} %copy.17), channel_id=1, source_target_pairs={{0,1},{1,2},{2,3},{4,5},{5,6},{6,7},{8,9},{9,10},{10,11},{12,13},{... | collective-permute-start | bytes 153224 | tf_op jit(solution)/shard_map/ppermute | solution.py:22
  44.4 1.1 copy.18
  45.5 1.5 collective-permute-start.11
  47.0 2.4 copy.15
  49.4 2.4 copy.16
  51.7 2.9 %pad_maximum_fusion = f32[28,76,140]{2,1,0:T(8,128)S(1)} fusion(f32[28,76,6]{2,1,0:T(8,128)} %copy.16, f32[28,6,128]{2,1,0:T(8,128)} %copy-done.19, f32[6,64,128]{2,1,0:T(8,128)} %copy-done.17, f32[16,64,128]{2,1,0:T(8,128)S(1)} %get-tuple-element.312, f32[6,64,128]{2,1,0:T(8,128)} %copy-done.16, f32[28,6,128]{2,1,0:T(8,128)} %copy-done.18, f32[28,76,6]{2,1,0:T(8,128)} %copy.15), kind=kLoop, calls=%fused_computation | loop fusion | flops 1787520 | bytes 2383360 | tf_op jit(solution)/shard_map/concatenate | solution.py:20
  54.6 8.0 %add_add_fusion = (f32[26,74,138]{2,1,0:T(8,128)}, f32[26,74,138]{2,1,0:T(8,128)}, f32[26,74,138]{2,1,0:T(8,128)}, f32[26,74,138]{2,1,0:T(8,128)}, f32[26,74,138...) fusion(f32[28,76,140]{2,1,0:T(8,128)S(1)} %pad_maximum_fusion), kind=kLoop, calls=%fused_computation.17 | loop fusion | flops 11151504 | bytes 14868672 | tf_op jit(solution)/shard_map/add | solution.py:58
  62.6 2.4 copy.19
  65.0 2.6 %copy.20 = f32[28,76,6]{2,1,0:T(8,128)} copy(f32[28,76,6]{1,0,2:T(8,128)} %collective-permute-done.11) | data formatting | bytes 102144 | tf_op jit(solution)/shard_map/ppermute | solution.py:24
  67.6 2.9 %pad_maximum_fusion.1 = f32[28,76,140]{2,1,0:T(8,128)S(1)} fusion(f32[28,76,6]{2,1,0:T(8,128)} %copy.20, f32[28,6,128]{2,1,0:T(8,128)} %collective-permute-done.9, f32[6,64,128]{2,1,0:T(8,128)S(1)} %copy-done.15, f32[16,64,128]{2,1,0:T(8,128)S(1)} %get-tuple-element.313, f32[6,64,128]{2,1,0:T(8,128)S(1)} %copy-done.13, ...), kind=kLoop, calls=%fused_computation.1 | loop fusion | flops 1787520 | bytes 2383360 | tf_op jit(solution)/shard_map/concatenate | solution.py:20
  70.6 5.6 %fusion.3 = f32[26,74,138]{2,1,0:T(8,128)S(1)} fusion(f32[26,74,138]{2,1,0:T(8,128)} %get-tuple-element.298, f32[28,76,140]{2,1,0:T(8,128)S(1)} %pad_maximum_fusion.1, f32[26,74,138]{2,1,0:T(8,128)} %get-tuple-element.297, f32[26,74,138]{2,1,0:T(8,128)} %get-tuple-element.296, f32[26,74,138]{2,1,0:T(8,128)S(1)} %copy-done.4, f32[26,74,138]{2,1,0:T(8,128)S(1)} %copy-done.3, ...), kind=kLoop, calls=%fused_computation.6 | loop fusion | flops 5575752 | bytes 14868672 | tf_op jit(solution)/shard_map/div | solution.py:72
  76.6 6.6 %fusion.11 = f32[24,72,136]{2,1,0:T(8,128)S(1)} fusion(f32[26,74,138]{2,1,0:T(8,128)S(1)} %fusion.3, f32[26,74,138]{2,1,0:T(8,128)S(1)} %copy-done.8, f32[26,74,138]{2,1,0:T(8,128)S(1)} %copy-done.7, f32[26,74,138]{2,1,0:T(8,128)S(1)} %copy-done.6, f32[26,74,138]{2,1,0:T(8,128)S(1)} %copy-done.5, f32[26,74,138]{2,1,0:T(8,128)S(1)} %copy-done.3, ...), kind=kLoop, calls=%fused_computation.27 | loop fusion | flops 3760128 | bytes 14100480 | tf_op jit(solution)/shard_map/div | solution.py:72
  83.2 6.2 %fusion.19 = f32[22,70,134]{2,1,0:T(8,128)S(1)} fusion(f32[24,72,136]{2,1,0:T(8,128)S(1)} %fusion.11, f32[26,74,138]{2,1,0:T(8,128)S(1)} %copy-done.8, f32[26,74,138]{2,1,0:T(8,128)S(1)} %copy-done.7, f32[26,74,138]{2,1,0:T(8,128)S(1)} %copy-done.6, f32[26,74,138]{2,1,0:T(8,128)S(1)} %copy-done.5, f32[26,74,138]{2,1,0:T(8,128)S(1)} %copy-done.3, ...), kind=kLoop, calls=%fused_computation.42 | loop fusion | flops 3301760 | bytes 12381600 | tf_op jit(solution)/shard_map/div | solution.py:72
  89.4 5.4 %fusion.27 = f32[20,68,132]{2,1,0:T(8,128)S(1)} fusion(f32[22,70,134]{2,1,0:T(8,128)S(1)} %fusion.19, f32[26,74,138]{2,1,0:T(8,128)S(1)} %copy-done.8, f32[26,74,138]{2,1,0:T(8,128)S(1)} %copy-done.7, f32[26,74,138]{2,1,0:T(8,128)S(1)} %copy-done.6, f32[26,74,138]{2,1,0:T(8,128)S(1)} %copy-done.5, f32[26,74,138]{2,1,0:T(8,128)S(1)} %copy-done.3, ...), kind=kLoop, calls=%fused_computation.57 | loop fusion | flops 2872320 | bytes 10771200 | tf_op jit(solution)/shard_map/div | solution.py:72
  94.9 4.9 %fusion.35 = f32[18,66,130]{2,1,0:T(8,128)S(1)} fusion(f32[20,68,132]{2,1,0:T(8,128)S(1)} %fusion.27, f32[26,74,138]{2,1,0:T(8,128)S(1)} %copy-done.8, f32[26,74,138]{2,1,0:T(8,128)S(1)} %copy-done.7, f32[26,74,138]{2,1,0:T(8,128)S(1)} %copy-done.6, f32[26,74,138]{2,1,0:T(8,128)S(1)} %copy-done.5, f32[26,74,138]{2,1,0:T(8,128)S(1)} %copy-done.3, ...), kind=kLoop, calls=%fused_computation.72 | loop fusion | flops 2471040 | bytes 9266400 | tf_op jit(solution)/shard_map/div | solution.py:72
  99.9 1.2 slice.1072
  101.0 1.0 slice.1057
  102.1 1.0 slice.1042
  103.1 1.0 slice.1027
  104.1 3.0 %broadcast_multiply_fusion = (f32[16,64,128]{2,1,0:T(8,128)}, f32[16,64,128]{2,1,0:T(8,128)}, f32[16,64,128]{2,1,0:T(8,128)}) fusion(f32[18,66,130]{2,1,0:T(8,128)S(1)} %fusion.35, f32[26,74,138]{2,1,0:T(8,128)S(1)} %copy-done.8, f32[26,74,138]{2,1,0:T(8,128)S(1)} %copy-done.7, f32[26,74,138]{2,1,0:T(8,128)S(1)} %copy-done.6, ...), kind=kLoop, calls=%fused_computation.106 | loop fusion | flops 2097152 | bytes 8912896 | tf_op jit(solution)/shard_map/div | solution.py:72
  107.1 11.5 %stack.52 = f32[7,16,64,128]{3,0,2,1:T(8,128)} concatenate(f32[1,16,64,128]{3,0,2,1:T(1,128)} %bitcast.98, f32[1,16,64,128]{3,0,2,1:T(1,128)} %bitcast.104, f32[1,16,64,128]{3,0,2,1:T(1,128)} %bitcast.103, f32[1,16,64,128]{3,0,2,1:T(1,128)} %bitcast.102, f32[1,16,64,128]{3,0,2,1:T(1,128)} %bitcast.101, f32[1,16,64,128]{3,0,2,1:T(1,128)} %bitcast.100, f32[1,16,64,128]{3,0,2,1:T(1,128)} %bitcast.99), dimensions={0} | concatenate | bytes 7340032 | tf_op jit(solution)/shard_map/stack | solution.py:129
  118.6 12.6 %convolution_bitcast_fusion = f32[7,7]{0,1:T(8,128)S(1)} fusion(f32[7,16,64,128]{3,0,2,1:T(8,128)} %stack.52), kind=kOutput, calls=%fused_computation.85 | convolution fusion | flops 77070336 | bytes 3670212 | tf_op jit(solution)/shard_map/dot_general | solution.py:130
  131.2 43.2 %psum.7 = f32[7,7]{0,1:T(8,128)S(1)} all-reduce(f32[7,7]{0,1:T(8,128)S(1)} %convolution_bitcast_fusion), channel_id=1, replica_groups=mesh['gx'=2,'gy'=4,'gz'=4] {'gx','gy','gz'}, use_global_device_ids=true, to_apply=%region_0.1 | all-reduce | flops 49 | bytes 392 | tf_op jit(solution)/shard_map/psum | solution.py:131
  175.8 0.8 fusion.49
  191.0 0.7 fusion.71
  216.2 0.7 fusion.76
  218.1 0.7 fusion.78
  233.9 3.7 %multiply_add_fusion.1 = f32[16,64,128]{2,1,0:T(8,128)} fusion(f32[16,64,128]{2,1,0:T(8,128)} %copy-done.10, f32[]{:T(128)} %div.124, f32[]{:T(128)} %div.125, f32[]{:T(128)} %div.126, f32[]{:T(128)} %div.127, f32[]{:T(128)} %div.128, f32[]{:T(128)} %div.129, f32[20,68,132]{2,1,0:T(8,128)} %copy-done.1, f32[22,70,134]{2,1,0:T(8,128)S(1)} %fusion.19, ...), kind=kLoop, calls=%fused_computation.103 | loop fusion | flops 1441792 | bytes 3670040 | tf_op jit(solution)/shard_map/add | solution.py:136
  237.8 0.7 fusion.74
  239.1 7.5 %multiply_add_fusion = f32[16,64,128]{2,1,0:T(8,128)} fusion(f32[16,64,128]{2,1,0:T(8,128)} %get-tuple-element.291, f32[16,64,128]{2,1,0:T(8,128)} %copy-done.10, f32[]{:T(128)} %bitcast.78, f32[]{:T(128)} %bitcast.77, f32[]{:T(128)} %bitcast.76, f32[]{:T(128)} %bitcast.75, f32[]{:T(128)} %bitcast.74, f32[]{:T(128)} %bitcast.73, f32[]{:T(128)} %bitcast.72, ...), kind=kLoop, calls=%fused_computation.102 | loop fusion | flops 1703936 | bytes 4194332 | tf_op jit(solution)/shard_map/add | solution.py:139
  (96 shorter events, 13.0 us)
Async XLA Ops:
  2.1 65.5 %copy-start.10 = (f32[16,64,128]{2,1,0:T(8,128)}, f32[16,64,128]{2,1,0:T(8,128)S(1)}, u32[]{:S(2)}) copy-start(f32[16,64,128]{2,1,0:T(8,128)S(1)} %get-tuple-element.313) | copy-start | bytes 1572868
  2.1 8.1 %collective-permute-start = (f32[6,64,128]{2,1,0:T(8,128)S(1)}, f32[6,64,128]{2,1,0:T(8,128)S(1)}, u32[]{:S(2)}, u32[]{:S(2)}) collective-permute-start(f32[6,64,128]{2,1,0:T(8,128)S(1)} %get-tuple-element.310), channel_id=1, source_target_pairs={{0,16},{1,17},{2,18},{3,19},{4,20},{5,21},{6,22},{7,23},{8,24},{9,... | collective-permute-start | bytes 589832 | tf_op jit(solution)/shard_map/ppermute | solution.py:22
  4.5 5.7 %collective-permute-start.1 = (f32[6,64,128]{2,1,0:T(8,128)S(1)}, f32[6,64,128]{2,1,0:T(8,128)S(1)}, u32[]{:S(2)}, u32[]{:S(2)}) collective-permute-start(f32[6,64,128]{2,1,0:T(8,128)S(1)} %get-tuple-element.311), channel_id=1, source_target_pairs={{16,0},{17,1},{18,2},{19,3},{20,4},{21,5},{22,6},{23,7},{24,8},{25... | collective-permute-start | bytes 589832 | tf_op jit(solution)/shard_map/ppermute | solution.py:24
  5.9 10.0 %collective-permute-start.6 = (f32[6,64,128]{2,1,0:T(8,128)S(1)}, f32[6,64,128]{2,1,0:T(8,128)S(1)}, u32[]{:S(2)}, u32[]{:S(2)}) collective-permute-start(f32[6,64,128]{2,1,0:T(8,128)S(1)} %get-tuple-element.308), channel_id=1, source_target_pairs={{0,16},{1,17},{2,18},{3,19},{4,20},{5,21},{6,22},{7,23},{8,24},{9,... | collective-permute-start | bytes 589832 | tf_op jit(solution)/shard_map/ppermute | solution.py:22
  8.9 6.9 %collective-permute-start.7 = (f32[6,64,128]{2,1,0:T(8,128)S(1)}, f32[6,64,128]{2,1,0:T(8,128)S(1)}, u32[]{:S(2)}, u32[]{:S(2)}) collective-permute-start(f32[6,64,128]{2,1,0:T(8,128)S(1)} %get-tuple-element.309), channel_id=1, source_target_pairs={{16,0},{17,1},{18,2},{19,3},{20,4},{21,5},{22,6},{23,7},{24,8},{25... | collective-permute-start | bytes 589832 | tf_op jit(solution)/shard_map/ppermute | solution.py:24
  10.2 12.3 %copy-start.16 = (f32[6,64,128]{2,1,0:T(8,128)}, f32[6,64,128]{2,1,0:T(8,128)S(1)}, u32[]{:S(2)}) copy-start(f32[6,64,128]{2,1,0:T(8,128)S(1)} %collective-permute-done) | copy-start | bytes 589828
  10.3 12.3 %copy-start.17 = (f32[6,64,128]{2,1,0:T(8,128)}, f32[6,64,128]{2,1,0:T(8,128)S(1)}, u32[]{:S(2)}) copy-start(f32[6,64,128]{2,1,0:T(8,128)S(1)} %collective-permute-done.1) | copy-start | bytes 589828
  10.3 12.2 %collective-permute-start.2 = (f32[28,6,128]{2,1,0:T(8,128)S(1)}, f32[28,6,128]{2,1,0:T(8,128)S(1)}, u32[]{:S(2)}, u32[]{:S(2)}) collective-permute-start(f32[28,6,128]{2,1,0:T(8,128)S(1)} %get-tuple-element.306), channel_id=1, source_target_pairs={{0,4},{4,8},{8,12},{1,5},{5,9},{9,13},{2,6},{6,10},{10,14},{3,7},{... | collective-permute-start | bytes 258056 | tf_op jit(solution)/shard_map/ppermute | solution.py:22
  14.5 8.0 %collective-permute-start.3 = (f32[28,6,128]{2,1,0:T(8,128)S(1)}, f32[28,6,128]{2,1,0:T(8,128)S(1)}, u32[]{:S(2)}, u32[]{:S(2)}) collective-permute-start(f32[28,6,128]{2,1,0:T(8,128)S(1)} %get-tuple-element.307), channel_id=1, source_target_pairs={{4,0},{8,4},{12,8},{5,1},{9,5},{13,9},{6,2},{10,6},{14,10},{7,3},{... | collective-permute-start | bytes 258056 | tf_op jit(solution)/shard_map/ppermute | solution.py:24
  15.8 6.7 %copy-start.12 = (f32[6,64,128]{2,1,0:T(8,128)}, f32[6,64,128]{2,1,0:T(8,128)S(1)}, u32[]{:S(2)}) copy-start(f32[6,64,128]{2,1,0:T(8,128)S(1)} %collective-permute-done.6) | copy-start | bytes 589828
  15.9 6.7 %copy-start.14 = (f32[6,64,128]{2,1,0:T(8,128)}, f32[6,64,128]{2,1,0:T(8,128)S(1)}, u32[]{:S(2)}) copy-start(f32[6,64,128]{2,1,0:T(8,128)S(1)} %collective-permute-done.7) | copy-start | bytes 589828
  16.7 17.6 %collective-permute-start.8 = (f32[28,6,128]{2,1,0:T(8,128)}, f32[28,6,128]{2,1,0:T(8,128)S(1)}, u32[]{:S(2)}, u32[]{:S(2)}) collective-permute-start(f32[28,6,128]{2,1,0:T(8,128)} %get-tuple-element.304), channel_id=1, source_target_pairs={{0,4},{4,8},{8,12},{1,5},{5,9},{9,13},{2,6},{6,10},{10,14},{3,7},{... | collective-permute-start | bytes 258056 | tf_op jit(solution)/shard_map/ppermute | solution.py:22
  21.2 13.0 %collective-permute-start.9 = (f32[28,6,128]{2,1,0:T(8,128)}, f32[28,6,128]{2,1,0:T(8,128)}, u32[]{:S(2)}, u32[]{:S(2)}) collective-permute-start(f32[28,6,128]{2,1,0:T(8,128)} %get-tuple-element.305), channel_id=1, source_target_pairs={{4,0},{8,4},{12,8},{5,1},{9,5},{13,9},{6,2},{10,6},{14,10},{7,3},{... | collective-permute-start | bytes 258056 | tf_op jit(solution)/shard_map/ppermute | solution.py:24
  22.5 0.6 copy-start.18
  23.2 0.7 copy-start.19
  27.7 19.3 %collective-permute-start.4 = (f32[28,76,6]{1,0,2:T(8,128)}, f32[28,76,6]{1,0,2:T(8,128)}, u32[]{:S(2)}, u32[]{:S(2)}) collective-permute-start(f32[28,76,6]{1,0,2:T(8,128)} %copy.13), channel_id=1, source_target_pairs={{0,1},{1,2},{2,3},{4,5},{5,6},{6,7},{8,9},{9,10},{10,11},{12,13},{... | collective-permute-start | bytes 153224 | tf_op jit(solution)/shard_map/ppermute | solution.py:22
  32.9 16.4 %collective-permute-start.5 = (f32[28,76,6]{1,0,2:T(8,128)}, f32[28,76,6]{1,0,2:T(8,128)}, u32[]{:S(2)}, u32[]{:S(2)}) collective-permute-start(f32[28,76,6]{1,0,2:T(8,128)} %copy.14), channel_id=1, source_target_pairs={{1,0},{2,1},{3,2},{5,4},{6,5},{7,6},{9,8},{10,9},{11,10},{13,12},{... | collective-permute-start | bytes 153224 | tf_op jit(solution)/shard_map/ppermute | solution.py:24
  39.2 23.4 %collective-permute-start.10 = (f32[28,76,6]{1,0,2:T(8,128)}, f32[28,76,6]{1,0,2:T(8,128)}, u32[]{:S(2)}, u32[]{:S(2)}) collective-permute-start(f32[28,76,6]{1,0,2:T(8,128)} %copy.17), channel_id=1, source_target_pairs={{0,1},{1,2},{2,3},{4,5},{5,6},{6,7},{8,9},{9,10},{10,11},{12,13},{... | collective-permute-start | bytes 153224 | tf_op jit(solution)/shard_map/ppermute | solution.py:22
  45.5 19.5 %collective-permute-start.11 = (f32[28,76,6]{1,0,2:T(8,128)}, f32[28,76,6]{1,0,2:T(8,128)}, u32[]{:S(2)}, u32[]{:S(2)}) collective-permute-start(f32[28,76,6]{1,0,2:T(8,128)} %copy.18), channel_id=1, source_target_pairs={{1,0},{2,1},{3,2},{5,4},{6,5},{7,6},{9,8},{10,9},{11,10},{13,12},{... | collective-permute-start | bytes 153224 | tf_op jit(solution)/shard_map/ppermute | solution.py:24
  62.6 5.0 %copy-start.13 = (f32[6,64,128]{2,1,0:T(8,128)S(1)}, f32[6,64,128]{2,1,0:T(8,128)}, u32[]{:S(2)}) copy-start(f32[6,64,128]{2,1,0:T(8,128)} %copy-done.12) | copy-start | bytes 589828
  62.6 5.0 %copy-start.15 = (f32[6,64,128]{2,1,0:T(8,128)S(1)}, f32[6,64,128]{2,1,0:T(8,128)}, u32[]{:S(2)}) copy-start(f32[6,64,128]{2,1,0:T(8,128)} %copy-done.14) | copy-start | bytes 589828
  65.0 5.5 %copy-start.4 = (f32[26,74,138]{2,1,0:T(8,128)S(1)}, f32[26,74,138]{2,1,0:T(8,128)}, u32[]{:S(2)}) copy-start(f32[26,74,138]{2,1,0:T(8,128)} %get-tuple-element.295) | copy-start | bytes 3186148
  67.6 2.9 %copy-start.2 = (f32[26,74,138]{2,1,0:T(8,128)S(1)}, f32[26,74,138]{2,1,0:T(8,128)}, u32[]{:S(2)}) copy-start(f32[26,74,138]{2,1,0:T(8,128)} %get-tuple-element.293) | copy-start | bytes 3186148
  67.6 3.0 %copy-start.3 = (f32[26,74,138]{2,1,0:T(8,128)S(1)}, f32[26,74,138]{2,1,0:T(8,128)}, u32[]{:S(2)}) copy-start(f32[26,74,138]{2,1,0:T(8,128)} %get-tuple-element.294) | copy-start | bytes 3186148
  70.6 5.7 %copy-start.5 = (f32[26,74,138]{2,1,0:T(8,128)S(1)}, f32[26,74,138]{2,1,0:T(8,128)}, u32[]{:S(2)}) copy-start(f32[26,74,138]{2,1,0:T(8,128)} %get-tuple-element.295) | copy-start | bytes 3186148
  70.6 5.7 %copy-start.6 = (f32[26,74,138]{2,1,0:T(8,128)S(1)}, f32[26,74,138]{2,1,0:T(8,128)}, u32[]{:S(2)}) copy-start(f32[26,74,138]{2,1,0:T(8,128)} %get-tuple-element.296) | copy-start | bytes 3186148
  70.6 5.7 %copy-start.7 = (f32[26,74,138]{2,1,0:T(8,128)S(1)}, f32[26,74,138]{2,1,0:T(8,128)}, u32[]{:S(2)}) copy-start(f32[26,74,138]{2,1,0:T(8,128)} %get-tuple-element.297) | copy-start | bytes 3186148
  70.6 5.7 %copy-start.8 = (f32[26,74,138]{2,1,0:T(8,128)S(1)}, f32[26,74,138]{2,1,0:T(8,128)}, u32[]{:S(2)}) copy-start(f32[26,74,138]{2,1,0:T(8,128)} %get-tuple-element.298) | copy-start | bytes 3186148
  70.6 6.0 %copy-start.9 = (f32[26,74,138]{2,1,0:T(8,128)S(1)}, f32[26,74,138]{2,1,0:T(8,128)}, u32[]{:S(2)}) copy-start(f32[26,74,138]{2,1,0:T(8,128)} %get-tuple-element.292) | copy-start | bytes 3186148
  76.2 26.9 %copy-start = (f32[26,74,138]{2,1,0:T(8,128)}, f32[26,74,138]{2,1,0:T(8,128)S(1)}, u32[]{:S(2)}) copy-start(f32[26,74,138]{2,1,0:T(8,128)S(1)} %fusion.3) | copy-start | bytes 3186148
  94.9 5.0 %copy-start.1 = (f32[20,68,132]{2,1,0:T(8,128)}, f32[20,68,132]{2,1,0:T(8,128)S(1)}, u32[]{:S(2)}) copy-start(f32[20,68,132]{2,1,0:T(8,128)S(1)} %fusion.27) | copy-start | bytes 2154244
  99.8 4.3 %copy-start.11 = (f32[18,66,130]{2,1,0:T(8,128)}, f32[18,66,130]{2,1,0:T(8,128)S(1)}, u32[]{:S(2)}) copy-start(f32[18,66,130]{2,1,0:T(8,128)S(1)} %fusion.35) | copy-start | bytes 1853284
where the time goes:
time: 249 us; the launch traced here: 247 us
  other arithmetic  62.3 us (25%)
  local copies, waits for them, and re-layouts  48.6 us (20%)
  between operations  47.5 us (19%)
  blocking collectives  43.2 us (17%)
  starting transfers between devices  31.4 us (13%)
  matrix products  13.6 us (5%)
    psum x1, blocking collectives, on_device(): gram_matrix = lax.psum(local_gram, ('gx', 'gy', 'gz'))  43.2 us
    div x6, other arithmetic, next_basis(): return (image_field - basis_shift * previous) / basis_scale  31.8 us
    ppermute x6, starting transfers between devices, extended(): lax.ppermute(tail, axis, [(i, (i + 1) % count) for i in range(ends)])  23.5 us
    dot_general x1, matrix products, on_device(): local_gram = jnp.dot(stacked, stacked.T, precision=lax.Precision.HIGHEST)  12.6 us
    another operation x1, local copies, waits for them, and re-layouts, on_device(): stacked = jnp.stack(basis_list).reshape(STEPS + 1, -1)  11.5 us
    add x1, other arithmetic, face_table(): diagonal = diagonal + face_value  8.03 us
    ppermute x6, starting transfers between devices, extended(): lax.ppermute(head, axis, [((i + 1) % count, i) for i in range(ends)])  7.91 us
    slice x6, local copies, waits for them, and re-layouts, extended(): lax.slice_in_dim(cells, cells.shape[dim] - width, cells.shape[dim], axis=...  7.57 us
  transfers between devices with their start and end apart: 12, of which 0 were waited for; matrix products, arithmetic and copies ran while one was open for 12% of the time, Pallas kernels for 0%

commit v1 on v0

v1 whole, which is shorter than its diff:
```python
import functools

import jax
import jax.numpy as jnp
from jax import lax
from jax.experimental import pallas as pl
from jax.experimental.pallas import tpu as pltpu
from jax.sharding import PartitionSpec as P

STEPS = 6
SHIFT = 7.0
GROUPS = 8
WIDE = 16
TOP = 8
VMEM = pltpu.VMEM
AXES = ("gx", "gy", "gz")


def vmem_spec():
    return pl.BlockSpec(memory_space=VMEM)


def resident(array):
    return pltpu.with_memory_space_constraint(array, VMEM)


def call(body, outs, name, scratch=(), grid=None, out_specs=None, limit=40, flops=0):
    return pl.pallas_call(
        body,
        out_shape=outs,
        grid=grid or (),
        out_specs=out_specs if out_specs is not None else [vmem_spec() for _ in outs],
        scratch_shapes=list(scratch),
        compiler_params=pltpu.CompilerParams(vmem_limit_bytes=limit << 20),
        cost_estimate=pl.CostEstimate(flops=flops, bytes_accessed=1 << 20, transcendentals=0),
        name=name,
    )


def kept(shape):
    return pltpu.VMEM(shape, jnp.float32)


def lanes(shape=(8, 128)):
    return lax.broadcasted_iota(jnp.int32, shape, len(shape) - 1)


class Plan:
    def __init__(self, mesh, nx, ny, nz):
        self.gx, self.gy, self.gz = (mesh.shape[a] for a in AXES)
        self.nx, self.ny, self.nz = nx, ny, nz
        self.sides = min(self.gx - 1, 2)
        self.planes = nx + STEPS * self.sides
        self.deep = self.planes // GROUPS + 1
        self.rows = ny + 16
        self.half = self.rows // 2
        self.tall = self.rows + 16

    def own(self):
        if self.sides == 1:
            return lax.axis_index("gx") * STEPS
        return STEPS if self.sides == 2 else 0

    def halo_starts(self):
        if self.sides == 1:
            return [(1 - lax.axis_index("gx")) * self.nx]
        return [0, STEPS + self.nx] if self.sides == 2 else []

    def span(self, level):
        if self.sides == 1:
            index = lax.axis_index("gx")
            return level * index, self.planes - level * (1 - index)
        cut = level if self.sides == 2 else 0
        return cut, self.planes - cut


def prepare(plan, rs, inv, act, v, w, *faces):
    for i in range(plan.nx):
        liquid = act[i].astype(jnp.float32)
        v[i] = rs[i] * liquid
        w[i] = inv[i] * liquid
    if plan.sides == 1:
        starts = [(1 - lax.axis_index("gx")) * (plan.nx - STEPS)]
    else:
        starts = [plan.nx - STEPS, 0]
    for start, face in zip(starts, faces):
        for i in range(STEPS):
            face[0, i] = v[start + i]
            face[1, i] = w[start + i]


def pack_rows(plan, v, w, *refs):
    halos, (first, second) = refs[: plan.sides], refs[plan.sides :]
    even = lax.axis_index("gy") % 2 == 0
    for field, own in enumerate((v, w)):
        sources = [(own, (i,)) for i in range(plan.nx)]
        sources += [(halo, (field, i)) for halo in halos for i in range(STEPS)]
        for p, (ref, at) in enumerate(sources):
            low = ref[at + (pl.ds(0, STEPS), slice(None))]
            high = ref[at + (pl.ds(plan.ny - STEPS, STEPS), slice(None))]
            first[field, pl.ds(p * STEPS, STEPS), :] = jnp.where(even, high, low)
            second[field, pl.ds(p * STEPS, STEPS), :] = jnp.where(even, low, high)


def pack_lanes(plan, v, w, *refs):
    halos, refs = refs[: plan.sides], refs[plan.sides :]
    from_first, from_second, v_ext, w_ext, first, second, packed = refs
    ny = plan.ny
    even_y = lax.axis_index("gy") % 2 == 0
    even_z = lax.axis_index("gz") % 2 == 0
    blank = jnp.zeros((plan.tall, 128), jnp.float32)
    lane = lanes()
    group = lane // WIDE
    right_half = (lane % WIDE) >= WIDE // 2
    for field, (own, ext) in enumerate(((v, v_ext), (w, w_ext))):
        for p in (0, plan.planes + 1):
            ext[p] = blank
        sources = [(own, (i,), 1 + plan.own() + i) for i in range(plan.nx)]
        for halo, start in zip(halos, plan.halo_starts()):
            sources += [(halo, (field, i), 1 + start + i) for i in range(STEPS)]
        for p, (ref, at, where) in enumerate(sources):
            one = from_first[field, pl.ds(p * STEPS, STEPS), :]
            two = from_second[field, pl.ds(p * STEPS, STEPS), :]
            ext[where, pl.ds(0, 8), :] = jnp.zeros((8, 128), jnp.float32)
            ext[where, pl.ds(TOP + ny, 24), :] = jnp.zeros((24, 128), jnp.float32)
            ext[where, pl.ds(TOP, ny), :] = ref[at]
            ext[where, pl.ds(TOP - STEPS, STEPS), :] = jnp.where(even_y, two, one)
            ext[where, pl.ds(TOP + ny, STEPS), :] = jnp.where(even_y, one, two)
        for i in range(plan.deep):
            for r in range(plan.rows // 8):
                block = jnp.zeros((8, 128), jnp.float32)
                for g in range(GROUPS):
                    p = g * plan.deep + i
                    if p < plan.planes:
                        moved = pltpu.roll(ext[1 + p, pl.ds(8 * r, 8), :], WIDE * g + 8, 1)
                        block = jnp.where(group == g, moved, block)
                packed[i, pl.ds(8 * r, 8), :] = block
            for r in range(plan.half // 8):
                upper = packed[i, pl.ds(8 * r, 8), :]
                lower = packed[i, pl.ds(plan.half + 8 * r, 8), :]
                to_right = jnp.where(right_half, pltpu.roll(lower, 8, 1), upper)
                to_left = jnp.where(right_half, lower, pltpu.roll(upper, 120, 1))
                first[field, i, pl.ds(8 * r, 8), :] = jnp.where(even_z, to_right, to_left)
                second[field, i, pl.ds(8 * r, 8), :] = jnp.where(even_z, to_left, to_right)


def coupling(one, two):
    total = jnp.maximum(one + two, 0.25)
    inverse = pl.reciprocal(total, approx=True)
    inverse = inverse * (2.0 - total * inverse)
    return (2.0 / SHIFT) * one * two * inverse


def missing(weight, others):
    total = jnp.zeros_like(weight)
    for other in others:
        total = total + jnp.where(other > 0.0, 0.0, weight)
    return total


def krylov(plan, v_ext, w_ext, from_first, from_second, basis, moments, *scratch):
    side_v, side_w, side_next, cx, cy, cz, cm, dg, sx, sy, sz, sm, sd = scratch
    planes, deep, half, tall = plan.planes, plan.deep, plan.half, plan.tall
    even_z = lax.axis_index("gz") % 2 == 0
    lane = lanes()
    group = lane // WIDE
    spot = lane % WIDE
    right_half = spot >= WIDE // 2
    first_lane, last_lane = lane == 0, lane == 127
    blank8 = jnp.zeros((8, 128), jnp.float32)

    for field, side in enumerate((side_v, side_w)):
        for i in range(deep):
            for r in range(half // 8):
                one = from_first[field, i, pl.ds(8 * r, 8), :]
                two = from_second[field, i, pl.ds(8 * r, 8), :]
                left = jnp.where(even_z, two, one)
                right = jnp.where(even_z, one, two)
                side[i, pl.ds(8 * r, 8), :] = jnp.where(right_half, pltpu.roll(right, 8, 1), left)
                side[i, pl.ds(half + 8 * r, 8), :] = jnp.where(
                    right_half, right, pltpu.roll(left, 120, 1)
                )
            side[i, pl.ds(plan.rows, 16), :] = jnp.zeros((16, 128), jnp.float32)

    def beside_main(ref, side, p, i, turn, at):
        center = ref[p, at, :]
        edge = pltpu.roll(side[i, at, :], turn, 1)
        after = pltpu.roll(jnp.where(first_lane, edge, center), 127, 1)
        before = pltpu.roll(jnp.where(last_lane, edge, center), 1, 1)
        return center, after, before

    def beside_side(ref, side, i, at):
        center = side[i, at, :]
        ends = center
        for g in range(GROUPS):
            p = g * deep + i
            if p < planes:
                ends = jnp.where(group == g, pltpu.roll(ref[1 + p, at, :], WIDE * g + 8, 1), ends)
        after = pltpu.roll(jnp.where(spot == 8, ends, center), 127, 1)
        before = pltpu.roll(jnp.where(spot == 7, ends, center), 1, 1)
        return center, after, before

    def next_plane(side, i, at):
        if i < deep - 1:
            return side[i + 1, at, :]
        return pltpu.roll(side[0, at, :], 128 - WIDE, 1)

    def last_plane(side, i, at):
        if i > 0:
            return side[i - 1, at, :]
        return pltpu.roll(side[deep - 1, at, :], WIDE, 1)

    def place(p):
        g = p // deep
        return p - g * deep, 120 - WIDE * g + jnp.where(WIDE * g > 120, 128, 0)

    table_rows = plan.rows
    for i in range(deep):
        for r in range(table_rows // 8):
            at = pl.ds(8 * r, 8)
            here, after, before = beside_side(w_ext, side_w, i, at)
            sx[i, at, :] = coupling(here, next_plane(side_w, i, at))
            sy[i, pl.ds(8 * r + 8, 8), :] = coupling(here, side_w[i, pl.ds(8 * r + 1, 8), :])
            sz[i, at, :] = coupling(here, after)
            sm[i, at, :] = coupling(here, before)
        sy[i, pl.ds(0, 8), :] = blank8
    for i in range(deep):
        for r in range(table_rows // 8):
            at = pl.ds(8 * r, 8)
            here, after, before = beside_side(w_ext, side_w, i, at)
            above = side_w[i, pl.ds(8 * r - 1, 8), :] if r else pltpu.roll(here, 1, 0)
            others = (
                next_plane(side_w, i, at),
                last_plane(side_w, i, at),
                side_w[i, pl.ds(8 * r + 1, 8), :],
                above,
                after,
                before,
            )
            faces = sx[i, at, :] + last_plane(sx, i, at)
            faces = faces + sy[i, pl.ds(8 * r + 8, 8), :] + sy[i, pl.ds(8 * r + 7, 8), :]
            faces = faces + sz[i, at, :] + sm[i, at, :]
            sd[i, at, :] = faces + missing(here, others) * (1.0 / SHIFT) - 1.0

    cx[0] = jnp.zeros((tall, 128), jnp.float32)

    def tables(p, _):
        i, turn = place(p)
        for r in range(table_rows // 8):
            at = pl.ds(8 * r, 8)
            here, after, before = beside_main(w_ext, side_w, 1 + p, i, turn, at)
            cx[1 + p, at, :] = coupling(here, w_ext[2 + p, at, :])
            cy[1 + p, pl.ds(8 * r + 8, 8), :] = coupling(here, w_ext[1 + p, pl.ds(8 * r + 1, 8), :])
            cz[1 + p, at, :] = coupling(here, after)
            cm[1 + p, at, :] = coupling(here, before)
        cy[1 + p, pl.ds(0, 8), :] = blank8
        for r in range(table_rows // 8):
            at = pl.ds(8 * r, 8)
            here, after, before = beside_main(w_ext, side_w, 1 + p, i, turn, at)
            above = w_ext[1 + p, pl.ds(8 * r - 1, 8), :] if r else pltpu.roll(here, 1, 0)
            others = (
                w_ext[2 + p, at, :],
                w_ext[p, at, :],
                w_ext[1 + p, pl.ds(8 * r + 1, 8), :],
                above,
                after,
                before,
            )
            faces = cx[1 + p, at, :] + cx[p, at, :]
            faces = faces + cy[1 + p, pl.ds(8 * r + 8, 8), :] + cy[1 + p, pl.ds(8 * r + 7, 8), :]
            faces = faces + cz[1 + p, at, :] + cm[1 + p, at, :]
            dg[1 + p, at, :] = faces + missing(here, others) * (1.0 / SHIFT) - 1.0
        return 0

    lax.fori_loop(0, planes, tables, 0)

    for k in range(STEPS):
        for p in (0, planes + 1):
            basis[k, p] = jnp.zeros((tall, 128), jnp.float32)

    for level in range(1, STEPS + 1):
        source = v_ext if level == 1 else basis.at[level - 2]
        target = basis.at[level - 1]
        side_from, side_to = (side_v, side_next) if level % 2 else (side_next, side_v)
        start = TOP - STEPS + level
        blocks = -(-(plan.ny + 2 * (STEPS - level)) // 8)

        def step(p, _):
            i, turn = place(p)
            for r in range(blocks):
                s = start + 8 * r
                at = pl.ds(s, 8)
                here, after, before = beside_main(source, side_from, 1 + p, i, turn, at)
                total = cx[1 + p, at, :] * source[2 + p, at, :]
                total = total + cx[p, at, :] * source[p, at, :]
                total = total + cy[1 + p, pl.ds(s + 8, 8), :] * source[1 + p, pl.ds(s + 1, 8), :]
                total = total + cy[1 + p, pl.ds(s + 7, 8), :] * source[1 + p, pl.ds(s - 1, 8), :]
                total = total + cz[1 + p, at, :] * after
                total = total + cm[1 + p, at, :] * before
                target[1 + p, at, :] = dg[1 + p, at, :] * here - total
            return 0

        low, high = plan.span(level)
        lax.fori_loop(low, high, step, 0)
        if level == STEPS:
            break
        for i in range(deep):
            for r in range(blocks):
                s = start + 8 * r
                at = pl.ds(s, 8)
                here, after, before = beside_side(source, side_from, i, at)
                total = sx[i, at, :] * next_plane(side_from, i, at)
                total = total + last_plane(sx, i, at) * last_plane(side_from, i, at)
                total = total + sy[i, pl.ds(s + 8, 8), :] * side_from[i, pl.ds(s + 1, 8), :]
                total = total + sy[i, pl.ds(s + 7, 8), :] * side_from[i, pl.ds(s - 1, 8), :]
                total = total + sz[i, at, :] * after
                total = total + sm[i, at, :] * before
                side_to[i, at, :] = sd[i, at, :] * here - total

    own = 1 + plan.own()

    def products(p, sums):
        sums = list(sums)
        for r in range(plan.ny // 8):
            at = pl.ds(TOP + 8 * r, 8)
            fields = [v_ext[own + p, at, :]] + [basis[k, own + p, at, :] for k in range(STEPS)]
            for k in range(STEPS + 1):
                sums[2 * k] = sums[2 * k] + fields[k] * fields[k]
                if k < STEPS:
                    sums[2 * k + 1] = sums[2 * k + 1] + fields[k] * fields[k + 1]
        return tuple(sums)

    sums = lax.fori_loop(0, plan.nx, products, (blank8,) * (2 * STEPS + 1))
    line = jnp.zeros((1, 128), jnp.float32)
    for j, part in enumerate(sums):
        line = jnp.where(lanes((1, 128)) == j, jnp.sum(part), line)
    for j in range(moments.shape[0]):
        moments[j] = line


def weigh(parts):
    line = jnp.sum(parts, axis=0)
    line = jnp.broadcast_to(line, (8, 128))
    moment = []
    for j in range(2 * STEPS + 1):
        picked = jnp.where(lanes() == j, line, 0.0)
        moment.append(jnp.broadcast_to(jnp.sum(picked, axis=1, keepdims=True), (8, 128)))
    count = STEPS + 1
    gram = [[moment[i + j] for j in range(count)] for i in range(count)]
    sign = [1.0 if k % 2 == 0 else -1.0 for k in range(count)]
    rhs = [jnp.full((8, 128), s, jnp.float32) for s in sign]
    inverse = []
    for p in range(count):
        inverse.append(1.0 / gram[p][p])
        for i in range(p + 1, count):
            factor = gram[p][i] * inverse[p]
            for j in range(i, count):
                gram[i][j] = gram[i][j] - factor * gram[p][j]
            rhs[i] = rhs[i] - factor * rhs[p]
    solved = [None] * count
    for p in reversed(range(count)):
        running = rhs[p]
        for j in range(p + 1, count):
            running = running - gram[p][j] * solved[j]
        solved[p] = running * inverse[p]
    scale = sign[0] * solved[0]
    for k in range(1, count):
        scale = scale + sign[k] * solved[k]
    scale = 1.0 / scale
    leftover = [s * scale for s in solved]
    coefficients = [(1.0 - leftover[0]) * (1.0 / SHIFT)]
    for k in range(1, STEPS):
        coefficients.append(leftover[k] * (-1.0 / SHIFT) - coefficients[-1])
    return coefficients, leftover


def combine(plan, chunk, parts, v_ext, basis, solution_field, residual, weights):
    @pl.when(pl.program_id(0) == 0)
    def _():
        coefficients, leftover = weigh(parts[...])
        for k, value in enumerate(coefficients + leftover):
            weights[k] = value

    own = 1 + plan.own() + pl.program_id(0) * chunk

    def plane(p, _):
        for r in range(plan.ny // 8):
            at = pl.ds(TOP + 8 * r, 8)
            fields = [v_ext[own + p, at, :]] + [basis[k, own + p, at, :] for k in range(STEPS)]
            out = weights[0] * fields[0]
            for k in range(1, STEPS):
                out = out + weights[k] * fields[k]
            solution_field[p, pl.ds(8 * r, 8), :] = out
            out = weights[STEPS] * fields[0]
            for k in range(1, STEPS + 1):
                out = out + weights[STEPS + k] * fields[k]
            residual[p, pl.ds(8 * r, 8), :] = out
        return 0

    lax.fori_loop(0, chunk, plane, 0)


def swaps(first, second, axis):
    count = lax.axis_size(axis)
    ones = [(i, i + 1) for i in range(0, count - 1, 2)]
    twos = [(i, i + 1) for i in range(1, count - 1, 2)]
    return tuple(
        lax.ppermute(value, axis, pairs + [(b, a) for a, b in pairs])
        for value, pairs in ((first, ones), (second, twos))
    )


def on_device(mesh, right_side, inv_density, active):
    nx, ny, nz = right_side.shape
    plan = Plan(mesh, nx, ny, nz)
    field = kept((nx, ny, nz))
    face = kept((2, STEPS, ny, nz))
    v, w, *faces = call(
        functools.partial(prepare, plan), [field, field] + [face] * plan.sides, "prepare"
    )(right_side, inv_density, active)
    if plan.sides == 1:
        halos = [lax.ppermute(faces[0], "gx", [(0, 1), (1, 0)])]
    else:
        steps = [(i, i + 1) for i in range(plan.gx - 1)]
        pairs = [steps, [(b, a) for a, b in steps]]
        halos = [lax.ppermute(f, "gx", p) for f, p in zip(faces, pairs)]
    v, w, *halos = [resident(a) for a in [v, w] + halos]
    strip = kept((2, plan.planes * STEPS, 128))
    first, second = call(functools.partial(pack_rows, plan), [strip, strip], "rows")(v, w, *halos)
    first, second = swaps(first, second, "gy")
    extended = kept((plan.planes + 2, plan.tall, 128))
    column = kept((2, plan.deep, plan.half, 128))
    v_ext, w_ext, first, second = call(
        functools.partial(pack_lanes, plan),
        [extended, extended, column, column],
        "columns",
        scratch=[kept((plan.deep, plan.rows, 128))],
    )(v, w, *halos, resident(first), resident(second))
    first, second = swaps(first, second, "gz")
    v_ext = resident(v_ext)
    devices = plan.gx * plan.gy * plan.gz
    side = (plan.deep, plan.tall, 128)
    table = (plan.planes + 2, plan.tall, 128)
    basis, moments = call(
        functools.partial(krylov, plan),
        [kept((STEPS,) + table), kept((devices, 1, 128))],
        "krylov",
        scratch=[kept(side)] * 3 + [kept(table)] * 5 + [kept(side)] * 5,
    )(v_ext, resident(w_ext), resident(first), resident(second))
    parts = lax.all_to_all(moments, AXES, 0, 0, tiled=True)
    chunk = 4
    block = pl.BlockSpec((chunk, ny, nz), lambda i: (i, 0, 0))
    shape = jax.ShapeDtypeStruct((nx, ny, nz), jnp.float32)
    out, residual = pl.pallas_call(
        functools.partial(combine, plan, chunk),
        out_shape=[shape, shape],
        grid=(nx // chunk,),
        in_specs=[vmem_spec()] * 3,
        out_specs=[block, block],
        scratch_shapes=[kept((2 * STEPS + 1, 8, 128))],
        compiler_params=pltpu.CompilerParams(vmem_limit_bytes=40 << 20),
        name="combine",
    )(resident(parts), v_ext, resident(basis))
    return out, residual


def solution(mesh):
    placed = P("gx", "gy", "gz")
    return jax.shard_map(
        functools.partial(on_device, mesh),
        mesh=mesh,
        in_specs=(placed,) * 3,
        out_specs=(placed, placed),
        check_vma=False,
    )
```

time: 249 us -> 74.5 us (0.30)
  other arithmetic: 62.3 us -> 0 us
  between operations: 47.5 us -> 0.69 us
  local copies, waits for them, and re-layouts: 48.6 us -> 3.12 us
  Pallas kernels: 0 us -> 38.2 us
  starting transfers between devices: 31.4 us -> 6.65 us
  blocking collectives: 43.2 us -> 18.5 us
  matrix products: 13.6 us -> 0 us
  waiting for transfers between devices: 0.03 us -> 7.05 us
    psum x1 -> x0, blocking collectives: 43.2 us -> none  [on_device(): gram_matrix = lax.psum(local_gram, ('gx', 'gy', 'gz'))]
    pallas_call x0 -> x5, Pallas kernels: none -> 38.2 us  [the longest x1 34.8 us: on_device(): call(functools.partial(krylov, plan), [kept((STEPS,) + table), kept((devi...]
    div x7 -> x0, other arithmetic: 31.8 us -> none  [the longest x6 31.8 us: next_basis(): return (image_field - basis_shift * previous) / basis_scale]
    slice x30 -> x0, local copies, waits for them, and re-layouts: 25.3 us -> none  [the longest x6 7.57 us: extended(): lax.slice_in_dim(cells, cells.shape[dim] - width, cells.shape[dim], axis=...]
    ppermute x12 -> x5, starting transfers between devices: 31.4 us -> 6.65 us  [the longest x4 6.13 us: swaps(): lax.ppermute(value, axis, pairs + [(b, a) for a, b in pairs])]
    add x10 -> x0, other arithmetic: 19.3 us -> none  [the longest x1 8.03 us: face_table(): diagonal = diagonal + face_value]
    all_to_all x0 -> x1, blocking collectives: none -> 18.5 us  [on_device(): parts = lax.all_to_all(moments, AXES, 0, 0, tiled=True)]
    dot_general x3 -> x0, matrix products: 13.6 us -> none  [the longest x1 12.6 us: on_device(): local_gram = jnp.dot(stacked, stacked.T, precision=lax.Precision.HIGHEST)]
  transfers between devices with their start and end apart: 12 -> 5, of which waited for: 0 -> 3; matrix products, arithmetic and copies ran while one was open for 12% -> 0% of each run, Pallas kernels for 0% -> 0%
where the time goes in v1:
time: 74.5 us; the launch traced here: 74.2 us
  Pallas kernels  38.2 us (51%)
  blocking collectives  18.5 us (25%)
  waiting for transfers between devices  7.05 us (9%)
  starting transfers between devices  6.65 us (9%)
  local copies, waits for them, and re-layouts  3.12 us (4%)
    pallas_call x1, Pallas kernels, on_device(): call(functools.partial(krylov, plan), [kept((STEPS,) + table), kept((devi...  34.8 us
    all_to_all x1, blocking collectives, on_device(): parts = lax.all_to_all(moments, AXES, 0, 0, tiled=True)  18.5 us
    ppermute x4, starting transfers between devices, swaps(): lax.ppermute(value, axis, pairs + [(b, a) for a, b in pairs])  6.13 us
    ppermute x4, waiting for transfers between devices, swaps(): lax.ppermute(value, axis, pairs + [(b, a) for a, b in pairs])  5.7 us
    unnamed x6, local copies, waits for them, and re-layouts  3.12 us
    pallas_call x1, Pallas kernels, on_device(): pl.pallas_call(functools.partial(combine, plan, chunk), out_shape=[shape,...  2.06 us
  transfers between devices with their start and end apart: 5, of which 3 were waited for; matrix products, arithmetic and copies ran while one was open for 0% of the time, Pallas kernels for 0%

profile of v1, /device:TPU:0, one launch (start us, length us, event | category | flops | bytes accessed | tf_op | source)
XLA Modules:
  0.0 74.2 jit_solution(9476891769611651167)
XLA Ops:
  0.6 0.0 copy-start
  0.6 1.0 %copy-done = f32[16,64,128]{2,1,0:T(8,128)S(1)} copy-done((f32[16,64,128]{2,1,0:T(8,128)S(1)}, f32[16,64,128]{2,1,0:T(8,128)}, u32[]{:S(2)}) %copy-start) | copy-done | bytes 524312
  1.7 0.0 copy-start.1
  1.7 1.0 %copy-done.1 = f32[16,64,128]{2,1,0:T(8,128)S(1)} copy-done((f32[16,64,128]{2,1,0:T(8,128)S(1)}, f32[16,64,128]{2,1,0:T(8,128)}, u32[]{:S(2)}) %copy-start.1) | copy-done | bytes 524312
  2.7 0.0 copy-start.2
  2.7 1.0 %copy-done.2 = s32[16,64,128]{2,1,0:T(8,128)S(1)} copy-done((s32[16,64,128]{2,1,0:T(8,128)S(1)}, s32[16,64,128]{2,1,0:T(8,128)}, u32[]{:S(2)}) %copy-start.2) | copy-done | bytes 524312
  3.8 0.1 prepare.1
  3.9 0.5 collective-permute-start
  4.4 1.3 %collective-permute-done.refs_0_ = f32[2,6,64,128]{3,2,1,0:T(8,128)S(1)} collective-permute-done((f32[2,6,64,128]{3,2,1,0:T(8,128)S(1)}, f32[2,6,64,128]{3,2,1,0:T(8,128)S(1)}, u32[]{:S(2)}, u32[]{:S(2)}) %collective-permute-start) | collective-permute-done | bytes 393248 | tf_op jit(solution)/shard_map/ppermute | solution.py:422
  5.8 2.9 %collective-permute-start.1 = (f32[2,132,128]{2,1,0:T(8,128)S(1)}, f32[2,132,128]{2,1,0:T(8,128)S(1)}, u32[]{:S(2)}, u32[]{:S(2)}) collective-permute-start(f32[2,132,128]{2,1,0:T(8,128)S(1)} %get-tuple-element.16), channel_id=1, source_target_pairs={{0,4},{8,12},{4,0},{12,8},{1,5},{9,13},{5,1},{13,9},{2,6},{10,14},... | collective-permute-start | bytes 405512 | tf_op jit(solution)/shard_map/ppermute | solution.py:408
  8.7 0.7 collective-permute-start.2
  9.4 3.3 %collective-permute-done.1.refs_1_ = f32[2,132,128]{2,1,0:T(8,128)S(1)} collective-permute-done((f32[2,132,128]{2,1,0:T(8,128)S(1)}, f32[2,132,128]{2,1,0:T(8,128)S(1)}, u32[]{:S(2)}, u32[]{:S(2)}) %collective-permute-start.1) | collective-permute-done | bytes 135200 | tf_op jit(solution)/shard_map/ppermute | solution.py:408
  12.7 0.0 collective-permute-done.2.refs_2_
  12.7 1.1 %columns.1 = (f32[24,96,128]{2,1,0:T(8,128)S(1)}, f32[24,96,128]{2,1,0:T(8,128)S(1)}, f32[2,3,40,128]{3,2,1,0:T(8,128)S(1)}, f32[2,3,40,128]{3,2,1,0:T(8,128)S(1)}) custom-call(f32[16,64,128]{2,1,0:T(8,128)S(1)} %get-tuple-element.13.v, f32[16,64,128]{2,1,0:T(8,128)S(1)} %get-tuple-element.14.w, f32[2,6,64,128]{3,2,1,0:T(8,128)S(1)} %collective-permute-done.refs_0_, ...), custom_call_target="tpu_custom_call" | custom-call | bytes 1048576 | tf_op jit(solution)/shard_map/columns/pallas_call | solution.py:433
  13.8 1.9 %collective-permute-start.3 = (f32[2,3,40,128]{3,2,1,0:T(8,128)S(1)}, f32[2,3,40,128]{3,2,1,0:T(8,128)S(1)}, u32[]{:S(2)}, u32[]{:S(2)}) collective-permute-start(f32[2,3,40,128]{3,2,1,0:T(8,128)S(1)} %get-tuple-element.20), channel_id=1, source_target_pairs={{0,1},{2,3},{1,0},{3,2},{4,5},{6,7},{5,4},{7,6},{8,9},{10,11},{9,8... | collective-permute-start | bytes 368648 | tf_op jit(solution)/shard_map/ppermute | solution.py:408
  15.7 0.7 collective-permute-start.4
  16.4 2.4 %collective-permute-done.3.from_first = f32[2,3,40,128]{3,2,1,0:T(8,128)S(1)} collective-permute-done((f32[2,3,40,128]{3,2,1,0:T(8,128)S(1)}, f32[2,3,40,128]{3,2,1,0:T(8,128)S(1)}, u32[]{:S(2)}, u32[]{:S(2)}) %collective-permute-start.3) | collective-permute-done | bytes 122912 | tf_op jit(solution)/shard_map/ppermute | solution.py:408
  18.8 0.0 collective-permute-done.4.from_second
  18.8 34.8 %krylov.1 = (f32[6,24,96,128]{3,2,1,0:T(8,128)S(1)}, f32[32,1,128]{2,1,0:T(1,128)S(1)}) custom-call(f32[24,96,128]{2,1,0:T(8,128)S(1)} %get-tuple-element.18.v_ext, f32[24,96,128]{2,1,0:T(8,128)S(1)} %get-tuple-element.19.w_ext, f32[2,3,40,128]{3,2,1,0:T(8,128)S(1)} %collective-permute-done.3.from_first, f32[2,3,40,128]{3,2,1,0:T(8,128)S(1)} %collective-permute-done.4.from_second), custom_call_target="tpu_custom_call" | custom-call | bytes 1048576 | tf_op jit(solution)/shard_map/krylov/pallas_call | solution.py:444
  53.6 18.5 %all_to_all.5.parts = f32[32,1,128]{2,1,0:T(1,128)S(1)} all-to-all(f32[32,1,128]{2,1,0:T(1,128)S(1)} %get-tuple-element.22), channel_id=1, replica_groups=mesh['gx'=2,'gy'=4,'gz'=4] {'gx','gy','gz'}, dimensions={0} | all-to-all | bytes 32768 | tf_op jit(solution)/shard_map/all_to_all | solution.py:450
  72.2 2.1 %combine.1 = (f32[16,64,128]{2,1,0:T(8,128)}, f32[16,64,128]{2,1,0:T(8,128)}) custom-call(f32[32,1,128]{2,1,0:T(1,128)S(1)} %all_to_all.5.parts, f32[24,96,128]{2,1,0:T(8,128)S(1)} %get-tuple-element.18.v_ext, f32[6,24,96,128]{3,2,1,0:T(8,128)S(1)} %get-tuple-element.23.basis), custom_call_target="tpu_custom_call" | custom-call | tf_op jit(solution)/shard_map/combine/pallas_call | solution.py:454
  (1 shorter events, 0.0 us)
Async XLA Ops:
  0.6 1.0 %copy-start = (f32[16,64,128]{2,1,0:T(8,128)S(1)}, f32[16,64,128]{2,1,0:T(8,128)}, u32[]{:S(2)}) copy-start(f32[16,64,128]{2,1,0:T(8,128)} %rs.1) | copy-start | bytes 1572868
  1.7 1.0 %copy-start.1 = (f32[16,64,128]{2,1,0:T(8,128)S(1)}, f32[16,64,128]{2,1,0:T(8,128)}, u32[]{:S(2)}) copy-start(f32[16,64,128]{2,1,0:T(8,128)} %inv.1) | copy-start | bytes 1572868
  2.7 1.0 %copy-start.2 = (s32[16,64,128]{2,1,0:T(8,128)S(1)}, s32[16,64,128]{2,1,0:T(8,128)}, u32[]{:S(2)}) copy-start(s32[16,64,128]{2,1,0:T(8,128)} %act.1) | copy-start | bytes 1572868
  3.9 1.9 %collective-permute-start = (f32[2,6,64,128]{3,2,1,0:T(8,128)S(1)}, f32[2,6,64,128]{3,2,1,0:T(8,128)S(1)}, u32[]{:S(2)}, u32[]{:S(2)}) collective-permute-start(f32[2,6,64,128]{3,2,1,0:T(8,128)S(1)} %get-tuple-element.15), channel_id=1, source_target_pairs={{0,16},{16,0},{1,17},{17,1},{2,18},{18,2},{3,19},{19,3},{4,20},{20... | collective-permute-start | bytes 1179656 | tf_op jit(solution)/shard_map/ppermute | solution.py:422
  5.8 6.9 %collective-permute-start.1 = (f32[2,132,128]{2,1,0:T(8,128)S(1)}, f32[2,132,128]{2,1,0:T(8,128)S(1)}, u32[]{:S(2)}, u32[]{:S(2)}) collective-permute-start(f32[2,132,128]{2,1,0:T(8,128)S(1)} %get-tuple-element.16), channel_id=1, source_target_pairs={{0,4},{8,12},{4,0},{12,8},{1,5},{9,13},{5,1},{13,9},{2,6},{10,14},... | collective-permute-start | bytes 405512 | tf_op jit(solution)/shard_map/ppermute | solution.py:408
  8.7 4.0 %collective-permute-start.2 = (f32[2,132,128]{2,1,0:T(8,128)S(1)}, f32[2,132,128]{2,1,0:T(8,128)S(1)}, u32[]{:S(2)}, u32[]{:S(2)}) collective-permute-start(f32[2,132,128]{2,1,0:T(8,128)S(1)} %get-tuple-element.17), channel_id=1, source_target_pairs={{4,8},{8,4},{5,9},{9,5},{6,10},{10,6},{7,11},{11,7},{20,24},{24,20... | collective-permute-start | bytes 405512 | tf_op jit(solution)/shard_map/ppermute | solution.py:408
  13.8 4.9 %collective-permute-start.3 = (f32[2,3,40,128]{3,2,1,0:T(8,128)S(1)}, f32[2,3,40,128]{3,2,1,0:T(8,128)S(1)}, u32[]{:S(2)}, u32[]{:S(2)}) collective-permute-start(f32[2,3,40,128]{3,2,1,0:T(8,128)S(1)} %get-tuple-element.20), channel_id=1, source_target_pairs={{0,1},{2,3},{1,0},{3,2},{4,5},{6,7},{5,4},{7,6},{8,9},{10,11},{9,8... | collective-permute-start | bytes 368648 | tf_op jit(solution)/shard_map/ppermute | solution.py:408
  15.7 3.1 %collective-permute-start.4 = (f32[2,3,40,128]{3,2,1,0:T(8,128)S(1)}, f32[2,3,40,128]{3,2,1,0:T(8,128)S(1)}, u32[]{:S(2)}, u32[]{:S(2)}) collective-permute-start(f32[2,3,40,128]{3,2,1,0:T(8,128)S(1)} %get-tuple-element.21), channel_id=1, source_target_pairs={{1,2},{2,1},{5,6},{6,5},{9,10},{10,9},{13,14},{14,13},{17,18},{18,... | collective-permute-start | bytes 368648 | tf_op jit(solution)/shard_map/ppermute | solution.py:408

commit v2 on v1

v2 whole, which is shorter than its diff:
```python
import functools

import jax
import jax.numpy as jnp
from jax import lax
from jax.experimental import pallas as pl
from jax.experimental.pallas import tpu as pltpu
from jax.sharding import PartitionSpec as P

STEPS = 6
SHIFT = 7.0
GROUPS = 8
WIDE = 16
RIMS = 3
BAND = 40
UNROLL = 3
TOP = 8
VMEM = pltpu.VMEM
AXES = ("gx", "gy", "gz")


def vmem_spec():
    return pl.BlockSpec(memory_space=VMEM)


def resident(array):
    return pltpu.with_memory_space_constraint(array, VMEM)


def call(body, outs, name, scratch=(), grid=None, out_specs=None, limit=40, flops=0):
    return pl.pallas_call(
        body,
        out_shape=outs,
        grid=grid or (),
        out_specs=out_specs if out_specs is not None else [vmem_spec() for _ in outs],
        scratch_shapes=list(scratch),
        compiler_params=pltpu.CompilerParams(vmem_limit_bytes=limit << 20),
        cost_estimate=pl.CostEstimate(flops=flops, bytes_accessed=1 << 20, transcendentals=0),
        name=name,
    )


def kept(shape):
    return pltpu.VMEM(shape, jnp.float32)


def lanes(shape=(8, 128)):
    return lax.broadcasted_iota(jnp.int32, shape, len(shape) - 1)


class Plan:
    def __init__(self, mesh, nx, ny, nz):
        self.gx, self.gy, self.gz = (mesh.shape[a] for a in AXES)
        self.nx, self.ny, self.nz = nx, ny, nz
        self.sides = min(self.gx - 1, 2)
        self.planes = nx + STEPS * self.sides
        self.deep = self.planes // GROUPS + 1
        self.rows = ny + 16
        self.half = self.rows // 2
        self.tall = self.rows + 16
        self.rim = self.planes // RIMS + 1

    def own(self):
        if self.sides == 1:
            return lax.axis_index("gx") * STEPS
        return STEPS if self.sides == 2 else 0

    def halo_starts(self):
        if self.sides == 1:
            return [(1 - lax.axis_index("gx")) * self.nx]
        return [0, STEPS + self.nx] if self.sides == 2 else []

    def span(self, level):
        if self.sides == 1:
            index = lax.axis_index("gx")
            return level * index, self.planes - level
        cut = level if self.sides == 2 else 0
        return cut, self.planes - 2 * cut


def prepare(plan, rs, inv, act, v, w, *faces):
    for i in range(plan.nx):
        liquid = act[i].astype(jnp.float32)
        v[i] = rs[i] * liquid
        w[i] = inv[i] * liquid * (2.0 / SHIFT)
    if plan.sides == 1:
        starts = [(1 - lax.axis_index("gx")) * (plan.nx - STEPS)]
    else:
        starts = [plan.nx - STEPS, 0]
    for start, face in zip(starts, faces):
        for i in range(STEPS):
            face[0, i] = v[start + i]
            face[1, i] = w[start + i]


def pack_rows(plan, v, w, *refs):
    halos, (first, second) = refs[: plan.sides], refs[plan.sides :]
    even = lax.axis_index("gy") % 2 == 0
    for field, own in enumerate((v, w)):
        sources = [(own, (i,)) for i in range(plan.nx)]
        sources += [(halo, (field, i)) for halo in halos for i in range(STEPS)]
        for p, (ref, at) in enumerate(sources):
            low = ref[at + (pl.ds(0, STEPS), slice(None))]
            high = ref[at + (pl.ds(plan.ny - STEPS, STEPS), slice(None))]
            first[field, pl.ds(p * STEPS, STEPS), :] = jnp.where(even, high, low)
            second[field, pl.ds(p * STEPS, STEPS), :] = jnp.where(even, low, high)


def pack_lanes(plan, v, w, *refs):
    halos, refs = refs[: plan.sides], refs[plan.sides :]
    from_first, from_second, v_ext, w_ext, first, second, packed = refs
    ny = plan.ny
    even_y = lax.axis_index("gy") % 2 == 0
    even_z = lax.axis_index("gz") % 2 == 0
    blank = jnp.zeros((plan.tall, 128), jnp.float32)
    lane = lanes()
    group = lane // WIDE
    right_half = (lane % WIDE) >= WIDE // 2
    for field, (own, ext) in enumerate(((v, v_ext), (w, w_ext))):
        ext[0] = blank
        for p in range(plan.planes + 1, ext.shape[0]):
            ext[p] = blank
        sources = [(own, (i,), 1 + plan.own() + i) for i in range(plan.nx)]
        for halo, start in zip(halos, plan.halo_starts()):
            sources += [(halo, (field, i), 1 + start + i) for i in range(STEPS)]
        for p, (ref, at, where) in enumerate(sources):
            one = from_first[field, pl.ds(p * STEPS, STEPS), :]
            two = from_second[field, pl.ds(p * STEPS, STEPS), :]
            ext[where, pl.ds(0, 8), :] = jnp.zeros((8, 128), jnp.float32)
            ext[where, pl.ds(TOP + ny, 24), :] = jnp.zeros((24, 128), jnp.float32)
            ext[where, pl.ds(TOP, ny), :] = ref[at]
            ext[where, pl.ds(TOP - STEPS, STEPS), :] = jnp.where(even_y, two, one)
            ext[where, pl.ds(TOP + ny, STEPS), :] = jnp.where(even_y, one, two)
        for i in range(plan.deep):
            for r in range(plan.rows // 8):
                block = jnp.zeros((8, 128), jnp.float32)
                for g in range(GROUPS):
                    p = g * plan.deep + i
                    if p < plan.planes:
                        moved = pltpu.roll(ext[1 + p, pl.ds(8 * r, 8), :], WIDE * g + 8, 1)
                        block = jnp.where(group == g, moved, block)
                packed[i, pl.ds(8 * r, 8), :] = block
            for r in range(plan.half // 8):
                upper = packed[i, pl.ds(8 * r, 8), :]
                lower = packed[i, pl.ds(plan.half + 8 * r, 8), :]
                to_right = jnp.where(right_half, pltpu.roll(lower, 8, 1), upper)
                to_left = jnp.where(right_half, lower, pltpu.roll(upper, 120, 1))
                first[field, i, pl.ds(8 * r, 8), :] = jnp.where(even_z, to_right, to_left)
                second[field, i, pl.ds(8 * r, 8), :] = jnp.where(even_z, to_left, to_right)


def coupling(one, two):
    total = jnp.maximum(one + two, 0.0625)
    inverse = pl.reciprocal(total, approx=True)
    inverse = inverse * (2.0 - total * inverse)
    return (one * two) * inverse


def face_tables(weight, tables, planes, blocks):
    cx, cy, cz, dg = tables

    def faces(p, _):
        for r in range(blocks):
            at = pl.ds(8 * r, 8)
            here = weight[p, at, :]
            cx[p, at, :] = coupling(here, weight[p + 1, at, :])
            cy[p, pl.ds(8 * r + 8, 8), :] = coupling(here, weight[p, pl.ds(8 * r + 1, 8), :])
            cz[p, at, :] = coupling(here, pltpu.roll(here, 127, 1))
        return 0

    lax.fori_loop(0, planes + 1, faces, 0)

    def diagonal(trip, _):
        for u in range(2):
            p = 1 + 2 * trip + u
            for r in range(blocks):
                at = pl.ds(8 * r, 8)
                air = 0.5 * weight[p, at, :]
                total = jnp.full((8, 128), -1.0, jnp.float32)
                ahead = cz[p, at, :]
                for face in (
                    cx[p, at, :],
                    cx[p - 1, at, :],
                    cy[p, pl.ds(8 * r + 8, 8), :],
                    cy[p, pl.ds(8 * r + 7, 8), :],
                    ahead,
                    pltpu.roll(ahead, 1, 1),
                ):
                    total = total + jnp.where(face > 0.0, face, air)
                dg[p, at, :] = total
        return 0

    lax.fori_loop(0, (planes + 1) // 2, diagonal, 0)


def advance(source, target, tables, first, trips, unroll, start, blocks):
    cx, cy, cz, dg = tables

    def body(trip, _):
        base = first + trip * unroll
        for r in range(blocks):
            s = start + 8 * r
            at = pl.ds(s, 8)
            fields = [source[base + u, at, :] for u in range(unroll + 2)]
            walls = [cx[base + u, at, :] for u in range(unroll + 1)]
            for u in range(unroll):
                p = base + u + 1
                here, ahead = fields[u + 1], cz[p, at, :]
                after = pltpu.roll(here, 127, 1)
                behind = pltpu.roll(ahead * here, 1, 1)
                total = walls[u + 1] * fields[u + 2] + walls[u] * fields[u]
                total = total + cy[p, pl.ds(s + 8, 8), :] * source[p, pl.ds(s + 1, 8), :]
                total = total + cy[p, pl.ds(s + 7, 8), :] * source[p, pl.ds(s - 1, 8), :]
                total = total + (ahead * after + behind)
                target[p, at, :] = dg[p, at, :] * here - total
        return 0

    lax.fori_loop(0, trips, body, 0)


def level_rows(plan, level):
    return TOP - STEPS + level, -(-(plan.ny + 2 * (STEPS - level)) // 8)


def products(fields, sums):
    for k in range(STEPS + 1):
        sums[2 * k] = sums[2 * k] + fields[k] * fields[k]
        if k < STEPS:
            sums[2 * k + 1] = sums[2 * k + 1] + fields[k] * fields[k + 1]
    return sums


def inner(plan, v_ext, w_ext, *refs):
    basis, (sums_ref, rim_v, rim_w), tables = refs[:STEPS], refs[STEPS : STEPS + 3], refs[STEPS + 3 :]
    planes = plan.planes
    blank8 = jnp.zeros((8, 128), jnp.float32)
    face_tables(w_ext, tables, planes, plan.rows // 8)
    for ref in basis:
        ref[0] = jnp.zeros(ref.shape[1:], jnp.float32)
        ref[planes + 1] = jnp.zeros(ref.shape[1:], jnp.float32)
    source = v_ext
    for level in range(1, STEPS + 1):
        low, count = plan.span(level)
        trips = -(-count // UNROLL)
        low = jnp.minimum(low, planes - UNROLL * trips)
        start, blocks = level_rows(plan, level)
        advance(source, basis[level - 1], tables, low, trips, UNROLL, start, blocks)
        source = basis[level - 1]

    own = 1 + plan.own()

    def gather(p, sums):
        sums = list(sums)
        for r in range(plan.ny // 8):
            at = pl.ds(TOP + 8 * r, 8)
            sums = products([ref[own + p, at, :] for ref in (v_ext,) + tuple(basis)], sums)
        return tuple(sums)

    sums = lax.fori_loop(0, plan.nx, gather, (blank8,) * (2 * STEPS + 1))
    lane = lanes()
    fresh = (lane >= STEPS) & (lane < 128 - STEPS)
    for j, part in enumerate(sums):
        sums_ref[j] = jnp.where(fresh, part, 0.0)

    band, spot = lane // BAND, lane % BAND
    for ext, rim in ((v_ext, rim_v), (w_ext, rim_w)):
        def fill(r, _):
            at = pl.ds(pl.multiple_of(8 * r, 8), 8)
            for i in range(plan.rim):
                block = blank8
                for g in range(RIMS):
                    p = g * plan.rim + i
                    if p < planes:
                        value = ext[1 + p, at, :]
                        high = pltpu.roll(value, BAND * g + 12, 1)
                        low = pltpu.roll(value, (BAND * g + 28) % 128, 1)
                        block = jnp.where((band == g) & (spot < 12), high, block)
                        block = jnp.where((band == g) & (spot >= 28), low, block)
                rim[1 + i, at, :] = block
            return 0

        lax.fori_loop(0, plan.rows // 8, fill, 0)


def outer(plan, first, second, rim_v, rim_w, sums_ref, *refs):
    basis, (moments, rim_0, rim_s), tables = refs[:STEPS], refs[STEPS : STEPS + 3], refs[STEPS + 3 :]
    planes, deep, half, rim = plan.planes, plan.deep, plan.half, plan.rim
    even_z = lax.axis_index("gz") % 2 == 0
    lane = lanes()
    right_half = (lane % WIDE) >= WIDE // 2
    band, spot = lane // BAND, lane % BAND
    halo = (spot >= 12) & (spot < 28)
    blank8 = jnp.zeros((8, 128), jnp.float32)

    def wrap(ref, start, blocks):
        for r in range(blocks):
            at = pl.ds(start + 8 * r, 8)
            ref[0, at, :] = pltpu.roll(ref[rim, at, :], BAND, 1)
            ref[rim + 1, at, :] = pltpu.roll(ref[1, at, :], 128 - BAND, 1)

    for field, (own, full) in enumerate(((rim_v, rim_0), (rim_w, rim_s))):
        columns = [[None] * (2 * (half // 8)) for _ in range(deep)]
        for i in range(deep):
            for r in range(half // 8):
                one = first[field, i, pl.ds(8 * r, 8), :]
                two = second[field, i, pl.ds(8 * r, 8), :]
                left = jnp.where(even_z, two, one)
                right = jnp.where(even_z, one, two)
                columns[i][r] = jnp.where(right_half, pltpu.roll(left, 8, 1), right)
                columns[i][half // 8 + r] = jnp.where(right_half, left, pltpu.roll(right, 120, 1))
        for r in range(plan.rows // 8):
            at = pl.ds(8 * r, 8)
            for i in range(rim):
                block = own[1 + i, at, :]
                for g in range(RIMS):
                    p = g * rim + i
                    if p < planes:
                        turn = (BAND * g + 12 - WIDE * (p // deep)) % 128
                        moved = pltpu.roll(columns[p % deep][r], turn, 1)
                        block = jnp.where((band == g) & halo, moved, block)
                full[1 + i, at, :] = block
        for i in range(rim + 2):
            full[i, pl.ds(plan.rows, 16), :] = jnp.zeros((16, 128), jnp.float32)
        wrap(full, 0, plan.rows // 8)

    face_tables(rim_s, tables, rim, plan.rows // 8)
    source = rim_0
    for level in range(1, STEPS + 1):
        start, blocks = level_rows(plan, level)
        advance(source, basis[level - 1], tables, 0, rim // 2, 2, start, blocks)
        source = basis[level - 1]
        if level < STEPS:
            wrap(source, start, blocks)

    own = plan.own()
    fresh = ((spot >= 6) & (spot < 12)) | ((spot >= 28) & (spot < 34))
    sums = [sums_ref[j] for j in range(2 * STEPS + 1)]
    for i in range(rim):
        part = [blank8] * (2 * STEPS + 1)
        for r in range(plan.ny // 8):
            at = pl.ds(TOP + 8 * r, 8)
            part = products([ref[1 + i, at, :] for ref in (rim_0,) + tuple(basis)], part)
        plane = band * rim + i
        mine = fresh & (plane >= own) & (plane < own + plan.nx)
        sums = [a + jnp.where(mine, b, 0.0) for a, b in zip(sums, part)]
    line = jnp.zeros((1, 128), jnp.float32)
    for j, part in enumerate(sums):
        line = jnp.where(lanes((1, 128)) == j, jnp.sum(part), line)
    for j in range(moments.shape[0]):
        moments[j] = line


def weigh(parts):
    line = jnp.sum(parts, axis=0)
    line = jnp.broadcast_to(line, (8, 128))
    moment = []
    for j in range(2 * STEPS + 1):
        picked = jnp.where(lanes() == j, line, 0.0)
        moment.append(jnp.broadcast_to(jnp.sum(picked, axis=1, keepdims=True), (8, 128)))
    count = STEPS + 1
    gram = [[moment[i + j] for j in range(count)] for i in range(count)]
    sign = [1.0 if k % 2 == 0 else -1.0 for k in range(count)]
    rhs = [jnp.full((8, 128), s, jnp.float32) for s in sign]
    inverse = []
    for p in range(count):
        inverse.append(1.0 / gram[p][p])
        for i in range(p + 1, count):
            factor = gram[p][i] * inverse[p]
            for j in range(i, count):
                gram[i][j] = gram[i][j] - factor * gram[p][j]
            rhs[i] = rhs[i] - factor * rhs[p]
    solved = [None] * count
    for p in reversed(range(count)):
        running = rhs[p]
        for j in range(p + 1, count):
            running = running - gram[p][j] * solved[j]
        solved[p] = running * inverse[p]
    scale = sign[0] * solved[0]
    for k in range(1, count):
        scale = scale + sign[k] * solved[k]
    scale = 1.0 / scale
    leftover = [s * scale for s in solved]
    coefficients = [(1.0 - leftover[0]) * (1.0 / SHIFT)]
    for k in range(1, STEPS):
        coefficients.append(leftover[k] * (-1.0 / SHIFT) - coefficients[-1])
    return coefficients, leftover


def combine(plan, chunk, parts, v_ext, rim_0, *refs):
    basis, rims = refs[:STEPS], refs[STEPS : 2 * STEPS]
    solution_field, residual, weights = refs[2 * STEPS :]

    @pl.when(pl.program_id(0) == 0)
    def _():
        coefficients, leftover = weigh(parts[...])
        for k, value in enumerate(coefficients + leftover):
            weights[k] = value

    own = plan.own() + pl.program_id(0) * chunk
    lane = lanes()

    def mix(refs, p, at):
        fields = [ref[p, at, :] for ref in refs]
        one, two = weights[0] * fields[0], weights[STEPS] * fields[0]
        for k in range(1, STEPS):
            one = one + weights[k] * fields[k]
            two = two + weights[STEPS + k] * fields[k]
        return one, two + weights[2 * STEPS] * fields[STEPS]

    for p in range(chunk):
        plane = own + p
        band = plane // plan.rim
        depth = plane - band * plan.rim
        low = 100 - BAND * band
        low = jnp.where(low < 0, low + 128, low)
        high = 116 - BAND * band
        for r in range(plan.ny // 8):
            at = pl.ds(TOP + 8 * r, 8)
            mains = mix((v_ext,) + tuple(basis), 1 + plane, at)
            edges = mix((rim_0,) + tuple(rims), 1 + depth, at)
            for out, main, edge in zip((solution_field, residual), mains, edges):
                value = jnp.where(lane < STEPS, pltpu.roll(edge, low, 1), main)
                value = jnp.where(lane >= 128 - STEPS, pltpu.roll(edge, high, 1), value)
                out[p, pl.ds(8 * r, 8), :] = value


def swaps(first, second, axis):
    count = lax.axis_size(axis)
    ones = [(i, i + 1) for i in range(0, count - 1, 2)]
    twos = [(i, i + 1) for i in range(1, count - 1, 2)]
    return tuple(
        lax.ppermute(value, axis, pairs + [(b, a) for a, b in pairs])
        for value, pairs in ((first, ones), (second, twos))
    )


def on_device(mesh, right_side, inv_density, active):
    nx, ny, nz = right_side.shape
    plan = Plan(mesh, nx, ny, nz)
    field = kept((nx, ny, nz))
    face = kept((2, STEPS, ny, nz))
    v, w, *faces = call(
        functools.partial(prepare, plan), [field, field] + [face] * plan.sides, "prepare"
    )(right_side, inv_density, active)
    if plan.sides == 1:
        halos = [lax.ppermute(faces[0], "gx", [(0, 1), (1, 0)])]
    else:
        steps = [(i, i + 1) for i in range(plan.gx - 1)]
        pairs = [steps, [(b, a) for a, b in steps]]
        halos = [lax.ppermute(f, "gx", p) for f, p in zip(faces, pairs)]
    v, w, *halos = [resident(a) for a in [v, w] + halos]
    strip = kept((2, plan.planes * STEPS, 128))
    first, second = call(functools.partial(pack_rows, plan), [strip, strip], "rows")(v, w, *halos)
    first, second = swaps(first, second, "gy")
    table = kept((plan.planes + 2, plan.tall, 128))
    column = kept((2, plan.deep, plan.half, 128))
    v_ext, w_ext, first, second = call(
        functools.partial(pack_lanes, plan),
        [table, table, column, column],
        "columns",
        scratch=[kept((plan.deep, plan.rows, 128))],
    )(v, w, *halos, resident(first), resident(second))
    first, second = swaps(first, second, "gz")
    v_ext, w_ext = resident(v_ext), resident(w_ext)
    devices = plan.gx * plan.gy * plan.gz
    rim = kept((plan.rim + 2, plan.tall, 128))
    sums = kept((2 * STEPS + 1, 8, 128))
    *basis, sums, rim_v, rim_w = call(
        functools.partial(inner, plan),
        [table] * STEPS + [sums, rim, rim],
        "inner",
        scratch=[table] * 4,
        flops=1 << 24,
    )(v_ext, w_ext)
    *rims, moments, rim_0 = call(
        functools.partial(outer, plan),
        [rim] * STEPS + [kept((devices, 1, 128)), rim],
        "outer",
        scratch=[rim] * 5,
    )(*[resident(a) for a in (first, second, rim_v, rim_w, sums)])
    parts = lax.all_to_all(moments, AXES, 0, 0, tiled=True)
    chunk = 4
    block = pl.BlockSpec((chunk, ny, nz), lambda i: (i, 0, 0))
    shape = jax.ShapeDtypeStruct((nx, ny, nz), jnp.float32)
    operands = [parts, v_ext, rim_0] + basis + rims
    out, residual = pl.pallas_call(
        functools.partial(combine, plan, chunk),
        out_shape=[shape, shape],
        grid=(nx // chunk,),
        in_specs=[vmem_spec()] * len(operands),
        out_specs=[block, block],
        scratch_shapes=[kept((2 * STEPS + 1, 8, 128))],
        compiler_params=pltpu.CompilerParams(vmem_limit_bytes=40 << 20),
        name="combine",
    )(*[resident(a) for a in operands])
    return out, residual


def solution(mesh):
    placed = P("gx", "gy", "gz")
    return jax.shard_map(
        functools.partial(on_device, mesh),
        mesh=mesh,
        in_specs=(placed,) * 3,
        out_specs=(placed, placed),
        check_vma=False,
    )
```

time: 74.5 us -> 52.8 us (0.71)
  Pallas kernels: 38.2 us -> 20.8 us
  waiting for transfers between devices: 7.05 us -> 4.67 us
  blocking collectives: 18.5 us -> 16.6 us
    pallas_call x2 -> x3, Pallas kernels: 36 us -> 17.8 us  [the longest x1 11 us: on_device(): call(functools.partial(inner, plan), [table] * STEPS + [sums, rim, rim],...]
    ppermute x4, waiting for transfers between devices: 5.7 us -> 3.32 us  [swaps(): lax.ppermute(value, axis, pairs + [(b, a) for a, b in pairs])]
    all_to_all x1, blocking collectives: 18.5 us -> 16.6 us  [on_device(): parts = lax.all_to_all(moments, AXES, 0, 0, tiled=True)]
  transfers between devices with their start and end apart: 5 -> 5, of which waited for: 3 -> 2; matrix products, arithmetic and copies ran while one was open for 0% -> 0% of each run, Pallas kernels for 0% -> 21%
where the time goes in v2:
time: 52.8 us; the launch traced here: 52.5 us
  Pallas kernels  20.8 us (39%)
  blocking collectives  16.6 us (31%)
  starting transfers between devices  6.65 us (13%)
  waiting for transfers between devices  4.67 us (9%)
  local copies, waits for them, and re-layouts  3.12 us (6%)
  between operations  0.71 us (1%)
    all_to_all x1, blocking collectives, on_device(): parts = lax.all_to_all(moments, AXES, 0, 0, tiled=True)  16.6 us
    pallas_call x1, Pallas kernels, on_device(): call(functools.partial(inner, plan), [table] * STEPS + [sums, rim, rim],...  11 us
    ppermute x4, starting transfers between devices, swaps(): lax.ppermute(value, axis, pairs + [(b, a) for a, b in pairs])  6.13 us
    pallas_call x1, Pallas kernels, on_device(): call(functools.partial(outer, plan), [rim] * STEPS + [kept((devices, 1, 1...  5.68 us
    ppermute x4, waiting for transfers between devices, swaps(): lax.ppermute(value, axis, pairs + [(b, a) for a, b in pairs])  3.32 us
    unnamed x6, local copies, waits for them, and re-layouts  3.12 us
    pallas_call x1, Pallas kernels, on_device(): pl.pallas_call(functools.partial(combine, plan, chunk), out_shape=[shape,...  2.77 us
    ppermute x1, waiting for transfers between devices, on_device(): halos = [lax.ppermute(faces[0], 'gx', [(0, 1), (1, 0)])]  1.35 us
  transfers between devices with their start and end apart: 5, of which 2 were waited for; matrix products, arithmetic and copies ran while one was open for 0% of the time, Pallas kernels for 21%

profile of v2, /device:TPU:0, one launch (start us, length us, event | category | flops | bytes accessed | tf_op | source)
XLA Modules:
  0.0 52.5 jit_solution(1991441176003407719)
XLA Ops:
  0.6 0.0 copy-start
  0.6 1.0 %copy-done = f32[16,64,128]{2,1,0:T(8,128)S(1)} copy-done((f32[16,64,128]{2,1,0:T(8,128)S(1)}, f32[16,64,128]{2,1,0:T(8,128)}, u32[]{:S(2)}) %copy-start) | copy-done | bytes 524312
  1.7 0.0 copy-start.1
  1.7 1.0 %copy-done.1 = f32[16,64,128]{2,1,0:T(8,128)S(1)} copy-done((f32[16,64,128]{2,1,0:T(8,128)S(1)}, f32[16,64,128]{2,1,0:T(8,128)}, u32[]{:S(2)}) %copy-start.1) | copy-done | bytes 524312
  2.7 0.0 copy-start.2
  2.7 1.0 %copy-done.2 = s32[16,64,128]{2,1,0:T(8,128)S(1)} copy-done((s32[16,64,128]{2,1,0:T(8,128)S(1)}, s32[16,64,128]{2,1,0:T(8,128)}, u32[]{:S(2)}) %copy-start.2) | copy-done | bytes 524312
  3.8 0.1 prepare.1
  3.9 0.5 collective-permute-start
  4.4 1.3 %collective-permute-done.refs_0_ = f32[2,6,64,128]{3,2,1,0:T(8,128)S(1)} collective-permute-done((f32[2,6,64,128]{3,2,1,0:T(8,128)S(1)}, f32[2,6,64,128]{3,2,1,0:T(8,128)S(1)}, u32[]{:S(2)}, u32[]{:S(2)}) %collective-permute-start) | collective-permute-done | bytes 393248 | tf_op jit(solution)/shard_map/ppermute | solution.py:446
  5.8 2.9 %collective-permute-start.1 = (f32[2,132,128]{2,1,0:T(8,128)S(1)}, f32[2,132,128]{2,1,0:T(8,128)S(1)}, u32[]{:S(2)}, u32[]{:S(2)}) collective-permute-start(f32[2,132,128]{2,1,0:T(8,128)S(1)} %get-tuple-element.31), channel_id=1, source_target_pairs={{0,4},{8,12},{4,0},{12,8},{1,5},{9,13},{5,1},{13,9},{2,6},{10,14},... | collective-permute-start | bytes 405512 | tf_op jit(solution)/shard_map/ppermute | solution.py:432
  8.7 0.7 %collective-permute-start.2 = (f32[2,132,128]{2,1,0:T(8,128)S(1)}, f32[2,132,128]{2,1,0:T(8,128)S(1)}, u32[]{:S(2)}, u32[]{:S(2)}) collective-permute-start(f32[2,132,128]{2,1,0:T(8,128)S(1)} %get-tuple-element.32), channel_id=1, source_target_pairs={{4,8},{8,4},{5,9},{9,5},{6,10},{10,6},{7,11},{11,7},{20,24},{24,20... | collective-permute-start | bytes 405512 | tf_op jit(solution)/shard_map/ppermute | solution.py:432
  9.4 3.3 %collective-permute-done.1.refs_1_ = f32[2,132,128]{2,1,0:T(8,128)S(1)} collective-permute-done((f32[2,132,128]{2,1,0:T(8,128)S(1)}, f32[2,132,128]{2,1,0:T(8,128)S(1)}, u32[]{:S(2)}, u32[]{:S(2)}) %collective-permute-start.1) | collective-permute-done | bytes 135200 | tf_op jit(solution)/shard_map/ppermute | solution.py:432
  12.7 0.0 collective-permute-done.2.refs_2_
  12.7 1.1 %columns.1 = (f32[24,96,128]{2,1,0:T(8,128)S(1)}, f32[24,96,128]{2,1,0:T(8,128)S(1)}, f32[2,3,40,128]{3,2,1,0:T(8,128)S(1)}, f32[2,3,40,128]{3,2,1,0:T(8,128)S(1)}) custom-call(f32[16,64,128]{2,1,0:T(8,128)S(1)} %get-tuple-element.28.v, f32[16,64,128]{2,1,0:T(8,128)S(1)} %get-tuple-element.29.w, f32[2,6,64,128]{3,2,1,0:T(8,128)S(1)} %collective-permute-done.refs_0_, ...), custom_call_target="tpu_custom_call" | custom-call | bytes 1048576 | tf_op jit(solution)/shard_map/columns/pallas_call | solution.py:457
  13.9 1.9 %collective-permute-start.3 = (f32[2,3,40,128]{3,2,1,0:T(8,128)S(1)}, f32[2,3,40,128]{3,2,1,0:T(8,128)S(1)}, u32[]{:S(2)}, u32[]{:S(2)}) collective-permute-start(f32[2,3,40,128]{3,2,1,0:T(8,128)S(1)} %get-tuple-element.33), channel_id=1, source_target_pairs={{0,1},{2,3},{1,0},{3,2},{4,5},{6,7},{5,4},{7,6},{8,9},{10,11},{9,8... | collective-permute-start | bytes 368648 | tf_op jit(solution)/shard_map/ppermute | solution.py:432
  15.7 0.7 %collective-permute-start.4 = (f32[2,3,40,128]{3,2,1,0:T(8,128)S(1)}, f32[2,3,40,128]{3,2,1,0:T(8,128)S(1)}, u32[]{:S(2)}, u32[]{:S(2)}) collective-permute-start(f32[2,3,40,128]{3,2,1,0:T(8,128)S(1)} %get-tuple-element.34), channel_id=1, source_target_pairs={{1,2},{2,1},{5,6},{6,5},{9,10},{10,9},{13,14},{14,13},{17,18},{18,... | collective-permute-start | bytes 368648 | tf_op jit(solution)/shard_map/ppermute | solution.py:432
  16.4 11.0 %inner.1 = (f32[24,96,128]{2,1,0:T(8,128)S(1)}, f32[24,96,128]{2,1,0:T(8,128)S(1)}, f32[24,96,128]{2,1,0:T(8,128)S(1)}, f32[24,96,128]{2,1,0:T(8,128)S(1)}, f32[...) custom-call(f32[24,96,128]{2,1,0:T(8,128)S(1)} %get-tuple-element.35, ...), custom_call_target="tpu_custom_call" | custom-call | flops 16777216 | bytes 1048576 | tf_op jit(solution)/shard_map/inner/pallas_call | solution.py:468
  27.4 0.0 collective-permute-done.3.first
  27.4 0.0 collective-permute-done.4.second
  27.5 5.7 %outer.1 = (f32[10,96,128]{2,1,0:T(8,128)S(1)}, f32[10,96,128]{2,1,0:T(8,128)S(1)}, f32[10,96,128]{2,1,0:T(8,128)S(1)}, f32[10,96,128]{2,1,0:T(8,128)S(1)}, f32[...) custom-call(f32[2,3,40,128]{3,2,1,0:T(8,128)S(1)} %collective-permut, ...), custom_call_target="tpu_custom_call" | custom-call | bytes 1048576 | tf_op jit(solution)/shard_map/outer/pallas_call | solution.py:475
  33.1 16.6 %all_to_all.5.parts = f32[32,1,128]{2,1,0:T(1,128)S(1)} all-to-all(f32[32,1,128]{2,1,0:T(1,128)S(1)} %get-tuple-element.40), channel_id=1, replica_groups=mesh['gx'=2,'gy'=4,'gz'=4] {'gx','gy','gz'}, dimensions={0} | all-to-all | bytes 32768 | tf_op jit(solution)/shard_map/all_to_all | solution.py:481
  49.8 2.8 %combine.1 = (f32[16,64,128]{2,1,0:T(8,128)}, f32[16,64,128]{2,1,0:T(8,128)}) custom-call(f32[32,1,128]{2,1,0:T(1,128)S(1)} %all_to_all.5.parts, f32[24,96,128]{2,1,0:T(8,128)S(1)} %get-tuple-element.35.v_ext, f32[10,96,128]{2,1,0:T(8,128)S(1)} %get-tuple-element.41.rim_0, f32[24,96,128]{2,1,0:T(8,128)S(1)} %get-tuple-element.42.refs_0_, ...), custom_call_target="tpu_custom_call" | custom-call | tf_op jit(solution)/shard_map/combine/pallas_call | solution.py:486
  (1 shorter events, 0.0 us)
Async XLA Ops:
  0.6 1.0 %copy-start = (f32[16,64,128]{2,1,0:T(8,128)S(1)}, f32[16,64,128]{2,1,0:T(8,128)}, u32[]{:S(2)}) copy-start(f32[16,64,128]{2,1,0:T(8,128)} %rs.1) | copy-start | bytes 1572868
  1.7 1.0 %copy-start.1 = (f32[16,64,128]{2,1,0:T(8,128)S(1)}, f32[16,64,128]{2,1,0:T(8,128)}, u32[]{:S(2)}) copy-start(f32[16,64,128]{2,1,0:T(8,128)} %inv.1) | copy-start | bytes 1572868
  2.7 1.0 %copy-start.2 = (s32[16,64,128]{2,1,0:T(8,128)S(1)}, s32[16,64,128]{2,1,0:T(8,128)}, u32[]{:S(2)}) copy-start(s32[16,64,128]{2,1,0:T(8,128)} %act.1) | copy-start | bytes 1572868
  3.9 1.9 %collective-permute-start = (f32[2,6,64,128]{3,2,1,0:T(8,128)S(1)}, f32[2,6,64,128]{3,2,1,0:T(8,128)S(1)}, u32[]{:S(2)}, u32[]{:S(2)}) collective-permute-start(f32[2,6,64,128]{3,2,1,0:T(8,128)S(1)} %get-tuple-element.30), channel_id=1, source_target_pairs={{0,16},{16,0},{1,17},{17,1},{2,18},{18,2},{3,19},{19,3},{4,20},{20... | collective-permute-start | bytes 1179656 | tf_op jit(solution)/shard_map/ppermute | solution.py:446
  5.8 6.9 %collective-permute-start.1 = (f32[2,132,128]{2,1,0:T(8,128)S(1)}, f32[2,132,128]{2,1,0:T(8,128)S(1)}, u32[]{:S(2)}, u32[]{:S(2)}) collective-permute-start(f32[2,132,128]{2,1,0:T(8,128)S(1)} %get-tuple-element.31), channel_id=1, source_target_pairs={{0,4},{8,12},{4,0},{12,8},{1,5},{9,13},{5,1},{13,9},{2,6},{10,14},... | collective-permute-start | bytes 405512 | tf_op jit(solution)/shard_map/ppermute | solution.py:432
  8.7 4.0 %collective-permute-start.2 = (f32[2,132,128]{2,1,0:T(8,128)S(1)}, f32[2,132,128]{2,1,0:T(8,128)S(1)}, u32[]{:S(2)}, u32[]{:S(2)}) collective-permute-start(f32[2,132,128]{2,1,0:T(8,128)S(1)} %get-tuple-element.32), channel_id=1, source_target_pairs={{4,8},{8,4},{5,9},{9,5},{6,10},{10,6},{7,11},{11,7},{20,24},{24,20... | collective-permute-start | bytes 405512 | tf_op jit(solution)/shard_map/ppermute | solution.py:432
  13.9 13.6 %collective-permute-start.3 = (f32[2,3,40,128]{3,2,1,0:T(8,128)S(1)}, f32[2,3,40,128]{3,2,1,0:T(8,128)S(1)}, u32[]{:S(2)}, u32[]{:S(2)}) collective-permute-start(f32[2,3,40,128]{3,2,1,0:T(8,128)S(1)} %get-tuple-element.33), channel_id=1, source_target_pairs={{0,1},{2,3},{1,0},{3,2},{4,5},{6,7},{5,4},{7,6},{8,9},{10,11},{9,8... | collective-permute-start | bytes 368648 | tf_op jit(solution)/shard_map/ppermute | solution.py:432
  15.7 11.7 %collective-permute-start.4 = (f32[2,3,40,128]{3,2,1,0:T(8,128)S(1)}, f32[2,3,40,128]{3,2,1,0:T(8,128)S(1)}, u32[]{:S(2)}, u32[]{:S(2)}) collective-permute-start(f32[2,3,40,128]{3,2,1,0:T(8,128)S(1)} %get-tuple-element.34), channel_id=1, source_target_pairs={{1,2},{2,1},{5,6},{6,5},{9,10},{10,9},{13,14},{14,13},{17,18},{18,... | collective-permute-start | bytes 368648 | tf_op jit(solution)/shard_map/ppermute | solution.py:432

commit v3 on v2

--- a/solution.py
+++ b/solution.py
@@ -13,7 +13,7 @@
 WIDE = 16
 RIMS = 3
 BAND = 40
-UNROLL = 3
+QUAD = 4
 TOP = 8
 VMEM = pltpu.VMEM
 AXES = ("gx", "gy", "gz")
@@ -27,14 +27,14 @@
     return pltpu.with_memory_space_constraint(array, VMEM)
 
 
-def call(body, outs, name, scratch=(), grid=None, out_specs=None, limit=40, flops=0):
+def call(body, outs, name, scratch=(), aliases=None, flops=0):
     return pl.pallas_call(
         body,
         out_shape=outs,
-        grid=grid or (),
-        out_specs=out_specs if out_specs is not None else [vmem_spec() for _ in outs],
+        out_specs=[vmem_spec() for _ in outs],
         scratch_shapes=list(scratch),
-        compiler_params=pltpu.CompilerParams(vmem_limit_bytes=limit << 20),
+        input_output_aliases=aliases or {},
+        compiler_params=pltpu.CompilerParams(vmem_limit_bytes=40 << 20),
         cost_estimate=pl.CostEstimate(flops=flops, bytes_accessed=1 << 20, transcendentals=0),
         name=name,
     )
@@ -70,6 +70,22 @@
             return [(1 - lax.axis_index("gx")) * self.nx]
         return [0, STEPS + self.nx] if self.sides == 2 else []
 
+    def strips(self):
+        parts = [(None, i, STEPS) for i in range(self.nx)]
+        for side in range(self.sides):
+            for distance in range(1, STEPS):
+                toward, away = STEPS - distance, distance - 1
+                if self.sides == 1:
+                    index = lax.axis_index("gx")
+                    plane = index * toward + (1 - index) * away
+                else:
+                    plane = away if side else toward
+                parts.append((side, plane, STEPS - distance))
+        return parts
+
+    def strip_rows(self):
+        return self.nx * STEPS + self.sides * STEPS * (STEPS - 1) // 2
+
     def span(self, level):
         if self.sides == 1:
             index = lax.axis_index("gx")
@@ -78,71 +94,106 @@
         return cut, self.planes - 2 * cut
 
 
-def prepare(plan, rs, inv, act, v, w, *faces):
+def prepare(plan, rs, inv, act, v_ext, w_ext, *faces):
+    own, ny = 1 + plan.own(), plan.ny
+    for ext in (v_ext, w_ext):
+        ext[...] = jnp.zeros(ext.shape, jnp.float32)
     for i in range(plan.nx):
         liquid = act[i].astype(jnp.float32)
-        v[i] = rs[i] * liquid
-        w[i] = inv[i] * liquid * (2.0 / SHIFT)
+        v_ext[own + i, pl.ds(TOP, ny), :] = rs[i] * liquid
+        w_ext[own + i, pl.ds(TOP, ny), :] = inv[i] * liquid * (2.0 / SHIFT)
     if plan.sides == 1:
         starts = [(1 - lax.axis_index("gx")) * (plan.nx - STEPS)]
     else:
         starts = [plan.nx - STEPS, 0]
     for start, face in zip(starts, faces):
         for i in range(STEPS):
-            face[0, i] = v[start + i]
-            face[1, i] = w[start + i]
-
-
-def pack_rows(plan, v, w, *refs):
-    halos, (first, second) = refs[: plan.sides], refs[plan.sides :]
+            face[0, i] = v_ext[own + start + i, pl.ds(TOP, ny), :]
+            face[1, i] = w_ext[own + start + i, pl.ds(TOP, ny), :]
+
+
+def pack_rows(plan, *refs):
+    halos, (v_ext, w_ext, first, second) = refs[2 : 2 + plan.sides], refs[2 + plan.sides :]
+    ny = plan.ny
     even = lax.axis_index("gy") % 2 == 0
-    for field, own in enumerate((v, w)):
-        sources = [(own, (i,)) for i in range(plan.nx)]
-        sources += [(halo, (field, i)) for halo in halos for i in range(STEPS)]
-        for p, (ref, at) in enumerate(sources):
-            low = ref[at + (pl.ds(0, STEPS), slice(None))]
-            high = ref[at + (pl.ds(plan.ny - STEPS, STEPS), slice(None))]
-            first[field, pl.ds(p * STEPS, STEPS), :] = jnp.where(even, high, low)
-            second[field, pl.ds(p * STEPS, STEPS), :] = jnp.where(even, low, high)
-
-
-def pack_lanes(plan, v, w, *refs):
-    halos, refs = refs[: plan.sides], refs[plan.sides :]
-    from_first, from_second, v_ext, w_ext, first, second, packed = refs
+    starts = plan.halo_starts()
+    for field, ext in enumerate((v_ext, w_ext)):
+        for start, halo in zip(starts, halos):
+            for i in range(STEPS):
+                ext[1 + start + i, pl.ds(TOP, ny), :] = halo[field, i]
+        offset = 0
+        for side, plane, rows in plan.strips():
+            at = 1 + plane + (plan.own() if side is None else starts[side])
+            low = ext[at, pl.ds(TOP, rows), :]
+            high = ext[at, pl.ds(TOP + ny - rows, rows), :]
+            first[field, pl.ds(offset, rows), :] = jnp.where(even, high, low)
+            second[field, pl.ds(offset, rows), :] = jnp.where(even, low, high)
+            offset += rows
+
+
+def column_block(plan, ext, i, r, group):
+    block = jnp.zeros((8, 128), jnp.float32)
+    for g in range(GROUPS):
+        p = g * plan.deep + i
+        if p < plan.planes:
+            moved = pltpu.roll(ext[1 + p, pl.ds(8 * r, 8), :], WIDE * g + 8, 1)
+            block = jnp.where(group == g, moved, block)
+    return block
+
+
+def rim_block(plan, ext, i, at, band, spot):
+    block = jnp.zeros((8, 128), jnp.float32)
+    for g in range(RIMS):
+        p = g * plan.rim + i
+        if p < plan.planes:
+            value = ext[1 + p, at, :]
+            high = pltpu.roll(value, BAND * g + 12, 1)
+            low = pltpu.roll(value, (BAND * g + 28) % 128, 1)
+            block = jnp.where((band == g) & (spot < 12), high, block)
+            block = jnp.where((band == g) & (spot >= 28), low, block)
+    return block
+
+
+def near(plan, v_ext, w_ext, packed, rim_v, rim_w, *tables):
+    inside = range(1, 1 + plan.ny // 8)
+    face_tables(w_ext, tables, plan.planes, plan.planes // 2, inside, inside, inside[1:-1])
+    group = lanes() // WIDE
+    band, spot = lanes() // BAND, lanes() % BAND
+    for field, (ext, rim) in enumerate(((v_ext, rim_v), (w_ext, rim_w))):
+        for r in inside:
+            at = pl.ds(8 * r, 8)
+            for i in range(plan.deep):
+                packed[field, i, at, :] = column_block(plan, ext, i, r, group)
+            for i in range(plan.rim):
+                rim[1 + i, at, :] = rim_block(plan, ext, i, at, band, spot)
+
+
+def pack_lanes(plan, *refs):
+    from_first, from_second, packed, v_ext, w_ext, first, second = refs[2:]
     ny = plan.ny
     even_y = lax.axis_index("gy") % 2 == 0
-    even_z = lax.axis_index("gz") % 2 == 0
-    blank = jnp.zeros((plan.tall, 128), jnp.float32)
+    even_z = lax.axis_index("gz") % 2 == 1
     lane = lanes()
     group = lane // WIDE
     right_half = (lane % WIDE) >= WIDE // 2
-    for field, (own, ext) in enumerate(((v, v_ext), (w, w_ext))):
-        ext[0] = blank
-        for p in range(plan.planes + 1, ext.shape[0]):
-            ext[p] = blank
-        sources = [(own, (i,), 1 + plan.own() + i) for i in range(plan.nx)]
-        for halo, start in zip(halos, plan.halo_starts()):
-            sources += [(halo, (field, i), 1 + start + i) for i in range(STEPS)]
-        for p, (ref, at, where) in enumerate(sources):
-            one = from_first[field, pl.ds(p * STEPS, STEPS), :]
-            two = from_second[field, pl.ds(p * STEPS, STEPS), :]
-            ext[where, pl.ds(0, 8), :] = jnp.zeros((8, 128), jnp.float32)
-            ext[where, pl.ds(TOP + ny, 24), :] = jnp.zeros((24, 128), jnp.float32)
-            ext[where, pl.ds(TOP, ny), :] = ref[at]
-            ext[where, pl.ds(TOP - STEPS, STEPS), :] = jnp.where(even_y, two, one)
-            ext[where, pl.ds(TOP + ny, STEPS), :] = jnp.where(even_y, one, two)
+    starts = plan.halo_starts()
+    last = plan.rows // 8 - 1
+    for field, ext in enumerate((v_ext, w_ext)):
+        offset = 0
+        for side, plane, rows in plan.strips():
+            at = 1 + plane + (plan.own() if side is None else starts[side])
+            one = from_first[field, pl.ds(offset, rows), :]
+            two = from_second[field, pl.ds(offset, rows), :]
+            ext[at, pl.ds(TOP - rows, rows), :] = jnp.where(even_y, two, one)
+            ext[at, pl.ds(TOP + ny, rows), :] = jnp.where(even_y, one, two)
+            offset += rows
+    for field, ext in enumerate((v_ext, w_ext)):
         for i in range(plan.deep):
-            for r in range(plan.rows // 8):
-                block = jnp.zeros((8, 128), jnp.float32)
-                for g in range(GROUPS):
-                    p = g * plan.deep + i
-                    if p < plan.planes:
-                        moved = pltpu.roll(ext[1 + p, pl.ds(8 * r, 8), :], WIDE * g + 8, 1)
-                        block = jnp.where(group == g, moved, block)
-                packed[i, pl.ds(8 * r, 8), :] = block
+            blocks = [packed[field, i, pl.ds(8 * r, 8), :] for r in range(1, last)]
+            blocks = [column_block(plan, ext, i, 0, group)] + blocks
+            blocks = blocks + [column_block(plan, ext, i, last, group)]
             for r in range(plan.half // 8):
-                upper = packed[i, pl.ds(8 * r, 8), :]
-                lower = packed[i, pl.ds(plan.half + 8 * r, 8), :]
+                upper, lower = blocks[r], blocks[plan.half // 8 + r]
                 to_right = jnp.where(right_half, pltpu.roll(lower, 8, 1), upper)
                 to_left = jnp.where(right_half, lower, pltpu.roll(upper, 120, 1))
                 first[field, i, pl.ds(8 * r, 8), :] = jnp.where(even_z, to_right, to_left)
@@ -156,24 +207,33 @@
     return (one * two) * inverse
 
 
-def face_tables(weight, tables, planes, blocks):
+def face_tables(weight, tables, planes, unroll, across, along, diagonals):
     cx, cy, cz, dg = tables
 
-    def faces(p, _):
-        for r in range(blocks):
-            at = pl.ds(8 * r, 8)
-            here = weight[p, at, :]
-            cx[p, at, :] = coupling(here, weight[p + 1, at, :])
-            cy[p, pl.ds(8 * r + 8, 8), :] = coupling(here, weight[p, pl.ds(8 * r + 1, 8), :])
-            cz[p, at, :] = coupling(here, pltpu.roll(here, 127, 1))
+    for r in across:
+        at = pl.ds(8 * r, 8)
+        cx[0, at, :] = coupling(weight[0, at, :], weight[1, at, :])
+
+    def faces(trip, _):
+        for u in range(unroll):
+            p = 1 + unroll * trip + u
+            for r in sorted({*across, *along}):
+                at = pl.ds(8 * r, 8)
+                here = weight[p, at, :]
+                if r in across:
+                    cx[p, at, :] = coupling(here, weight[p + 1, at, :])
+                    cz[p, at, :] = coupling(here, pltpu.roll(here, 127, 1))
+                if r in along:
+                    below = weight[p, pl.ds(8 * r + 1, 8), :]
+                    cy[p, pl.ds(8 * r + 8, 8), :] = coupling(here, below)
         return 0
 
-    lax.fori_loop(0, planes + 1, faces, 0)
+    lax.fori_loop(0, planes // unroll, faces, 0)
 
     def diagonal(trip, _):
-        for u in range(2):
-            p = 1 + 2 * trip + u
-            for r in range(blocks):
+        for u in range(unroll):
+            p = 1 + unroll * trip + u
+            for r in diagonals:
                 at = pl.ds(8 * r, 8)
                 air = 0.5 * weight[p, at, :]
                 total = jnp.full((8, 128), -1.0, jnp.float32)
@@ -190,7 +250,7 @@
                 dg[p, at, :] = total
         return 0
 
-    lax.fori_loop(0, (planes + 1) // 2, diagonal, 0)
+    lax.fori_loop(0, planes // unroll, diagonal, 0)
 
 
 def advance(source, target, tables, first, trips, unroll, start, blocks):
@@ -198,12 +258,13 @@
 
     def body(trip, _):
         base = first + trip * unroll
-        for r in range(blocks):
+        for u0, r in [(u0, r) for u0 in range(0, unroll, QUAD) for r in range(blocks)]:
             s = start + 8 * r
             at = pl.ds(s, 8)
-            fields = [source[base + u, at, :] for u in range(unroll + 2)]
-            walls = [cx[base + u, at, :] for u in range(unroll + 1)]
-            for u in range(unroll):
+            top = min(u0 + QUAD, unroll)
+            fields = {u: source[base + u, at, :] for u in range(u0, top + 2)}
+            walls = {u: cx[base + u, at, :] for u in range(u0, top + 1)}
+            for u in range(u0, top):
                 p = base + u + 1
                 here, ahead = fields[u + 1], cz[p, at, :]
                 after = pltpu.roll(here, 127, 1)
@@ -230,21 +291,25 @@
     return sums
 
 
-def inner(plan, v_ext, w_ext, *refs):
-    basis, (sums_ref, rim_v, rim_w), tables = refs[:STEPS], refs[STEPS : STEPS + 3], refs[STEPS + 3 :]
+def inner(plan, *refs):
+    v_ext, w_ext = refs[:2]
+    basis, (sums_ref, rim_v, rim_w), tables = refs[8 : 8 + STEPS], refs[8 + STEPS : -4], refs[-4:]
     planes = plan.planes
     blank8 = jnp.zeros((8, 128), jnp.float32)
-    face_tables(w_ext, tables, planes, plan.rows // 8)
+    last = plan.rows // 8 - 1
+    halo = (0, last)
+    face_tables(w_ext, tables, planes, planes // 2, halo, (0, last - 1, last), (0, 1, last - 1, last))
     for ref in basis:
         ref[0] = jnp.zeros(ref.shape[1:], jnp.float32)
         ref[planes + 1] = jnp.zeros(ref.shape[1:], jnp.float32)
     source = v_ext
     for level in range(1, STEPS + 1):
         low, count = plan.span(level)
-        trips = -(-count // UNROLL)
-        low = jnp.minimum(low, planes - UNROLL * trips)
+        trips = 2
+        unroll = -(-count // trips)
+        low = jnp.minimum(low, planes - unroll * trips)
         start, blocks = level_rows(plan, level)
-        advance(source, basis[level - 1], tables, low, trips, UNROLL, start, blocks)
+        advance(source, basis[level - 1], tables, low, trips, unroll, start, blocks)
         source = basis[level - 1]
 
     own = 1 + plan.own()
@@ -264,28 +329,16 @@
 
     band, spot = lane // BAND, lane % BAND
     for ext, rim in ((v_ext, rim_v), (w_ext, rim_w)):
-        def fill(r, _):
-            at = pl.ds(pl.multiple_of(8 * r, 8), 8)
+        for r in halo:
+            at = pl.ds(8 * r, 8)
             for i in range(plan.rim):
-                block = blank8
-                for g in range(RIMS):
-                    p = g * plan.rim + i
-                    if p < planes:
-                        value = ext[1 + p, at, :]
-                        high = pltpu.roll(value, BAND * g + 12, 1)
-                        low = pltpu.roll(value, (BAND * g + 28) % 128, 1)
-                        block = jnp.where((band == g) & (spot < 12), high, block)
-                        block = jnp.where((band == g) & (spot >= 28), low, block)
-                rim[1 + i, at, :] = block
-            return 0
-
-        lax.fori_loop(0, plan.rows // 8, fill, 0)
+                rim[1 + i, at, :] = rim_block(plan, ext, i, at, band, spot)
 
 
 def outer(plan, first, second, rim_v, rim_w, sums_ref, *refs):
     basis, (moments, rim_0, rim_s), tables = refs[:STEPS], refs[STEPS : STEPS + 3], refs[STEPS + 3 :]
     planes, deep, half, rim = plan.planes, plan.deep, plan.half, plan.rim
-    even_z = lax.axis_index("gz") % 2 == 0
+    even_z = lax.axis_index("gz") % 2 == 1
     lane = lanes()
     right_half = (lane % WIDE) >= WIDE // 2
     band, spot = lane // BAND, lane % BAND
@@ -323,11 +376,12 @@
             full[i, pl.ds(plan.rows, 16), :] = jnp.zeros((16, 128), jnp.float32)
         wrap(full, 0, plan.rows // 8)
 
-    face_tables(rim_s, tables, rim, plan.rows // 8)
+    every = range(plan.rows // 8)
+    face_tables(rim_s, tables, rim, rim, every, every, every)
     source = rim_0
     for level in range(1, STEPS + 1):
         start, blocks = level_rows(plan, level)
-        advance(source, basis[level - 1], tables, 0, rim // 2, 2, start, blocks)
+        advance(source, basis[level - 1], tables, 0, 1, rim, start, blocks)
         source = basis[level - 1]
         if level < STEPS:
             wrap(source, start, blocks)
@@ -426,8 +480,8 @@
 
 def swaps(first, second, axis):
     count = lax.axis_size(axis)
-    ones = [(i, i + 1) for i in range(0, count - 1, 2)]
-    twos = [(i, i + 1) for i in range(1, count - 1, 2)]
+    starts = (0, 1) if axis == "gy" else (1, 0)
+    ones, twos = ([(i, i + 1) for i in range(s, count - 1, 2)] for s in starts)
     return tuple(
         lax.ppermute(value, axis, pairs + [(b, a) for a, b in pairs])
         for value, pairs in ((first, ones), (second, twos))
@@ -437,41 +491,50 @@
 def on_device(mesh, right_side, inv_density, active):
     nx, ny, nz = right_side.shape
     plan = Plan(mesh, nx, ny, nz)
-    field = kept((nx, ny, nz))
+    table = kept((plan.planes + 2, plan.tall, 128))
     face = kept((2, STEPS, ny, nz))
-    v, w, *faces = call(
-        functools.partial(prepare, plan), [field, field] + [face] * plan.sides, "prepare"
-    )(right_side, inv_density, active)
+    inputs = [
+        pltpu.with_memory_space_constraint(a, pltpu.HBM) for a in (right_side, inv_density, active)
+    ]
+    v_ext, w_ext, *faces = call(
+        functools.partial(prepare, plan), [table, table] + [face] * plan.sides, "prepare"
+    )(*inputs)
     if plan.sides == 1:
         halos = [lax.ppermute(faces[0], "gx", [(0, 1), (1, 0)])]
     else:
         steps = [(i, i + 1) for i in range(plan.gx - 1)]
         pairs = [steps, [(b, a) for a, b in steps]]
         halos = [lax.ppermute(f, "gx", p) for f, p in zip(faces, pairs)]
-    v, w, *halos = [resident(a) for a in [v, w] + halos]
-    strip = kept((2, plan.planes * STEPS, 128))
-    first, second = call(functools.partial(pack_rows, plan), [strip, strip], "rows")(v, w, *halos)
+    strip = kept((2, plan.strip_rows(), 128))
+    v_ext, w_ext, first, second = call(
+        functools.partial(pack_rows, plan), [table, table, strip, strip], "rows", aliases={0: 0, 1: 1}
+    )(*[resident(a) for a in (v_ext, w_ext, *halos)])
     first, second = swaps(first, second, "gy")
-    table = kept((plan.planes + 2, plan.tall, 128))
+    rim = kept((plan.rim + 2, plan.tall, 128))
+    packed, rim_v, rim_w, *tables = call(
+        functools.partial(near, plan),
+        [kept((2, plan.deep, plan.rows, 128)), rim, rim] + [table] * 4,
+        "near",
+        flops=1 << 24,
+    )(resident(v_ext), resident(w_ext))
     column = kept((2, plan.deep, plan.half, 128))
     v_ext, w_ext, first, second = call(
         functools.partial(pack_lanes, plan),
         [table, table, column, column],
         "columns",
-        scratch=[kept((plan.deep, plan.rows, 128))],
-    )(v, w, *halos, resident(first), resident(second))
+        aliases={0: 0, 1: 1},
+    )(*[resident(a) for a in (v_ext, w_ext, first, second, packed)])
     first, second = swaps(first, second, "gz")
     v_ext, w_ext = resident(v_ext), resident(w_ext)
     devices = plan.gx * plan.gy * plan.gz
-    rim = kept((plan.rim + 2, plan.tall, 128))
     sums = kept((2 * STEPS + 1, 8, 128))
     *basis, sums, rim_v, rim_w = call(
         functools.partial(inner, plan),
-        [table] * STEPS + [sums, rim, rim],
+        [table] * STEPS + [sums, rim, rim] + [table] * 4,
         "inner",
-        scratch=[table] * 4,
+        aliases={i: i + STEPS - 1 for i in range(2, 8)},
         flops=1 << 24,
-    )(v_ext, w_ext)
+    )(v_ext, w_ext, *[resident(a) for a in (rim_v, rim_w, *tables)])[: STEPS + 3]
     *rims, moments, rim_0 = call(
         functools.partial(outer, plan),
         [rim] * STEPS + [kept((devices, 1, 128)), rim],

time: 52.8 us -> 41.5 us (0.79)
  Pallas kernels: 20.8 us -> 15.6 us
  local copies, waits for them, and re-layouts: 3.12 us -> 0 us
  blocking collectives: 16.6 us -> 13.6 us
  starting transfers between devices: 6.65 us -> 9.47 us
  waiting for transfers between devices: 4.67 us -> 1.91 us
    unnamed x6 -> x0, local copies, waits for them, and re-layouts: 3.12 us -> none
    all_to_all x1, blocking collectives: 16.6 us -> 13.6 us  [on_device(): parts = lax.all_to_all(moments, AXES, 0, 0, tiled=True)]
    ppermute x4, starting transfers between devices: 6.13 us -> 8.96 us  [swaps(): lax.ppermute(value, axis, pairs + [(b, a) for a, b in pairs])]
    ppermute x4, waiting for transfers between devices: 3.32 us -> 0.57 us  [swaps(): lax.ppermute(value, axis, pairs + [(b, a) for a, b in pairs])]
    pallas_call x1, Pallas kernels: 5.68 us -> 3.3 us  [on_device(): call(functools.partial(outer, plan), [rim] * STEPS + [kept((devices, 1, 1...]
    pallas_call x3 -> x4, Pallas kernels: 11.2 us -> 9.17 us  [the longest x1 5.26 us: on_device(): call(functools.partial(inner, plan), [table] * STEPS + [sums, rim, rim] +...]
    pallas_call x1, Pallas kernels: 1.14 us -> 0.35 us  [on_device(): call(functools.partial(pack_lanes, plan), [table, table, column, column],...]
  transfers between devices with their start and end apart: 5 -> 5, of which waited for: 2 -> 2; matrix products, arithmetic and copies ran while one was open for 0% -> 0% of each run, Pallas kernels for 21% -> 18%
where the time goes in v3:
time: 41.5 us; the launch traced here: 41.3 us
  Pallas kernels  15.6 us (38%)
  blocking collectives  13.6 us (33%)
  starting transfers between devices  9.47 us (23%)
  waiting for transfers between devices  1.91 us (5%)
  between operations  0.7 us (2%)
    all_to_all x1, blocking collectives, on_device(): parts = lax.all_to_all(moments, AXES, 0, 0, tiled=True)  13.6 us
    ppermute x4, starting transfers between devices, swaps(): lax.ppermute(value, axis, pairs + [(b, a) for a, b in pairs])  8.96 us
    pallas_call x1, Pallas kernels, on_device(): call(functools.partial(inner, plan), [table] * STEPS + [sums, rim, rim] +...  5.26 us
    pallas_call x1, Pallas kernels, on_device(): call(functools.partial(outer, plan), [rim] * STEPS + [kept((devices, 1, 1...  3.3 us
    pallas_call x1, Pallas kernels, on_device(): pl.pallas_call(functools.partial(combine, plan, chunk), out_shape=[shape,...  2.8 us
    pallas_call x1, Pallas kernels, on_device(): call(functools.partial(near, plan), [kept((2, plan.deep, plan.rows, 128))...  2.22 us
    pallas_call x1, Pallas kernels, on_device(): call(functools.partial(prepare, plan), [table, table] + [face] * plan.sid...  1.63 us
    ppermute x1, waiting for transfers between devices, on_device(): halos = [lax.ppermute(faces[0], 'gx', [(0, 1), (1, 0)])]  1.35 us
  transfers between devices with their start and end apart: 5, of which 2 were waited for; matrix products, arithmetic and copies ran while one was open for 0% of the time, Pallas kernels for 18%

profile of v3, /device:TPU:0, one launch (start us, length us, event | category | flops | bytes accessed | tf_op | source)
XLA Modules:
  0.0 41.3 jit_solution(8383421818479446197)
XLA Ops:
  0.6 1.6 %prepare.1 = (f32[24,96,128]{2,1,0:T(8,128)S(1)}, f32[24,96,128]{2,1,0:T(8,128)S(1)}, f32[2,6,64,128]{3,2,1,0:T(8,128)S(1)}) custom-call(f32[16,64,128]{2,1,0:T(8,128)} %rs.1, f32[16,64,128]{2,1,0:T(8,128)} %inv.1, s32[16,64,128]{2,1,0:T(8,128)} %act.1), custom_call_target="tpu_custom_call" | custom-call | bytes 1048576 | tf_op jit(solution)/shard_map/prepare/pallas_call | solution.py:499
  2.3 0.5 %collective-permute-start = (f32[2,6,64,128]{3,2,1,0:T(8,128)S(1)}, f32[2,6,64,128]{3,2,1,0:T(8,128)S(1)}, u32[]{:S(2)}, u32[]{:S(2)}) collective-permute-start(f32[2,6,64,128]{3,2,1,0:T(8,128)S(1)} %get-tuple-element.39), channel_id=1, source_target_pairs={{0,16},{16,0},{1,17},{17,1},{2,18},{18,2},{3,19},{19,3},{4,20},{20... | collective-permute-start | bytes 1179656 | tf_op jit(solution)/shard_map/ppermute | solution.py:503
  2.8 1.3 %collective-permute-done.refs_2_ = f32[2,6,64,128]{3,2,1,0:T(8,128)S(1)} collective-permute-done((f32[2,6,64,128]{3,2,1,0:T(8,128)S(1)}, f32[2,6,64,128]{3,2,1,0:T(8,128)S(1)}, u32[]{:S(2)}, u32[]{:S(2)}) %collective-permute-start) | collective-permute-done | bytes 393248 | tf_op jit(solution)/shard_map/ppermute | solution.py:503
  4.1 0.1 rows.1
  4.2 2.9 %collective-permute-start.1 = (f32[2,111,128]{2,1,0:T(8,128)S(1)}, f32[2,111,128]{2,1,0:T(8,128)S(1)}, u32[]{:S(2)}, u32[]{:S(2)}) collective-permute-start(f32[2,111,128]{2,1,0:T(8,128)S(1)} %get-tuple-element.42), channel_id=1, source_target_pairs={{0,4},{8,12},{4,0},{12,8},{1,5},{9,13},{5,1},{13,9},{2,6},{10,14},... | collective-permute-start | bytes 341000 | tf_op jit(solution)/shard_map/ppermute | solution.py:486
  7.1 0.7 %collective-permute-start.2 = (f32[2,111,128]{2,1,0:T(8,128)S(1)}, f32[2,111,128]{2,1,0:T(8,128)S(1)}, u32[]{:S(2)}, u32[]{:S(2)}) collective-permute-start(f32[2,111,128]{2,1,0:T(8,128)S(1)} %get-tuple-element.43), channel_id=1, source_target_pairs={{4,8},{8,4},{5,9},{9,5},{6,10},{10,6},{7,11},{11,7},{20,24},{24,20... | collective-permute-start | bytes 341000 | tf_op jit(solution)/shard_map/ppermute | solution.py:486
  7.8 2.2 %near.1 = (f32[2,3,80,128]{3,2,1,0:T(8,128)S(1)}, f32[10,96,128]{2,1,0:T(8,128)S(1)}, f32[10,96,128]{2,1,0:T(8,128)S(1)}, f32[24,96,128]{2,1,0:T(8,128)S(1)}, f3...) custom-call(f32[24,96,128]{2,1,0:T(8,128)S(1)} %get-tuple-element.40.v_ext.refs_0_, ...), custom_call_target="tpu_custom_call" | custom-call | flops 16777216 | bytes 1048576 | tf_op jit(solution)/shard_map/near/pallas_call | solution.py:514
  10.0 0.6 %collective-permute-done.1.refs_2_ = f32[2,111,128]{2,1,0:T(8,128)S(1)} collective-permute-done((f32[2,111,128]{2,1,0:T(8,128)S(1)}, f32[2,111,128]{2,1,0:T(8,128)S(1)}, u32[]{:S(2)}, u32[]{:S(2)}) %collective-permute-start.1) | collective-permute-done | bytes 113696 | tf_op jit(solution)/shard_map/ppermute | solution.py:486
  10.6 0.0 collective-permute-done.2.refs_3_
  10.6 0.3 columns.1
  10.9 0.7 %collective-permute-start.3 = (f32[2,3,40,128]{3,2,1,0:T(8,128)S(1)}, f32[2,3,40,128]{3,2,1,0:T(8,128)S(1)}, u32[]{:S(2)}, u32[]{:S(2)}) collective-permute-start(f32[2,3,40,128]{3,2,1,0:T(8,128)S(1)} %get-tuple-element.45), channel_id=1, source_target_pairs={{1,2},{2,1},{5,6},{6,5},{9,10},{10,9},{13,14},{14,13},{17,18},{18,... | collective-permute-start | bytes 368648 | tf_op jit(solution)/shard_map/ppermute | solution.py:486
  11.6 4.7 %collective-permute-start.4 = (f32[2,3,40,128]{3,2,1,0:T(8,128)S(1)}, f32[2,3,40,128]{3,2,1,0:T(8,128)S(1)}, u32[]{:S(2)}, u32[]{:S(2)}) collective-permute-start(f32[2,3,40,128]{3,2,1,0:T(8,128)S(1)} %get-tuple-element.46), channel_id=1, source_target_pairs={{0,1},{2,3},{1,0},{3,2},{4,5},{6,7},{5,4},{7,6},{8,9},{10,11},{9,8... | collective-permute-start | bytes 368648 | tf_op jit(solution)/shard_map/ppermute | solution.py:486
  16.3 5.3 %inner.1 = (f32[24,96,128]{2,1,0:T(8,128)S(1)}, f32[24,96,128]{2,1,0:T(8,128)S(1)}, f32[24,96,128]{2,1,0:T(8,128)S(1)}, f32[24,96,128]{2,1,0:T(8,128)S(1)}, f32[...) custom-call(f32[24,96,128]{2,1,0:T(8,128)S(1)} %get-tuple-element.47, ...), custom_call_target="tpu_custom_call", output_to_operand_aliasing={{7}: (2, {}), {8}: (3, {}), {9}: (4, {}), {10}: (5, {}), {1... | custom-call | flops 16777216 | bytes 1048576 | tf_op jit(solution)/shard_map/inner/pallas_call | solution.py:531
  21.6 0.0 collective-permute-done.3.first
  21.6 0.0 collective-permute-done.4.second
  21.6 3.3 %outer.1 = (f32[10,96,128]{2,1,0:T(8,128)S(1)}, f32[10,96,128]{2,1,0:T(8,128)S(1)}, f32[10,96,128]{2,1,0:T(8,128)S(1)}, f32[10,96,128]{2,1,0:T(8,128)S(1)}, f32[...) custom-call(f32[2,3,40,128]{3,2,1,0:T(8,128)S(1)} %collective-permut, ...), custom_call_target="tpu_custom_call" | custom-call | bytes 1048576 | tf_op jit(solution)/shard_map/outer/pallas_call | solution.py:538
  24.9 13.6 %all_to_all.5.parts = f32[32,1,128]{2,1,0:T(1,128)S(1)} all-to-all(f32[32,1,128]{2,1,0:T(1,128)S(1)} %get-tuple-element.58), channel_id=1, replica_groups=mesh['gx'=2,'gy'=4,'gz'=4] {'gx','gy','gz'}, dimensions={0} | all-to-all | bytes 32768 | tf_op jit(solution)/shard_map/all_to_all | solution.py:544
  38.5 2.8 %combine.1 = (f32[16,64,128]{2,1,0:T(8,128)}, f32[16,64,128]{2,1,0:T(8,128)}) custom-call(f32[32,1,128]{2,1,0:T(1,128)S(1)} %all_to_all.5.parts, f32[24,96,128]{2,1,0:T(8,128)S(1)} %get-tuple-element.47.refs_0_.v_ext, f32[10,96,128]{2,1,0:T(8,128)S(1)} %get-tuple-element.59.rim_0, f32[24,96,128]{2,1,0:T(8,128)S(1)} %get-tuple-element.60.refs_0_, ...), custom_call_target="tpu_custom_call" | custom-call | tf_op jit(solution)/shard_map/combine/pallas_call | solution.py:549
Async XLA Ops:
  2.3 1.9 %collective-permute-start = (f32[2,6,64,128]{3,2,1,0:T(8,128)S(1)}, f32[2,6,64,128]{3,2,1,0:T(8,128)S(1)}, u32[]{:S(2)}, u32[]{:S(2)}) collective-permute-start(f32[2,6,64,128]{3,2,1,0:T(8,128)S(1)} %get-tuple-element.39), channel_id=1, source_target_pairs={{0,16},{16,0},{1,17},{17,1},{2,18},{18,2},{3,19},{19,3},{4,20},{20... | collective-permute-start | bytes 1179656 | tf_op jit(solution)/shard_map/ppermute | solution.py:503
  4.2 6.4 %collective-permute-start.1 = (f32[2,111,128]{2,1,0:T(8,128)S(1)}, f32[2,111,128]{2,1,0:T(8,128)S(1)}, u32[]{:S(2)}, u32[]{:S(2)}) collective-permute-start(f32[2,111,128]{2,1,0:T(8,128)S(1)} %get-tuple-element.42), channel_id=1, source_target_pairs={{0,4},{8,12},{4,0},{12,8},{1,5},{9,13},{5,1},{13,9},{2,6},{10,14},... | collective-permute-start | bytes 341000 | tf_op jit(solution)/shard_map/ppermute | solution.py:486
  7.1 3.5 %collective-permute-start.2 = (f32[2,111,128]{2,1,0:T(8,128)S(1)}, f32[2,111,128]{2,1,0:T(8,128)S(1)}, u32[]{:S(2)}, u32[]{:S(2)}) collective-permute-start(f32[2,111,128]{2,1,0:T(8,128)S(1)} %get-tuple-element.43), channel_id=1, source_target_pairs={{4,8},{8,4},{5,9},{9,5},{6,10},{10,6},{7,11},{11,7},{20,24},{24,20... | collective-permute-start | bytes 341000 | tf_op jit(solution)/shard_map/ppermute | solution.py:486
  10.9 10.6 %collective-permute-start.3 = (f32[2,3,40,128]{3,2,1,0:T(8,128)S(1)}, f32[2,3,40,128]{3,2,1,0:T(8,128)S(1)}, u32[]{:S(2)}, u32[]{:S(2)}) collective-permute-start(f32[2,3,40,128]{3,2,1,0:T(8,128)S(1)} %get-tuple-element.45), channel_id=1, source_target_pairs={{1,2},{2,1},{5,6},{6,5},{9,10},{10,9},{13,14},{14,13},{17,18},{18,... | collective-permute-start | bytes 368648 | tf_op jit(solution)/shard_map/ppermute | solution.py:486
  11.6 10.0 %collective-permute-start.4 = (f32[2,3,40,128]{3,2,1,0:T(8,128)S(1)}, f32[2,3,40,128]{3,2,1,0:T(8,128)S(1)}, u32[]{:S(2)}, u32[]{:S(2)}) collective-permute-start(f32[2,3,40,128]{3,2,1,0:T(8,128)S(1)} %get-tuple-element.46), channel_id=1, source_target_pairs={{0,1},{2,3},{1,0},{3,2},{4,5},{6,7},{5,4},{7,6},{8,9},{10,11},{9,8... | collective-permute-start | bytes 368648 | tf_op jit(solution)/shard_map/ppermute | solution.py:486

commit v4 on v3

--- a/solution.py
+++ b/solution.py
@@ -13,6 +13,7 @@
 WIDE = 16
 RIMS = 3
 BAND = 40
+EARLY = 4
 QUAD = 4
 TOP = 8
 VMEM = pltpu.VMEM
@@ -154,9 +155,13 @@
     return block
 
 
-def near(plan, v_ext, w_ext, packed, rim_v, rim_w, *tables):
+def near(plan, v_ext, w_ext, packed, rim_v, rim_w, *refs):
+    tables, basis = refs[:4], refs[4:]
+    planes = plan.planes
     inside = range(1, 1 + plan.ny // 8)
-    face_tables(w_ext, tables, plan.planes, plan.planes // 2, inside, inside, inside[1:-1])
+    for p in range(planes + 2):
+        tables[1][p, pl.ds(TOP, 8), :] = jnp.zeros((8, 128), jnp.float32)
+    face_tables(w_ext, tables, planes, planes // 2, inside, inside, inside)
     group = lanes() // WIDE
     band, spot = lanes() // BAND, lanes() % BAND
     for field, (ext, rim) in enumerate(((v_ext, rim_v), (w_ext, rim_w))):
@@ -166,6 +171,13 @@
                 packed[field, i, at, :] = column_block(plan, ext, i, r, group)
             for i in range(plan.rim):
                 rim[1 + i, at, :] = rim_block(plan, ext, i, at, band, spot)
+    for ref in basis:
+        ref[0] = jnp.zeros(ref.shape[1:], jnp.float32)
+        ref[planes + 1] = jnp.zeros(ref.shape[1:], jnp.float32)
+    source = v_ext
+    for level in range(1, EARLY + 1):
+        sweep(plan, level, source, basis[level - 1], tables, [8 * r for r in inside])
+        source = basis[level - 1]
 
 
 def pack_lanes(plan, *refs):
@@ -253,13 +265,12 @@
     lax.fori_loop(0, planes // unroll, diagonal, 0)
 
 
-def advance(source, target, tables, first, trips, unroll, start, blocks):
+def advance(source, target, tables, first, trips, unroll, starts):
     cx, cy, cz, dg = tables
 
     def body(trip, _):
         base = first + trip * unroll
-        for u0, r in [(u0, r) for u0 in range(0, unroll, QUAD) for r in range(blocks)]:
-            s = start + 8 * r
+        for u0, s in [(u0, s) for u0 in range(0, unroll, QUAD) for s in starts]:
             at = pl.ds(s, 8)
             top = min(u0 + QUAD, unroll)
             fields = {u: source[base + u, at, :] for u in range(u0, top + 2)}
@@ -276,11 +287,71 @@
                 target[p, at, :] = dg[p, at, :] * here - total
         return 0
 
-    lax.fori_loop(0, trips, body, 0)
+    if trips == 1:
+        body(0, 0)
+    else:
+        lax.fori_loop(0, trips, body, 0)
+
+
+def march(source, target, tables, first, trips, unroll, starts):
+    cx, cy, cz, dg = tables
+    row = lax.broadcasted_iota(jnp.int32, (8, 128), 0)
+    top_row, end_row = row == 0, row == 7
+
+    def body(trip, _):
+        base = first + trip * unroll
+        for u0 in range(0, unroll, QUAD):
+            here = {u: None for u in range(u0, min(u0 + QUAD, unroll))}
+            lifted, passed = {}, {}
+            for s in starts:
+                at, beyond = pl.ds(s, 8), pl.ds(s + 8, 8)
+                for u in here:
+                    p = base + u + 1
+                    if s == starts[0]:
+                        here[u] = source[p, at, :]
+                        lifted[u] = pltpu.roll(here[u], 7, 0)
+                        if s:
+                            previous = cy[p, at, :] * source[p, pl.ds(s - 8, 8), :]
+                            passed[u] = pltpu.roll(previous, 1, 0)
+                fields = {u + 1: value for u, value in here.items()}
+                fields[u0] = source[base + u0, at, :]
+                final = max(here)
+                fields[final + 2] = source[base + final + 2, at, :]
+                walls = {u: cx[base + u, at, :] for u in range(u0, final + 2)}
+                for u in here:
+                    p = base + u + 1
+                    value, ahead = here[u], cz[p, at, :]
+                    wall = cy[p, beyond, :]
+                    after = pltpu.roll(value, 127, 1)
+                    behind = pltpu.roll(ahead * value, 1, 1)
+                    sunk = pltpu.roll(wall * value, 1, 0)
+                    upper = jnp.where(top_row, passed.get(u, sunk), sunk)
+                    passed[u] = sunk
+                    here[u] = source[p, beyond, :]
+                    rising = pltpu.roll(here[u], 7, 0)
+                    lower = jnp.where(end_row, rising, lifted[u])
+                    lifted[u] = rising
+                    total = walls[u + 1] * fields[u + 2] + walls[u] * fields[u]
+                    total = total + (wall * lower + upper)
+                    total = total + (ahead * after + behind)
+                    target[p, at, :] = dg[p, at, :] * value - total
+        return 0
+
+    if trips == 1:
+        body(0, 0)
+    else:
+        lax.fori_loop(0, trips, body, 0)
+
+
+def sweep(plan, level, source, target, tables, starts):
+    low, count = plan.span(level)
+    half = -(-count // 2)
+    low = jnp.minimum(low, plan.planes - 2 * half)
+    march(source, target, tables, low, 2, half, starts)
 
 
 def level_rows(plan, level):
-    return TOP - STEPS + level, -(-(plan.ny + 2 * (STEPS - level)) // 8)
+    return range(0, plan.rows, 8) if level < STEPS else range(TOP, TOP + plan.ny, 8)
 
 
 def products(fields, sums):
@@ -293,23 +364,21 @@
 
 def inner(plan, *refs):
     v_ext, w_ext = refs[:2]
-    basis, (sums_ref, rim_v, rim_w), tables = refs[8 : 8 + STEPS], refs[8 + STEPS : -4], refs[-4:]
+    sums_ref, rim_v, rim_w, *refs = refs[8 + STEPS :]
+    tables, basis = refs[:4], refs[4:]
     planes = plan.planes
     blank8 = jnp.zeros((8, 128), jnp.float32)
     last = plan.rows // 8 - 1
     halo = (0, last)
     face_tables(w_ext, tables, planes, planes // 2, halo, (0, last - 1, last), (0, 1, last - 1, last))
-    for ref in basis:
-        ref[0] = jnp.zeros(ref.shape[1:], jnp.float32)
-        ref[planes + 1] = jnp.zeros(ref.shape[1:], jnp.float32)
     source = v_ext
     for level in range(1, STEPS + 1):
-        low, count = plan.span(level)
-        trips = 2
-        unroll = -(-count // trips)
-        low = jnp.minimum(low, planes - unroll * trips)
-        start, blocks = level_rows(plan, level)
-        advance(source, basis[level - 1], tables, low, trips, unroll, start, blocks)
+        if level <= EARLY:
+            low, count = plan.span(level)
+            starts = [TOP - STEPS + level, TOP + plan.ny - 2 - level]
+            advance(source, basis[level - 1], tables, low, 1, count, starts)
+        else:
+            sweep(plan, level, source, basis[level - 1], tables, level_rows(plan, level))
         source = basis[level - 1]
 
     own = 1 + plan.own()
@@ -336,7 +405,8 @@
 
 
 def outer(plan, first, second, rim_v, rim_w, sums_ref, *refs):
-    basis, (moments, rim_0, rim_s), tables = refs[:STEPS], refs[STEPS : STEPS + 3], refs[STEPS + 3 :]
+    levels, moments, rim_s, *tables = refs
+    rim_0, *basis = [levels.at[k] for k in range(STEPS + 1)]
     planes, deep, half, rim = plan.planes, plan.deep, plan.half, plan.rim
     even_z = lax.axis_index("gz") % 2 == 1
     lane = lanes()
@@ -345,9 +415,9 @@
     halo = (spot >= 12) & (spot < 28)
     blank8 = jnp.zeros((8, 128), jnp.float32)
 
-    def wrap(ref, start, blocks):
-        for r in range(blocks):
-            at = pl.ds(start + 8 * r, 8)
+    def wrap(ref, starts):
+        for start in starts:
+            at = pl.ds(start, 8)
             ref[0, at, :] = pltpu.roll(ref[rim, at, :], BAND, 1)
             ref[rim + 1, at, :] = pltpu.roll(ref[1, at, :], 128 - BAND, 1)
 
@@ -374,17 +444,20 @@
                 full[1 + i, at, :] = block
         for i in range(rim + 2):
             full[i, pl.ds(plan.rows, 16), :] = jnp.zeros((16, 128), jnp.float32)
-        wrap(full, 0, plan.rows // 8)
+        wrap(full, range(0, plan.rows, 8))
 
     every = range(plan.rows // 8)
     face_tables(rim_s, tables, rim, rim, every, every, every)
     source = rim_0
     for level in range(1, STEPS + 1):
-        start, blocks = level_rows(plan, level)
-        advance(source, basis[level - 1], tables, 0, 1, rim, start, blocks)
-        source = basis[level - 1]
+        starts = level_rows(plan, level)
+        target = basis[level - 1]
+        march(source, target, tables, 0, 1, 1, starts)
+        march(source, target, tables, rim - 1, 1, 1, starts)
         if level < STEPS:
-            wrap(source, start, blocks)
+            wrap(target, starts)
+        march(source, target, tables, 1, 1, rim - 2, starts)
+        source = target
 
     own = plan.own()
     fresh = ((spot >= 6) & (spot < 12)) | ((spot >= 28) & (spot < 34))
@@ -397,9 +470,12 @@
         plane = band * rim + i
         mine = fresh & (plane >= own) & (plane < own + plan.nx)
         sums = [a + jnp.where(mine, b, 0.0) for a, b in zip(sums, part)]
-    line = jnp.zeros((1, 128), jnp.float32)
+    row = lax.broadcasted_iota(jnp.int32, (16, 128), 0)
+    stacked = jnp.zeros((16, 128), jnp.float32)
     for j, part in enumerate(sums):
-        line = jnp.where(lanes((1, 128)) == j, jnp.sum(part), line)
+        stacked = jnp.where(row == j, jnp.sum(part, axis=0, keepdims=True), stacked)
+    stacked = jnp.sum(stacked, axis=1, keepdims=True)
+    line = jnp.sum(jnp.where(lanes((16, 128)) == row, stacked, 0.0), axis=0, keepdims=True)
     for j in range(moments.shape[0]):
         moments[j] = line
 
@@ -440,17 +516,11 @@
     return coefficients, leftover
 
 
-def combine(plan, chunk, parts, v_ext, rim_0, *refs):
-    basis, rims = refs[:STEPS], refs[STEPS : 2 * STEPS]
-    solution_field, residual, weights = refs[2 * STEPS :]
-
-    @pl.when(pl.program_id(0) == 0)
-    def _():
-        coefficients, leftover = weigh(parts[...])
-        for k, value in enumerate(coefficients + leftover):
-            weights[k] = value
-
-    own = plan.own() + pl.program_id(0) * chunk
+def combine(plan, chunk, parts, v_ext, rims, *refs):
+    basis, outs, buffers, sems = refs[:STEPS], refs[STEPS : STEPS + 2], refs[-3:-1], refs[-1]
+    coefficients, leftover = weigh(parts[...])
+    weights = coefficients + leftover
+    own = plan.own()
     lane = lanes()
 
     def mix(refs, p, at):
@@ -461,7 +531,8 @@
             two = two + weights[STEPS + k] * fields[k]
         return one, two + weights[2 * STEPS] * fields[STEPS]
 
-    for p in range(chunk):
+    copies = []
+    for p in range(plan.nx):
         plane = own + p
         band = plane // plan.rim
         depth = plane - band * plan.rim
@@ -471,11 +542,19 @@
         for r in range(plan.ny // 8):
             at = pl.ds(TOP + 8 * r, 8)
             mains = mix((v_ext,) + tuple(basis), 1 + plane, at)
-            edges = mix((rim_0,) + tuple(rims), 1 + depth, at)
-            for out, main, edge in zip((solution_field, residual), mains, edges):
+            edges = mix([rims.at[k] for k in range(STEPS + 1)], 1 + depth, at)
+            for out, main, edge in zip(buffers, mains, edges):
                 value = jnp.where(lane < STEPS, pltpu.roll(edge, low, 1), main)
                 value = jnp.where(lane >= 128 - STEPS, pltpu.roll(edge, high, 1), value)
                 out[p, pl.ds(8 * r, 8), :] = value
+        if (p + 1) % chunk == 0:
+            there = pl.ds(p + 1 - chunk, chunk)
+            for f, (buffer, out) in enumerate(zip(buffers, outs)):
+                sem = sems.at[f, p // chunk]
+                copies.append(pltpu.make_async_copy(buffer.at[there], out.at[there], sem))
+                copies[-1].start()
+    for copy in copies:
+        copy.wait()
 
 
 def swaps(first, second, axis):
@@ -511,9 +590,9 @@
     )(*[resident(a) for a in (v_ext, w_ext, *halos)])
     first, second = swaps(first, second, "gy")
     rim = kept((plan.rim + 2, plan.tall, 128))
-    packed, rim_v, rim_w, *tables = call(
+    packed, rim_v, rim_w, *fields = call(
         functools.partial(near, plan),
-        [kept((2, plan.deep, plan.rows, 128)), rim, rim] + [table] * 4,
+        [kept((2, plan.deep, plan.rows, 128)), rim, rim] + [table] * (4 + STEPS),
         "near",
         flops=1 << 24,
     )(resident(v_ext), resident(w_ext))
@@ -528,31 +607,30 @@
     v_ext, w_ext = resident(v_ext), resident(w_ext)
     devices = plan.gx * plan.gy * plan.gz
     sums = kept((2 * STEPS + 1, 8, 128))
-    *basis, sums, rim_v, rim_w = call(
+    sums, rim_v, rim_w, *fields = call(
         functools.partial(inner, plan),
-        [table] * STEPS + [sums, rim, rim] + [table] * 4,
+        [sums, rim, rim] + [table] * (4 + STEPS),
         "inner",
-        aliases={i: i + STEPS - 1 for i in range(2, 8)},
+        aliases={i: i - 1 for i in range(2, 8 + STEPS)},
         flops=1 << 24,
-    )(v_ext, w_ext, *[resident(a) for a in (rim_v, rim_w, *tables)])[: STEPS + 3]
-    *rims, moments, rim_0 = call(
+    )(v_ext, w_ext, *[resident(a) for a in (rim_v, rim_w, *fields)])
+    basis = fields[4:]
+    rims, moments = call(
         functools.partial(outer, plan),
-        [rim] * STEPS + [kept((devices, 1, 128)), rim],
+        [kept((STEPS + 1, plan.rim + 2, plan.tall, 128)), kept((devices, 1, 128))],
         "outer",
         scratch=[rim] * 5,
     )(*[resident(a) for a in (first, second, rim_v, rim_w, sums)])
     parts = lax.all_to_all(moments, AXES, 0, 0, tiled=True)
     chunk = 4
-    block = pl.BlockSpec((chunk, ny, nz), lambda i: (i, 0, 0))
     shape = jax.ShapeDtypeStruct((nx, ny, nz), jnp.float32)
-    operands = [parts, v_ext, rim_0] + basis + rims
+    operands = [parts, v_ext, rims] + basis
     out, residual = pl.pallas_call(
         functools.partial(combine, plan, chunk),
         out_shape=[shape, shape],
-        grid=(nx // chunk,),
         in_specs=[vmem_spec()] * len(operands),
-        out_specs=[block, block],
-        scratch_shapes=[kept((2 * STEPS + 1, 8, 128))],
+        out_specs=[pl.BlockSpec(memory_space=pl.ANY)] * 2,
+        scratch_shapes=[kept((nx, ny, nz))] * 2 + [pltpu.SemaphoreType.DMA((2, nx // chunk))],
         compiler_params=pltpu.CompilerParams(vmem_limit_bytes=40 << 20),
         name="combine",
     )(*[resident(a) for a in operands])

time: 41.5 us -> 38.6 us (0.930)
  Pallas kernels: 15.6 us -> 14.3 us
  blocking collectives: 13.6 us -> 12.8 us
  waiting for transfers between devices: 1.91 us -> 1.38 us
    pallas_call x2, Pallas kernels: 8.56 us -> 6.06 us  [the longest x1 3.04 us: on_device(): call(functools.partial(outer, plan), [kept((STEPS + 1, plan.rim + 2, plan...]
    pallas_call x1, Pallas kernels: 2.22 us -> 4.32 us  [on_device(): call(functools.partial(near, plan), [kept((2, plan.deep, plan.rows, 128))...]
    pallas_call x1, Pallas kernels: 2.8 us -> 1.9 us  [on_device(): pl.pallas_call(functools.partial(combine, plan, chunk), out_shape=[shape,...]
    all_to_all x1, blocking collectives: 13.6 us -> 12.8 us  [on_device(): parts = lax.all_to_all(moments, AXES, 0, 0, tiled=True)]
    ppermute x4, waiting for transfers between devices: 0.57 us -> 0.03 us  [swaps(): lax.ppermute(value, axis, pairs + [(b, a) for a, b in pairs])]
  transfers between devices with their start and end apart: 5 -> 5, of which waited for: 2 -> 1; matrix products, arithmetic and copies ran while one was open for 0% -> 0% of each run, Pallas kernels for 18% -> 19%
where the time goes in v4:
time: 38.6 us; the launch traced here: 38.4 us
  Pallas kernels  14.3 us (37%)
  blocking collectives  12.8 us (33%)
  starting transfers between devices  9.22 us (24%)
  waiting for transfers between devices  1.38 us (4%)
  between operations  0.71 us (2%)
    all_to_all x1, blocking collectives, on_device(): parts = lax.all_to_all(moments, AXES, 0, 0, tiled=True)  12.8 us
    ppermute x4, starting transfers between devices, swaps(): lax.ppermute(value, axis, pairs + [(b, a) for a, b in pairs])  8.71 us
    pallas_call x1, Pallas kernels, on_device(): call(functools.partial(near, plan), [kept((2, plan.deep, plan.rows, 128))...  4.32 us
    pallas_call x1, Pallas kernels, on_device(): call(functools.partial(outer, plan), [kept((STEPS + 1, plan.rim + 2, plan...  3.04 us
    pallas_call x1, Pallas kernels, on_device(): call(functools.partial(inner, plan), [sums, rim, rim] + [table] * (4 + ST...  3.02 us
    pallas_call x1, Pallas kernels, on_device(): pl.pallas_call(functools.partial(combine, plan, chunk), out_shape=[shape,...  1.9 us
    pallas_call x1, Pallas kernels, on_device(): call(functools.partial(prepare, plan), [table, table] + [face] * plan.sid...  1.63 us
    ppermute x1, waiting for transfers between devices, on_device(): halos = [lax.ppermute(faces[0], 'gx', [(0, 1), (1, 0)])]  1.35 us
  transfers between devices with their start and end apart: 5, of which 1 were waited for; matrix products, arithmetic and copies ran while one was open for 0% of the time, Pallas kernels for 19%

profile of v4, /device:TPU:0, one launch (start us, length us, event | category | flops | bytes accessed | tf_op | source)
XLA Modules:
  0.0 38.4 jit_solution(8644065195539315124)
XLA Ops:
  0.6 1.6 %prepare.1 = (f32[24,96,128]{2,1,0:T(8,128)S(1)}, f32[24,96,128]{2,1,0:T(8,128)S(1)}, f32[2,6,64,128]{3,2,1,0:T(8,128)S(1)}) custom-call(f32[16,64,128]{2,1,0:T(8,128)} %rs.1, f32[16,64,128]{2,1,0:T(8,128)} %inv.1, s32[16,64,128]{2,1,0:T(8,128)} %act.1), custom_call_target="tpu_custom_call" | custom-call | bytes 1048576 | tf_op jit(solution)/shard_map/prepare/pallas_call | solution.py:578
  2.3 0.5 %collective-permute-start = (f32[2,6,64,128]{3,2,1,0:T(8,128)S(1)}, f32[2,6,64,128]{3,2,1,0:T(8,128)S(1)}, u32[]{:S(2)}, u32[]{:S(2)}) collective-permute-start(f32[2,6,64,128]{3,2,1,0:T(8,128)S(1)} %get-tuple-element.39), channel_id=1, source_target_pairs={{0,16},{16,0},{1,17},{17,1},{2,18},{18,2},{3,19},{19,3},{4,20},{20... | collective-permute-start | bytes 1179656 | tf_op jit(solution)/shard_map/ppermute | solution.py:582
  2.8 1.3 %collective-permute-done.refs_2_ = f32[2,6,64,128]{3,2,1,0:T(8,128)S(1)} collective-permute-done((f32[2,6,64,128]{3,2,1,0:T(8,128)S(1)}, f32[2,6,64,128]{3,2,1,0:T(8,128)S(1)}, u32[]{:S(2)}, u32[]{:S(2)}) %collective-permute-start) | collective-permute-done | bytes 393248 | tf_op jit(solution)/shard_map/ppermute | solution.py:582
  4.1 0.1 rows.1
  4.2 2.9 %collective-permute-start.1 = (f32[2,111,128]{2,1,0:T(8,128)S(1)}, f32[2,111,128]{2,1,0:T(8,128)S(1)}, u32[]{:S(2)}, u32[]{:S(2)}) collective-permute-start(f32[2,111,128]{2,1,0:T(8,128)S(1)} %get-tuple-element.42), channel_id=1, source_target_pairs={{0,4},{8,12},{4,0},{12,8},{1,5},{9,13},{5,1},{13,9},{2,6},{10,14},... | collective-permute-start | bytes 341000 | tf_op jit(solution)/shard_map/ppermute | solution.py:565
  7.1 0.7 %collective-permute-start.2 = (f32[2,111,128]{2,1,0:T(8,128)S(1)}, f32[2,111,128]{2,1,0:T(8,128)S(1)}, u32[]{:S(2)}, u32[]{:S(2)}) collective-permute-start(f32[2,111,128]{2,1,0:T(8,128)S(1)} %get-tuple-element.43), channel_id=1, source_target_pairs={{4,8},{8,4},{5,9},{9,5},{6,10},{10,6},{7,11},{11,7},{20,24},{24,20... | collective-permute-start | bytes 341000 | tf_op jit(solution)/shard_map/ppermute | solution.py:565
  7.8 4.3 %near.1 = (f32[2,3,80,128]{3,2,1,0:T(8,128)S(1)}, f32[10,96,128]{2,1,0:T(8,128)S(1)}, f32[10,96,128]{2,1,0:T(8,128)S(1)}, f32[24,96,128]{2,1,0:T(8,128)S(1)}, f3...) custom-call(f32[24,96,128]{2,1,0:T(8,128)S(1)} %get-tuple-element.40, ...), custom_call_target="tpu_custom_call" | custom-call | flops 16777216 | bytes 1048576 | tf_op jit(solution)/shard_map/near/pallas_call | solution.py:593
  12.1 0.0 collective-permute-done.1.refs_2_
  12.1 0.0 collective-permute-done.2.refs_3_
  12.1 0.3 columns.1
  12.5 0.7 %collective-permute-start.3 = (f32[2,3,40,128]{3,2,1,0:T(8,128)S(1)}, f32[2,3,40,128]{3,2,1,0:T(8,128)S(1)}, u32[]{:S(2)}, u32[]{:S(2)}) collective-permute-start(f32[2,3,40,128]{3,2,1,0:T(8,128)S(1)} %get-tuple-element.45), channel_id=1, source_target_pairs={{1,2},{2,1},{5,6},{6,5},{9,10},{10,9},{13,14},{14,13},{17,18},{18,... | collective-permute-start | bytes 368648 | tf_op jit(solution)/shard_map/ppermute | solution.py:565
  13.2 4.5 %collective-permute-start.4 = (f32[2,3,40,128]{3,2,1,0:T(8,128)S(1)}, f32[2,3,40,128]{3,2,1,0:T(8,128)S(1)}, u32[]{:S(2)}, u32[]{:S(2)}) collective-permute-start(f32[2,3,40,128]{3,2,1,0:T(8,128)S(1)} %get-tuple-element.46), channel_id=1, source_target_pairs={{0,1},{2,3},{1,0},{3,2},{4,5},{6,7},{5,4},{7,6},{8,9},{10,11},{9,8... | collective-permute-start | bytes 368648 | tf_op jit(solution)/shard_map/ppermute | solution.py:565
  17.6 3.0 %inner.1 = (f32[13,8,128]{2,1,0:T(8,128)S(1)}, f32[10,96,128]{2,1,0:T(8,128)S(1)}, f32[10,96,128]{2,1,0:T(8,128)S(1)}, f32[24,96,128]{2,1,0:T(8,128)S(1)}, f32[2...) custom-call(f32[24,96,128]{2,1,0:T(8,128)S(1)} %get-tuple-element.47, ...), custom_call_target="tpu_custom_call", output_to_operand_aliasing={{1}: (2, {}), {2}: (3, {}), {3}: (4, {}), {4}: (5, {}), {5}... | custom-call | flops 16777216 | bytes 1048576 | tf_op jit(solution)/shard_map/inner/pallas_call | solution.py:610
  20.7 0.0 collective-permute-done.3.first
  20.7 0.0 collective-permute-done.4.second
  20.7 3.0 %outer.1 = (f32[7,10,96,128]{3,2,1,0:T(8,128)S(1)}, f32[32,1,128]{2,1,0:T(1,128)S(1)}) custom-call(f32[2,3,40,128]{3,2,1,0:T(8,128)S(1)} %collective-permute-done.3.first, f32[2,3,40,128]{3,2,1,0:T(8,128)S(1)} %collective-permute-done.4.second, f32[10,96,128]{2,1,0:T(8,128)S(1)} %get-tuple-element.61.rim_v, f32[10,96,128]{2,1,0:T(8,128)S(1)} %get-tuple-element.62.rim_w, ...), custom_call_target="tpu_custom_call" | custom-call | bytes 1048576 | tf_op jit(solution)/shard_map/outer/pallas_call | solution.py:618
  23.7 12.8 %all_to_all.5.parts = f32[32,1,128]{2,1,0:T(1,128)S(1)} all-to-all(f32[32,1,128]{2,1,0:T(1,128)S(1)} %get-tuple-element.64), channel_id=1, replica_groups=mesh['gx'=2,'gy'=4,'gz'=4] {'gx','gy','gz'}, dimensions={0} | all-to-all | bytes 32768 | tf_op jit(solution)/shard_map/all_to_all | solution.py:624
  36.5 1.9 %combine.1 = (f32[16,64,128]{2,1,0:T(8,128)}, f32[16,64,128]{2,1,0:T(8,128)}) custom-call(f32[32,1,128]{2,1,0:T(1,128)S(1)} %all_to_all.5.parts, f32[24,96,128]{2,1,0:T(8,128)S(1)} %get-tuple-element.47.refs_0_.v_ext, f32[7,10,96,128]{3,2,1,0:T(8,128)S(1)} %get-tuple-element.65.rims, f32[24,96,128]{2,1,0:T(8,128)S(1)} %get-tuple-element.66.refs_0_, ...), custom_call_target="tpu_custom_call" | custom-call | tf_op jit(solution)/shard_map/combine/pallas_call | solution.py:628
Async XLA Ops:
  2.3 1.9 %collective-permute-start = (f32[2,6,64,128]{3,2,1,0:T(8,128)S(1)}, f32[2,6,64,128]{3,2,1,0:T(8,128)S(1)}, u32[]{:S(2)}, u32[]{:S(2)}) collective-permute-start(f32[2,6,64,128]{3,2,1,0:T(8,128)S(1)} %get-tuple-element.39), channel_id=1, source_target_pairs={{0,16},{16,0},{1,17},{17,1},{2,18},{18,2},{3,19},{19,3},{4,20},{20... | collective-permute-start | bytes 1179656 | tf_op jit(solution)/shard_map/ppermute | solution.py:582
  4.2 7.9 %collective-permute-start.1 = (f32[2,111,128]{2,1,0:T(8,128)S(1)}, f32[2,111,128]{2,1,0:T(8,128)S(1)}, u32[]{:S(2)}, u32[]{:S(2)}) collective-permute-start(f32[2,111,128]{2,1,0:T(8,128)S(1)} %get-tuple-element.42), channel_id=1, source_target_pairs={{0,4},{8,12},{4,0},{12,8},{1,5},{9,13},{5,1},{13,9},{2,6},{10,14},... | collective-permute-start | bytes 341000 | tf_op jit(solution)/shard_map/ppermute | solution.py:565
  7.1 5.0 %collective-permute-start.2 = (f32[2,111,128]{2,1,0:T(8,128)S(1)}, f32[2,111,128]{2,1,0:T(8,128)S(1)}, u32[]{:S(2)}, u32[]{:S(2)}) collective-permute-start(f32[2,111,128]{2,1,0:T(8,128)S(1)} %get-tuple-element.43), channel_id=1, source_target_pairs={{4,8},{8,4},{5,9},{9,5},{6,10},{10,6},{7,11},{11,7},{20,24},{24,20... | collective-permute-start | bytes 341000 | tf_op jit(solution)/shard_map/ppermute | solution.py:565
  12.5 8.2 %collective-permute-start.3 = (f32[2,3,40,128]{3,2,1,0:T(8,128)S(1)}, f32[2,3,40,128]{3,2,1,0:T(8,128)S(1)}, u32[]{:S(2)}, u32[]{:S(2)}) collective-permute-start(f32[2,3,40,128]{3,2,1,0:T(8,128)S(1)} %get-tuple-element.45), channel_id=1, source_target_pairs={{1,2},{2,1},{5,6},{6,5},{9,10},{10,9},{13,14},{14,13},{17,18},{18,... | collective-permute-start | bytes 368648 | tf_op jit(solution)/shard_map/ppermute | solution.py:565
  13.2 7.5 %collective-permute-start.4 = (f32[2,3,40,128]{3,2,1,0:T(8,128)S(1)}, f32[2,3,40,128]{3,2,1,0:T(8,128)S(1)}, u32[]{:S(2)}, u32[]{:S(2)}) collective-permute-start(f32[2,3,40,128]{3,2,1,0:T(8,128)S(1)} %get-tuple-element.46), channel_id=1, source_target_pairs={{0,1},{2,3},{1,0},{3,2},{4,5},{6,7},{5,4},{7,6},{8,9},{10,11},{9,8... | collective-permute-start | bytes 368648 | tf_op jit(solution)/shard_map/ppermute | solution.py:565

commit v5 on v4

--- a/solution.py
+++ b/solution.py
@@ -13,7 +13,7 @@
 WIDE = 16
 RIMS = 3
 BAND = 40
-EARLY = 4
+EARLY = 3
 QUAD = 4
 TOP = 8
 VMEM = pltpu.VMEM
@@ -65,6 +65,11 @@
         if self.sides == 1:
             return lax.axis_index("gx") * STEPS
         return STEPS if self.sides == 2 else 0
+
+    def face_starts(self):
+        if self.sides == 1:
+            return [(1 - lax.axis_index("gx")) * (self.nx - STEPS)]
+        return [self.nx - STEPS, 0]
 
     def halo_starts(self):
         if self.sides == 1:
@@ -95,7 +100,7 @@
         return cut, self.planes - 2 * cut
 
 
-def prepare(plan, rs, inv, act, v_ext, w_ext, *faces):
+def prepare(plan, rs, inv, act, v_ext, w_ext, *edges):
     own, ny = 1 + plan.own(), plan.ny
     for ext in (v_ext, w_ext):
         ext[...] = jnp.zeros(ext.shape, jnp.float32)
@@ -103,30 +108,31 @@
         liquid = act[i].astype(jnp.float32)
         v_ext[own + i, pl.ds(TOP, ny), :] = rs[i] * liquid
         w_ext[own + i, pl.ds(TOP, ny), :] = inv[i] * liquid * (2.0 / SHIFT)
-    if plan.sides == 1:
-        starts = [(1 - lax.axis_index("gx")) * (plan.nx - STEPS)]
-    else:
-        starts = [plan.nx - STEPS, 0]
-    for start, face in zip(starts, faces):
-        for i in range(STEPS):
-            face[0, i] = v_ext[own + start + i, pl.ds(TOP, ny), :]
-            face[1, i] = w_ext[own + start + i, pl.ds(TOP, ny), :]
-
-
-def pack_rows(plan, *refs):
-    halos, (v_ext, w_ext, first, second) = refs[2 : 2 + plan.sides], refs[2 + plan.sides :]
-    ny = plan.ny
+    for start, edge in zip(plan.face_starts(), edges):
+        for field, ext in enumerate((v_ext, w_ext)):
+            for i in range(STEPS):
+                p = own + start + i
+                edge[field, i, pl.ds(0, 8), :] = ext[p, pl.ds(TOP, 8), :]
+                edge[field, i, pl.ds(8, 8), :] = ext[p, pl.ds(TOP + ny - 8, 8), :]
+
+
+def pack_rows(plan, v_ext, w_ext, *refs):
+    edges, (first, second, *faces) = refs[: plan.sides], refs[plan.sides :]
+    own, ny = 1 + plan.own(), plan.ny
+    for start, face in zip(plan.face_starts(), faces):
+        for field, ext in enumerate((v_ext, w_ext)):
+            for i in range(STEPS):
+                face[field, i] = ext[own + start + i, pl.ds(TOP, ny), :]
     even = lax.axis_index("gy") % 2 == 0
-    starts = plan.halo_starts()
     for field, ext in enumerate((v_ext, w_ext)):
-        for start, halo in zip(starts, halos):
-            for i in range(STEPS):
-                ext[1 + start + i, pl.ds(TOP, ny), :] = halo[field, i]
         offset = 0
         for side, plane, rows in plan.strips():
-            at = 1 + plane + (plan.own() if side is None else starts[side])
-            low = ext[at, pl.ds(TOP, rows), :]
-            high = ext[at, pl.ds(TOP + ny - rows, rows), :]
+            if side is None:
+                low = ext[own + plane, pl.ds(TOP, rows), :]
+                high = ext[own + plane, pl.ds(TOP + ny - rows, rows), :]
+            else:
+                low = edges[side][field, plane, pl.ds(0, rows), :]
+                high = edges[side][field, plane, pl.ds(16 - rows, rows), :]
             first[field, pl.ds(offset, rows), :] = jnp.where(even, high, low)
             second[field, pl.ds(offset, rows), :] = jnp.where(even, low, high)
             offset += rows
@@ -155,10 +161,15 @@
     return block
 
 
-def near(plan, v_ext, w_ext, packed, rim_v, rim_w, *refs):
+def near(plan, *refs):
+    halos, (v_ext, w_ext, packed, rim_v, rim_w, *refs) = refs[2 : 2 + plan.sides], refs[2 + plan.sides :]
     tables, basis = refs[:4], refs[4:]
     planes = plan.planes
     inside = range(1, 1 + plan.ny // 8)
+    for start, halo in zip(plan.halo_starts(), halos):
+        for field, ext in enumerate((v_ext, w_ext)):
+            for i in range(STEPS):
+                ext[1 + start + i, pl.ds(TOP, plan.ny), :] = halo[field, i]
     for p in range(planes + 2):
         tables[1][p, pl.ds(TOP, 8), :] = jnp.zeros((8, 128), jnp.float32)
     face_tables(w_ext, tables, planes, planes // 2, inside, inside, inside)
@@ -481,8 +492,10 @@
 
 
 def weigh(parts):
-    line = jnp.sum(parts, axis=0)
-    line = jnp.broadcast_to(line, (8, 128))
+    lines = [parts[i] for i in range(parts.shape[0])]
+    while len(lines) > 1:
+        lines = [sum(lines[i + 1 : i + 2], lines[i]) for i in range(0, len(lines), 2)]
+    line = jnp.broadcast_to(lines[0], (8, 128))
     moment = []
     for j in range(2 * STEPS + 1):
         picked = jnp.where(lanes() == j, line, 0.0)
@@ -501,10 +514,9 @@
             rhs[i] = rhs[i] - factor * rhs[p]
     solved = [None] * count
     for p in reversed(range(count)):
-        running = rhs[p]
-        for j in range(p + 1, count):
-            running = running - gram[p][j] * solved[j]
-        solved[p] = running * inverse[p]
+        solved[p] = rhs[p] * inverse[p]
+        for i in range(p):
+            rhs[i] = rhs[i] - gram[i][p] * solved[p]
     scale = sign[0] * solved[0]
     for k in range(1, count):
         scale = scale + sign[k] * solved[k]
@@ -557,6 +569,14 @@
         copy.wait()
 
 
+def across(plan, values):
+    if plan.sides == 1:
+        return [lax.ppermute(values[0], "gx", [(0, 1), (1, 0)])]
+    steps = [(i, i + 1) for i in range(plan.gx - 1)]
+    pairs = [steps, [(b, a) for a, b in steps]]
+    return [lax.ppermute(value, "gx", p) for value, p in zip(values, pairs)]
+
+
 def swaps(first, second, axis):
     count = lax.axis_size(axis)
     starts = (0, 1) if axis == "gy" else (1, 0)
@@ -575,27 +595,25 @@
     inputs = [
         pltpu.with_memory_space_constraint(a, pltpu.HBM) for a in (right_side, inv_density, active)
     ]
-    v_ext, w_ext, *faces = call(
-        functools.partial(prepare, plan), [table, table] + [face] * plan.sides, "prepare"
+    edge = kept((2, STEPS, 16, 128))
+    v_ext, w_ext, *edges = call(
+        functools.partial(prepare, plan), [table, table] + [edge] * plan.sides, "prepare"
     )(*inputs)
-    if plan.sides == 1:
-        halos = [lax.ppermute(faces[0], "gx", [(0, 1), (1, 0)])]
-    else:
-        steps = [(i, i + 1) for i in range(plan.gx - 1)]
-        pairs = [steps, [(b, a) for a, b in steps]]
-        halos = [lax.ppermute(f, "gx", p) for f, p in zip(faces, pairs)]
+    edges = across(plan, edges)
     strip = kept((2, plan.strip_rows(), 128))
-    v_ext, w_ext, first, second = call(
-        functools.partial(pack_rows, plan), [table, table, strip, strip], "rows", aliases={0: 0, 1: 1}
-    )(*[resident(a) for a in (v_ext, w_ext, *halos)])
+    first, second, *faces = call(
+        functools.partial(pack_rows, plan), [strip, strip] + [face] * plan.sides, "rows"
+    )(*[resident(a) for a in (v_ext, w_ext, *edges)])
+    halos = across(plan, faces)
     first, second = swaps(first, second, "gy")
     rim = kept((plan.rim + 2, plan.tall, 128))
-    packed, rim_v, rim_w, *fields = call(
+    v_ext, w_ext, packed, rim_v, rim_w, *fields = call(
         functools.partial(near, plan),
-        [kept((2, plan.deep, plan.rows, 128)), rim, rim] + [table] * (4 + STEPS),
+        [table, table, kept((2, plan.deep, plan.rows, 128)), rim, rim] + [table] * (4 + STEPS),
         "near",
+        aliases={0: 0, 1: 1},
         flops=1 << 24,
-    )(resident(v_ext), resident(w_ext))
+    )(*[resident(a) for a in (v_ext, w_ext, *halos)])
     column = kept((2, plan.deep, plan.half, 128))
     v_ext, w_ext, first, second = call(
         functools.partial(pack_lanes, plan),

time: 38.6 us -> 38.5 us (level)
  waiting for transfers between devices: 1.38 us -> 0.96 us
    pallas_call x3, Pallas kernels: 6.01 us -> 5.58 us  [the longest x1 3.91 us: on_device(): call(functools.partial(near, plan), [table, table, kept((2, plan.deep, pl...]
    ppermute x1 -> x2, starting transfers between devices: 0.52 us -> 0.94 us  [across(): return [lax.ppermute(values[0], 'gx', [(0, 1), (1, 0)])]]
    ppermute x1 -> x2, waiting for transfers between devices: 1.35 us -> 0.95 us  [across(): return [lax.ppermute(values[0], 'gx', [(0, 1), (1, 0)])]]
  transfers between devices with their start and end apart: 5 -> 6, of which waited for: 1 -> 1; matrix products, arithmetic and copies ran while one was open for 0% -> 0% of each run, Pallas kernels for 19% -> 19%
where the time goes in v5:
time: 38.5 us; the launch traced here: 38.3 us
  Pallas kernels  14.2 us (37%)
  blocking collectives  13 us (34%)
  starting transfers between devices  9.38 us (24%)
  waiting for transfers between devices  0.96 us (2%)
  between operations  0.72 us (2%)
    all_to_all x1, blocking collectives, on_device(): parts = lax.all_to_all(moments, AXES, 0, 0, tiled=True)  13 us
    ppermute x4, starting transfers between devices, swaps(): lax.ppermute(value, axis, pairs + [(b, a) for a, b in pairs])  8.43 us
    pallas_call x1, Pallas kernels, on_device(): call(functools.partial(near, plan), [table, table, kept((2, plan.deep, pl...  3.91 us
    pallas_call x1, Pallas kernels, on_device(): call(functools.partial(inner, plan), [sums, rim, rim] + [table] * (4 + ST...  3.38 us
    pallas_call x1, Pallas kernels, on_device(): call(functools.partial(outer, plan), [kept((STEPS + 1, plan.rim + 2, plan...  3.05 us
    pallas_call x1, Pallas kernels, on_device(): pl.pallas_call(functools.partial(combine, plan, chunk), out_shape=[shape,...  1.87 us
    pallas_call x1, Pallas kernels, on_device(): call(functools.partial(prepare, plan), [table, table] + [edge] * plan.sid...  1.61 us
    ppermute x2, waiting for transfers between devices, across(): return [lax.ppermute(values[0], 'gx', [(0, 1), (1, 0)])]  0.95 us
  transfers between devices with their start and end apart: 6, of which 1 were waited for; matrix products, arithmetic and copies ran while one was open for 0% of the time, Pallas kernels for 19%

profile of v5, /device:TPU:0, one launch (start us, length us, event | category | flops | bytes accessed | tf_op | source)
XLA Modules:
  0.0 38.3 jit_solution(3157249383697253701)
XLA Ops:
  0.6 1.6 %prepare.1 = (f32[24,96,128]{2,1,0:T(8,128)S(1)}, f32[24,96,128]{2,1,0:T(8,128)S(1)}, f32[2,6,16,128]{3,2,1,0:T(8,128)S(1)}) custom-call(f32[16,64,128]{2,1,0:T(8,128)} %rs.1, f32[16,64,128]{2,1,0:T(8,128)} %inv.1, s32[16,64,128]{2,1,0:T(8,128)} %act.1), custom_call_target="tpu_custom_call" | custom-call | bytes 1048576 | tf_op jit(solution)/shard_map/prepare/pallas_call | solution.py:599
  2.2 0.5 %collective-permute-start = (f32[2,6,16,128]{3,2,1,0:T(8,128)S(1)}, f32[2,6,16,128]{3,2,1,0:T(8,128)S(1)}, u32[]{:S(2)}, u32[]{:S(2)}) collective-permute-start(f32[2,6,16,128]{3,2,1,0:T(8,128)S(1)} %get-tuple-element.40), channel_id=1, source_target_pairs={{0,16},{16,0},{1,17},{17,1},{2,18},{18,2},{3,19},{19,3},{4,20},{20... | collective-permute-start | bytes 294920 | tf_op jit(solution)/shard_map/ppermute | solution.py:574
  2.8 0.9 %collective-permute-done.refs_0_ = f32[2,6,16,128]{3,2,1,0:T(8,128)S(1)} collective-permute-done((f32[2,6,16,128]{3,2,1,0:T(8,128)S(1)}, f32[2,6,16,128]{3,2,1,0:T(8,128)S(1)}, u32[]{:S(2)}, u32[]{:S(2)}) %collective-permute-start) | collective-permute-done | bytes 98336 | tf_op jit(solution)/shard_map/ppermute | solution.py:574
  3.7 0.1 rows.1
  3.8 0.4 %collective-permute-start.1 = (f32[2,6,64,128]{3,2,1,0:T(8,128)S(1)}, f32[2,6,64,128]{3,2,1,0:T(8,128)S(1)}, u32[]{:S(2)}, u32[]{:S(2)}) collective-permute-start(f32[2,6,64,128]{3,2,1,0:T(8,128)S(1)} %get-tuple-element.41), channel_id=1, source_target_pairs={{0,16},{16,0},{1,17},{17,1},{2,18},{18,2},{3,19},{19,3},{4,20},{20... | collective-permute-start | bytes 1179656 | tf_op jit(solution)/shard_map/ppermute | solution.py:574
  4.2 2.7 %collective-permute-start.2 = (f32[2,111,128]{2,1,0:T(8,128)S(1)}, f32[2,111,128]{2,1,0:T(8,128)S(1)}, u32[]{:S(2)}, u32[]{:S(2)}) collective-permute-start(f32[2,111,128]{2,1,0:T(8,128)S(1)} %get-tuple-element.44), channel_id=1, source_target_pairs={{0,4},{8,12},{4,0},{12,8},{1,5},{9,13},{5,1},{13,9},{2,6},{10,14},... | collective-permute-start | bytes 341000 | tf_op jit(solution)/shard_map/ppermute | solution.py:585
  6.8 0.7 %collective-permute-start.3 = (f32[2,111,128]{2,1,0:T(8,128)S(1)}, f32[2,111,128]{2,1,0:T(8,128)S(1)}, u32[]{:S(2)}, u32[]{:S(2)}) collective-permute-start(f32[2,111,128]{2,1,0:T(8,128)S(1)} %get-tuple-element.45), channel_id=1, source_target_pairs={{4,8},{8,4},{5,9},{9,5},{6,10},{10,6},{7,11},{11,7},{20,24},{24,20... | collective-permute-start | bytes 341000 | tf_op jit(solution)/shard_map/ppermute | solution.py:585
  7.5 0.0 collective-permute-done.1.refs_2_
  7.5 3.9 %near.1 = (f32[24,96,128]{2,1,0:T(8,128)S(1)}, f32[24,96,128]{2,1,0:T(8,128)S(1)}, f32[2,3,80,128]{3,2,1,0:T(8,128)S(1)}, f32[10,96,128]{2,1,0:T(8,128)S(1)}, f3...) custom-call(f32[24,96,128]{2,1,0:T(8,128)S(1)} %get-tuple-element.38, ...), custom_call_target="tpu_custom_call", output_to_operand_aliasing={{0}: (0, {}), {1}: (1, {})} | custom-call | flops 16777216 | bytes 1048576 | tf_op jit(solution)/shard_map/near/pallas_call | solution.py:610
  11.4 0.0 collective-permute-done.2.refs_2_
  11.5 0.0 collective-permute-done.3.refs_3_
  11.5 0.3 columns.1
  11.8 0.7 %collective-permute-start.4 = (f32[2,3,40,128]{3,2,1,0:T(8,128)S(1)}, f32[2,3,40,128]{3,2,1,0:T(8,128)S(1)}, u32[]{:S(2)}, u32[]{:S(2)}) collective-permute-start(f32[2,3,40,128]{3,2,1,0:T(8,128)S(1)} %get-tuple-element.47), channel_id=1, source_target_pairs={{1,2},{2,1},{5,6},{6,5},{9,10},{10,9},{13,14},{14,13},{17,18},{18,... | collective-permute-start | bytes 368648 | tf_op jit(solution)/shard_map/ppermute | solution.py:585
  12.5 4.5 %collective-permute-start.5 = (f32[2,3,40,128]{3,2,1,0:T(8,128)S(1)}, f32[2,3,40,128]{3,2,1,0:T(8,128)S(1)}, u32[]{:S(2)}, u32[]{:S(2)}) collective-permute-start(f32[2,3,40,128]{3,2,1,0:T(8,128)S(1)} %get-tuple-element.48), channel_id=1, source_target_pairs={{0,1},{2,3},{1,0},{3,2},{4,5},{6,7},{5,4},{7,6},{8,9},{10,11},{9,8... | collective-permute-start | bytes 368648 | tf_op jit(solution)/shard_map/ppermute | solution.py:585
  16.9 3.4 %inner.1 = (f32[13,8,128]{2,1,0:T(8,128)S(1)}, f32[10,96,128]{2,1,0:T(8,128)S(1)}, f32[10,96,128]{2,1,0:T(8,128)S(1)}, f32[24,96,128]{2,1,0:T(8,128)S(1)}, f32[2...) custom-call(f32[24,96,128]{2,1,0:T(8,128)S(1)} %get-tuple-element.49, ...), custom_call_target="tpu_custom_call", output_to_operand_aliasing={{1}: (2, {}), {2}: (3, {}), {3}: (4, {}), {4}: (5, {}), {5}... | custom-call | flops 16777216 | bytes 1048576 | tf_op jit(solution)/shard_map/inner/pallas_call | solution.py:628
  20.3 0.0 collective-permute-done.4.first
  20.3 0.0 collective-permute-done.5.second
  20.4 3.1 %outer.1 = (f32[7,10,96,128]{3,2,1,0:T(8,128)S(1)}, f32[32,1,128]{2,1,0:T(1,128)S(1)}) custom-call(f32[2,3,40,128]{3,2,1,0:T(8,128)S(1)} %collective-permute-done.4.first, f32[2,3,40,128]{3,2,1,0:T(8,128)S(1)} %collective-permute-done.5.second, f32[10,96,128]{2,1,0:T(8,128)S(1)} %get-tuple-element.63.rim_v, f32[10,96,128]{2,1,0:T(8,128)S(1)} %get-tuple-element.64.rim_w, ...), custom_call_target="tpu_custom_call" | custom-call | bytes 1048576 | tf_op jit(solution)/shard_map/outer/pallas_call | solution.py:636
  23.4 13.0 %all_to_all.5.parts = f32[32,1,128]{2,1,0:T(1,128)S(1)} all-to-all(f32[32,1,128]{2,1,0:T(1,128)S(1)} %get-tuple-element.66), channel_id=1, replica_groups=mesh['gx'=2,'gy'=4,'gz'=4] {'gx','gy','gz'}, dimensions={0} | all-to-all | bytes 32768 | tf_op jit(solution)/shard_map/all_to_all | solution.py:642
  36.4 1.9 %combine.1 = (f32[16,64,128]{2,1,0:T(8,128)}, f32[16,64,128]{2,1,0:T(8,128)}) custom-call(f32[32,1,128]{2,1,0:T(1,128)S(1)} %all_to_all.5.parts, f32[24,96,128]{2,1,0:T(8,128)S(1)} %get-tuple-element.49.refs_0_.v_ext, f32[7,10,96,128]{3,2,1,0:T(8,128)S(1)} %get-tuple-element.67.rims, f32[24,96,128]{2,1,0:T(8,128)S(1)} %get-tuple-element.68.refs_0_, ...), custom_call_target="tpu_custom_call" | custom-call | tf_op jit(solution)/shard_map/combine/pallas_call | solution.py:646
Async XLA Ops:
  2.2 1.5 %collective-permute-start = (f32[2,6,16,128]{3,2,1,0:T(8,128)S(1)}, f32[2,6,16,128]{3,2,1,0:T(8,128)S(1)}, u32[]{:S(2)}, u32[]{:S(2)}) collective-permute-start(f32[2,6,16,128]{3,2,1,0:T(8,128)S(1)} %get-tuple-element.40), channel_id=1, source_target_pairs={{0,16},{16,0},{1,17},{17,1},{2,18},{18,2},{3,19},{19,3},{4,20},{20... | collective-permute-start | bytes 294920 | tf_op jit(solution)/shard_map/ppermute | solution.py:574
  3.8 3.7 %collective-permute-start.1 = (f32[2,6,64,128]{3,2,1,0:T(8,128)S(1)}, f32[2,6,64,128]{3,2,1,0:T(8,128)S(1)}, u32[]{:S(2)}, u32[]{:S(2)}) collective-permute-start(f32[2,6,64,128]{3,2,1,0:T(8,128)S(1)} %get-tuple-element.41), channel_id=1, source_target_pairs={{0,16},{16,0},{1,17},{17,1},{2,18},{18,2},{3,19},{19,3},{4,20},{20... | collective-permute-start | bytes 1179656 | tf_op jit(solution)/shard_map/ppermute | solution.py:574
  4.2 7.3 %collective-permute-start.2 = (f32[2,111,128]{2,1,0:T(8,128)S(1)}, f32[2,111,128]{2,1,0:T(8,128)S(1)}, u32[]{:S(2)}, u32[]{:S(2)}) collective-permute-start(f32[2,111,128]{2,1,0:T(8,128)S(1)} %get-tuple-element.44), channel_id=1, source_target_pairs={{0,4},{8,12},{4,0},{12,8},{1,5},{9,13},{5,1},{13,9},{2,6},{10,14},... | collective-permute-start | bytes 341000 | tf_op jit(solution)/shard_map/ppermute | solution.py:585
  6.8 4.6 %collective-permute-start.3 = (f32[2,111,128]{2,1,0:T(8,128)S(1)}, f32[2,111,128]{2,1,0:T(8,128)S(1)}, u32[]{:S(2)}, u32[]{:S(2)}) collective-permute-start(f32[2,111,128]{2,1,0:T(8,128)S(1)} %get-tuple-element.45), channel_id=1, source_target_pairs={{4,8},{8,4},{5,9},{9,5},{6,10},{10,6},{7,11},{11,7},{20,24},{24,20... | collective-permute-start | bytes 341000 | tf_op jit(solution)/shard_map/ppermute | solution.py:585
  11.8 8.5 %collective-permute-start.4 = (f32[2,3,40,128]{3,2,1,0:T(8,128)S(1)}, f32[2,3,40,128]{3,2,1,0:T(8,128)S(1)}, u32[]{:S(2)}, u32[]{:S(2)}) collective-permute-start(f32[2,3,40,128]{3,2,1,0:T(8,128)S(1)} %get-tuple-element.47), channel_id=1, source_target_pairs={{1,2},{2,1},{5,6},{6,5},{9,10},{10,9},{13,14},{14,13},{17,18},{18,... | collective-permute-start | bytes 368648 | tf_op jit(solution)/shard_map/ppermute | solution.py:585
  12.5 7.9 %collective-permute-start.5 = (f32[2,3,40,128]{3,2,1,0:T(8,128)S(1)}, f32[2,3,40,128]{3,2,1,0:T(8,128)S(1)}, u32[]{:S(2)}, u32[]{:S(2)}) collective-permute-start(f32[2,3,40,128]{3,2,1,0:T(8,128)S(1)} %get-tuple-element.48), channel_id=1, source_target_pairs={{0,1},{2,3},{1,0},{3,2},{4,5},{6,7},{5,4},{7,6},{8,9},{10,11},{9,8... | collective-permute-start | bytes 368648 | tf_op jit(solution)/shard_map/ppermute | solution.py:585

commit v6 on v5

--- a/solution.py
+++ b/solution.py
@@ -358,7 +358,8 @@
     low, count = plan.span(level)
     half = -(-count // 2)
     low = jnp.minimum(low, plan.planes - 2 * half)
-    march(source, target, tables, low, 2, half, starts)
+    move = advance if starts[0] else march
+    move(source, target, tables, low, 2, half, starts)
 
 
 def level_rows(plan, level):

time: 38.5 us -> 38.5 us (level)
  no operation moved by 1% of the time
where the time goes in v6:
time: 38.5 us; the launch traced here: 38.3 us
  Pallas kernels  14.2 us (37%)
  blocking collectives  13 us (34%)
  starting transfers between devices  9.38 us (24%)
  waiting for transfers between devices  0.96 us (2%)
  between operations  0.72 us (2%)
    all_to_all x1, blocking collectives, on_device(): parts = lax.all_to_all(moments, AXES, 0, 0, tiled=True)  13 us
    ppermute x4, starting transfers between devices, swaps(): lax.ppermute(value, axis, pairs + [(b, a) for a, b in pairs])  8.43 us
    pallas_call x1, Pallas kernels, on_device(): call(functools.partial(near, plan), [table, table, kept((2, plan.deep, pl...  3.92 us
    pallas_call x1, Pallas kernels, on_device(): call(functools.partial(inner, plan), [sums, rim, rim] + [table] * (4 + ST...  3.38 us
    pallas_call x1, Pallas kernels, on_device(): call(functools.partial(outer, plan), [kept((STEPS + 1, plan.rim + 2, plan...  3.05 us
    pallas_call x1, Pallas kernels, on_device(): pl.pallas_call(functools.partial(combine, plan, chunk), out_shape=[shape,...  1.87 us
    pallas_call x1, Pallas kernels, on_device(): call(functools.partial(prepare, plan), [table, table] + [edge] * plan.sid...  1.61 us
    ppermute x2, waiting for transfers between devices, across(): return [lax.ppermute(values[0], 'gx', [(0, 1), (1, 0)])]  0.95 us
  transfers between devices with their start and end apart: 6, of which 1 were waited for; matrix products, arithmetic and copies ran while one was open for 0% of the time, Pallas kernels for 19%

profile of v6, /device:TPU:0, one launch (start us, length us, event | category | flops | bytes accessed | tf_op | source)
XLA Modules:
  0.0 38.3 jit_solution(16105644363272260532)
XLA Ops:
  0.6 1.6 %prepare.1 = (f32[24,96,128]{2,1,0:T(8,128)S(1)}, f32[24,96,128]{2,1,0:T(8,128)S(1)}, f32[2,6,16,128]{3,2,1,0:T(8,128)S(1)}) custom-call(f32[16,64,128]{2,1,0:T(8,128)} %rs.1, f32[16,64,128]{2,1,0:T(8,128)} %inv.1, s32[16,64,128]{2,1,0:T(8,128)} %act.1), custom_call_target="tpu_custom_call" | custom-call | bytes 1048576 | tf_op jit(solution)/shard_map/prepare/pallas_call | solution.py:600
  2.2 0.5 %collective-permute-start = (f32[2,6,16,128]{3,2,1,0:T(8,128)S(1)}, f32[2,6,16,128]{3,2,1,0:T(8,128)S(1)}, u32[]{:S(2)}, u32[]{:S(2)}) collective-permute-start(f32[2,6,16,128]{3,2,1,0:T(8,128)S(1)} %get-tuple-element.40), channel_id=1, source_target_pairs={{0,16},{16,0},{1,17},{17,1},{2,18},{18,2},{3,19},{19,3},{4,20},{20... | collective-permute-start | bytes 294920 | tf_op jit(solution)/shard_map/ppermute | solution.py:575
  2.8 0.9 %collective-permute-done.refs_0_ = f32[2,6,16,128]{3,2,1,0:T(8,128)S(1)} collective-permute-done((f32[2,6,16,128]{3,2,1,0:T(8,128)S(1)}, f32[2,6,16,128]{3,2,1,0:T(8,128)S(1)}, u32[]{:S(2)}, u32[]{:S(2)}) %collective-permute-start) | collective-permute-done | bytes 98336 | tf_op jit(solution)/shard_map/ppermute | solution.py:575
  3.7 0.1 rows.1
  3.8 0.4 %collective-permute-start.1 = (f32[2,6,64,128]{3,2,1,0:T(8,128)S(1)}, f32[2,6,64,128]{3,2,1,0:T(8,128)S(1)}, u32[]{:S(2)}, u32[]{:S(2)}) collective-permute-start(f32[2,6,64,128]{3,2,1,0:T(8,128)S(1)} %get-tuple-element.41), channel_id=1, source_target_pairs={{0,16},{16,0},{1,17},{17,1},{2,18},{18,2},{3,19},{19,3},{4,20},{20... | collective-permute-start | bytes 1179656 | tf_op jit(solution)/shard_map/ppermute | solution.py:575
  4.2 2.7 %collective-permute-start.2 = (f32[2,111,128]{2,1,0:T(8,128)S(1)}, f32[2,111,128]{2,1,0:T(8,128)S(1)}, u32[]{:S(2)}, u32[]{:S(2)}) collective-permute-start(f32[2,111,128]{2,1,0:T(8,128)S(1)} %get-tuple-element.44), channel_id=1, source_target_pairs={{0,4},{8,12},{4,0},{12,8},{1,5},{9,13},{5,1},{13,9},{2,6},{10,14},... | collective-permute-start | bytes 341000 | tf_op jit(solution)/shard_map/ppermute | solution.py:586
  6.8 0.7 %collective-permute-start.3 = (f32[2,111,128]{2,1,0:T(8,128)S(1)}, f32[2,111,128]{2,1,0:T(8,128)S(1)}, u32[]{:S(2)}, u32[]{:S(2)}) collective-permute-start(f32[2,111,128]{2,1,0:T(8,128)S(1)} %get-tuple-element.45), channel_id=1, source_target_pairs={{4,8},{8,4},{5,9},{9,5},{6,10},{10,6},{7,11},{11,7},{20,24},{24,20... | collective-permute-start | bytes 341000 | tf_op jit(solution)/shard_map/ppermute | solution.py:586
  7.5 0.0 collective-permute-done.1.refs_2_
  7.5 3.9 %near.1 = (f32[24,96,128]{2,1,0:T(8,128)S(1)}, f32[24,96,128]{2,1,0:T(8,128)S(1)}, f32[2,3,80,128]{3,2,1,0:T(8,128)S(1)}, f32[10,96,128]{2,1,0:T(8,128)S(1)}, f3...) custom-call(f32[24,96,128]{2,1,0:T(8,128)S(1)} %get-tuple-element.38, ...), custom_call_target="tpu_custom_call", output_to_operand_aliasing={{0}: (0, {}), {1}: (1, {})} | custom-call | flops 16777216 | bytes 1048576 | tf_op jit(solution)/shard_map/near/pallas_call | solution.py:611
  11.4 0.0 collective-permute-done.2.refs_2_
  11.5 0.0 collective-permute-done.3.refs_3_
  11.5 0.3 columns.1
  11.8 0.7 %collective-permute-start.4 = (f32[2,3,40,128]{3,2,1,0:T(8,128)S(1)}, f32[2,3,40,128]{3,2,1,0:T(8,128)S(1)}, u32[]{:S(2)}, u32[]{:S(2)}) collective-permute-start(f32[2,3,40,128]{3,2,1,0:T(8,128)S(1)} %get-tuple-element.47), channel_id=1, source_target_pairs={{1,2},{2,1},{5,6},{6,5},{9,10},{10,9},{13,14},{14,13},{17,18},{18,... | collective-permute-start | bytes 368648 | tf_op jit(solution)/shard_map/ppermute | solution.py:586
  12.5 4.5 %collective-permute-start.5 = (f32[2,3,40,128]{3,2,1,0:T(8,128)S(1)}, f32[2,3,40,128]{3,2,1,0:T(8,128)S(1)}, u32[]{:S(2)}, u32[]{:S(2)}) collective-permute-start(f32[2,3,40,128]{3,2,1,0:T(8,128)S(1)} %get-tuple-element.48), channel_id=1, source_target_pairs={{0,1},{2,3},{1,0},{3,2},{4,5},{6,7},{5,4},{7,6},{8,9},{10,11},{9,8... | collective-permute-start | bytes 368648 | tf_op jit(solution)/shard_map/ppermute | solution.py:586
  17.0 3.4 %inner.1 = (f32[13,8,128]{2,1,0:T(8,128)S(1)}, f32[10,96,128]{2,1,0:T(8,128)S(1)}, f32[10,96,128]{2,1,0:T(8,128)S(1)}, f32[24,96,128]{2,1,0:T(8,128)S(1)}, f32[2...) custom-call(f32[24,96,128]{2,1,0:T(8,128)S(1)} %get-tuple-element.49, ...), custom_call_target="tpu_custom_call", output_to_operand_aliasing={{1}: (2, {}), {2}: (3, {}), {3}: (4, {}), {4}: (5, {}), {5}... | custom-call | flops 16777216 | bytes 1048576 | tf_op jit(solution)/shard_map/inner/pallas_call | solution.py:629
  20.3 0.0 collective-permute-done.4.first
  20.3 0.0 collective-permute-done.5.second
  20.4 3.1 %outer.1 = (f32[7,10,96,128]{3,2,1,0:T(8,128)S(1)}, f32[32,1,128]{2,1,0:T(1,128)S(1)}) custom-call(f32[2,3,40,128]{3,2,1,0:T(8,128)S(1)} %collective-permute-done.4.first, f32[2,3,40,128]{3,2,1,0:T(8,128)S(1)} %collective-permute-done.5.second, f32[10,96,128]{2,1,0:T(8,128)S(1)} %get-tuple-element.63.rim_v, f32[10,96,128]{2,1,0:T(8,128)S(1)} %get-tuple-element.64.rim_w, ...), custom_call_target="tpu_custom_call" | custom-call | bytes 1048576 | tf_op jit(solution)/shard_map/outer/pallas_call | solution.py:637
  23.4 13.0 %all_to_all.5.parts = f32[32,1,128]{2,1,0:T(1,128)S(1)} all-to-all(f32[32,1,128]{2,1,0:T(1,128)S(1)} %get-tuple-element.66), channel_id=1, replica_groups=mesh['gx'=2,'gy'=4,'gz'=4] {'gx','gy','gz'}, dimensions={0} | all-to-all | bytes 32768 | tf_op jit(solution)/shard_map/all_to_all | solution.py:643
  36.4 1.9 %combine.1 = (f32[16,64,128]{2,1,0:T(8,128)}, f32[16,64,128]{2,1,0:T(8,128)}) custom-call(f32[32,1,128]{2,1,0:T(1,128)S(1)} %all_to_all.5.parts, f32[24,96,128]{2,1,0:T(8,128)S(1)} %get-tuple-element.49.refs_0_.v_ext, f32[7,10,96,128]{3,2,1,0:T(8,128)S(1)} %get-tuple-element.67.rims, f32[24,96,128]{2,1,0:T(8,128)S(1)} %get-tuple-element.68.refs_0_, ...), custom_call_target="tpu_custom_call" | custom-call | tf_op jit(solution)/shard_map/combine/pallas_call | solution.py:647
Async XLA Ops:
  2.2 1.5 %collective-permute-start = (f32[2,6,16,128]{3,2,1,0:T(8,128)S(1)}, f32[2,6,16,128]{3,2,1,0:T(8,128)S(1)}, u32[]{:S(2)}, u32[]{:S(2)}) collective-permute-start(f32[2,6,16,128]{3,2,1,0:T(8,128)S(1)} %get-tuple-element.40), channel_id=1, source_target_pairs={{0,16},{16,0},{1,17},{17,1},{2,18},{18,2},{3,19},{19,3},{4,20},{20... | collective-permute-start | bytes 294920 | tf_op jit(solution)/shard_map/ppermute | solution.py:575
  3.8 3.7 %collective-permute-start.1 = (f32[2,6,64,128]{3,2,1,0:T(8,128)S(1)}, f32[2,6,64,128]{3,2,1,0:T(8,128)S(1)}, u32[]{:S(2)}, u32[]{:S(2)}) collective-permute-start(f32[2,6,64,128]{3,2,1,0:T(8,128)S(1)} %get-tuple-element.41), channel_id=1, source_target_pairs={{0,16},{16,0},{1,17},{17,1},{2,18},{18,2},{3,19},{19,3},{4,20},{20... | collective-permute-start | bytes 1179656 | tf_op jit(solution)/shard_map/ppermute | solution.py:575
  4.2 7.3 %collective-permute-start.2 = (f32[2,111,128]{2,1,0:T(8,128)S(1)}, f32[2,111,128]{2,1,0:T(8,128)S(1)}, u32[]{:S(2)}, u32[]{:S(2)}) collective-permute-start(f32[2,111,128]{2,1,0:T(8,128)S(1)} %get-tuple-element.44), channel_id=1, source_target_pairs={{0,4},{8,12},{4,0},{12,8},{1,5},{9,13},{5,1},{13,9},{2,6},{10,14},... | collective-permute-start | bytes 341000 | tf_op jit(solution)/shard_map/ppermute | solution.py:586
  6.8 4.6 %collective-permute-start.3 = (f32[2,111,128]{2,1,0:T(8,128)S(1)}, f32[2,111,128]{2,1,0:T(8,128)S(1)}, u32[]{:S(2)}, u32[]{:S(2)}) collective-permute-start(f32[2,111,128]{2,1,0:T(8,128)S(1)} %get-tuple-element.45), channel_id=1, source_target_pairs={{4,8},{8,4},{5,9},{9,5},{6,10},{10,6},{7,11},{11,7},{20,24},{24,20... | collective-permute-start | bytes 341000 | tf_op jit(solution)/shard_map/ppermute | solution.py:586
  11.8 8.5 %collective-permute-start.4 = (f32[2,3,40,128]{3,2,1,0:T(8,128)S(1)}, f32[2,3,40,128]{3,2,1,0:T(8,128)S(1)}, u32[]{:S(2)}, u32[]{:S(2)}) collective-permute-start(f32[2,3,40,128]{3,2,1,0:T(8,128)S(1)} %get-tuple-element.47), channel_id=1, source_target_pairs={{1,2},{2,1},{5,6},{6,5},{9,10},{10,9},{13,14},{14,13},{17,18},{18,... | collective-permute-start | bytes 368648 | tf_op jit(solution)/shard_map/ppermute | solution.py:586
  12.5 7.9 %collective-permute-start.5 = (f32[2,3,40,128]{3,2,1,0:T(8,128)S(1)}, f32[2,3,40,128]{3,2,1,0:T(8,128)S(1)}, u32[]{:S(2)}, u32[]{:S(2)}) collective-permute-start(f32[2,3,40,128]{3,2,1,0:T(8,128)S(1)} %get-tuple-element.48), channel_id=1, source_target_pairs={{0,1},{2,3},{1,0},{3,2},{4,5},{6,7},{5,4},{7,6},{8,9},{10,11},{9,8... | collective-permute-start | bytes 368648 | tf_op jit(solution)/shard_map/ppermute | solution.py:586
